TPU v7x, 256 devices: a whole 4x4x8 slice. The times are simulated.
256 devices in a mesh: patch: 64 (over x, z, core), visit: 4 (over y).
Axes of the slice: x: 4, y: 4, z: 8, core: 2. Of those that a mesh axis runs over, the one named last changes fastest.
Arguments:
- image: float32 [4, 1536, 128, 128], P('visit', 'patch'), may hold values from -6 to 6
- variance: float32 [4, 1536, 128, 128], P('visit', 'patch'), may hold values from 0.01 to 3600, as said below
- patches: int32 [4, 1536, 2], P('visit', 'patch'), may hold values from 0 to 63, all different within a row; in each aligned block of 24 rows (0 to 23, 24 to 47, ..., all dimensions but the last counted through in order) at most 2 rows name the same one
- offsets: int32 [4, 1536, 2, 2], P('visit', 'patch'), may hold values from -64 to 192
- psf_index: int32 [4, 1536], P('visit', 'patch'), may hold values from 0 to 15
- coeff_table: float32 [16, 3], replicated, may hold values from -4 to 4
- basis_taps: float32 [3, 2, 21], replicated, may hold values from -1.25 to 1.25
Outputs:
- coadd: float32 [64, 256, 256], P('patch', 'visit')
Inputs may be any that keep to these rules, and one draw needn't show every extreme that they name: Each row names 2 different patches; in the rows of one device no patch is named more than 2 times, a bound that some block reaches. `variance`: positive.
All inputs are finite; a program needn't handle non-finite values.
Results may differ from a plain program's by a relative error of at most 0.00014.
Values sent between devices are 32-bit elements; how exact they have to be, the bound alone decides.
No kernel may reach another device: no remote copies, remote signals or barrier semaphores. Data moves between devices by JAX's collectives and lax.ppermute only.
A program may use at most 64 MiB of HBM per device.

v0:
```python
import math

import jax
import jax.numpy as jnp
from jax import lax
from jax.sharding import PartitionSpec as P

PATCH_PIX = 256


def band_matrices(basis_taps, pixels):
    tap_count = basis_taps.shape[-1]
    margin = tap_count // 2
    lines = jnp.arange(pixels, dtype=jnp.int32)
    offset_idx = lines[None, :] - lines[:, None] + margin
    band_hits = (
        offset_idx[:, :, None] == jnp.arange(tap_count, dtype=jnp.int32)[None, None, :]
    ).astype(jnp.float32)
    row_mats = jnp.einsum(
        "ikt,bt->bik", band_hits, basis_taps[:, 0], precision=lax.Precision.HIGHEST
    )
    col_mats = jnp.einsum(
        "ljt,bt->blj", band_hits, basis_taps[:, 1], precision=lax.Precision.HIGHEST
    )
    return (row_mats, col_mats)


def blur_slots(tile_stack, coeffs, row_mats, col_mats):
    smoothed = jnp.einsum("bik,nkj->nbij", row_mats, tile_stack, precision=lax.Precision.HIGHEST)
    smoothed = jnp.einsum("nbij,blj->nbil", smoothed, col_mats, precision=lax.Precision.HIGHEST)
    return jnp.einsum("nbil,nb->nil", smoothed, coeffs, precision=lax.Precision.HIGHEST)


def body(image, variance, patches, offsets, psf_index, coeff_table, basis_taps):
    tile_dev = image.shape[1]
    pixels = image.shape[-1]
    top_count = patches.shape[-1]
    npatch = lax.axis_size("patch")
    nvisit = lax.axis_size("visit")
    capacity = max(2, 5 * tile_dev * top_count // (4 * npatch))
    slot_count = npatch * capacity
    pair_count = tile_dev * top_count
    tile_data = image.reshape(tile_dev, pixels, pixels)
    weights = 1.0 / jnp.mean(variance.reshape(tile_dev, pixels * pixels), axis=1)
    coef_count = coeff_table.shape[0]
    lookup = (
        psf_index.reshape(tile_dev)[:, None] == jnp.arange(coef_count, dtype=jnp.int32)[None, :]
    ).astype(jnp.float32)
    coeffs = jnp.dot(lookup, coeff_table, precision=lax.Precision.HIGHEST)
    row_mats, col_mats = band_matrices(basis_taps, pixels)
    targets = patches.reshape(pair_count)
    matches = (targets[:, None] == jnp.arange(npatch, dtype=jnp.int32)[None, :]).astype(jnp.int32)
    earlier = jnp.sum((jnp.cumsum(matches, axis=0) - matches) * matches, axis=1)
    slot_of = targets * capacity + earlier
    chooser = (jnp.arange(slot_count, dtype=jnp.int32)[:, None] == slot_of[None, :]).astype(
        jnp.float32
    )
    per_tile = chooser.reshape(slot_count, tile_dev, top_count).sum(axis=2)
    moved_off = jnp.dot(
        chooser, offsets.reshape(pair_count, 2).astype(jnp.float32), precision=lax.Precision.HIGHEST
    )
    moved_w = jnp.dot(per_tile, weights, precision=lax.Precision.HIGHEST)
    moved_c = jnp.dot(per_tile, coeffs, precision=lax.Precision.HIGHEST)
    packed = jnp.einsum("st,tij->sij", per_tile, tile_data, precision=lax.Precision.HIGHEST)
    got_img = lax.all_to_all(
        packed.reshape(npatch, capacity, pixels, pixels),
        "patch",
        split_axis=0,
        concat_axis=0,
        tiled=True,
    )
    got_coef = lax.all_to_all(
        moved_c.reshape(npatch, capacity, -1), "patch", split_axis=0, concat_axis=0, tiled=True
    )
    got_w = lax.all_to_all(
        moved_w.reshape(npatch, capacity), "patch", split_axis=0, concat_axis=0, tiled=True
    )
    got_off = lax.all_to_all(
        moved_off.reshape(npatch, capacity, 2), "patch", split_axis=0, concat_axis=0, tiled=True
    )

    def prepare(slot_img, slot_coef, slot_wts):
        return slot_wts[:, None, None] * blur_slots(slot_img, slot_coef, row_mats, col_mats)

    group_size = math.gcd(slot_count, 32)
    block_count = slot_count // group_size
    patch_rows = jnp.arange(PATCH_PIX, dtype=jnp.int32)
    tile_rows = jnp.arange(pixels, dtype=jnp.int32)

    def place_block(running, sliced):
        numerator, denominator = running
        slot_img, slot_coef, slot_wts, slot_offs = sliced
        layered = prepare(slot_img, slot_coef, slot_wts)
        row_pick = (
            patch_rows[None, :, None] == slot_offs[:, 0, None, None] + tile_rows[None, None, :]
        ).astype(jnp.float32)
        col_pick = (
            patch_rows[None, :, None] == slot_offs[:, 1, None, None] + tile_rows[None, None, :]
        ).astype(jnp.float32)
        spread = jnp.einsum("nai,nij->naj", row_pick, layered, precision=lax.Precision.HIGHEST)
        numerator = numerator + jnp.einsum(
            "naj,nbj->ab", spread, col_pick, precision=lax.Precision.HIGHEST
        )
        denominator = denominator + jnp.einsum(
            "na,nb->ab",
            slot_wts[:, None] * row_pick.sum(axis=2),
            col_pick.sum(axis=2),
            precision=lax.Precision.HIGHEST,
        )
        return ((numerator, denominator), None)

    zero_sums = (
        jnp.zeros((PATCH_PIX, PATCH_PIX), jnp.float32),
        jnp.zeros((PATCH_PIX, PATCH_PIX), jnp.float32),
    )
    stacked = (
        got_img.reshape(block_count, group_size, pixels, pixels),
        got_coef.reshape(block_count, group_size, -1),
        got_w.reshape(block_count, group_size),
        got_off.reshape(block_count, group_size, 2).astype(jnp.int32),
    )
    (numerator, denominator), unused = lax.scan(place_block, zero_sums, stacked)
    all_num, all_den = lax.psum((numerator, denominator), "visit")
    strip = PATCH_PIX // nvisit
    first_row = lax.axis_index("visit") * strip
    own_num = lax.dynamic_slice_in_dim(all_num, first_row, strip, 0)
    own_den = lax.dynamic_slice_in_dim(all_den, first_row, strip, 0)
    coadd = own_num / (own_den + 1.0)
    return coadd[None]


def solution(mesh):
    return jax.shard_map(
        body,
        mesh=mesh,
        in_specs=(
            P("visit", "patch", None, None),
            P("visit", "patch", None, None),
            P("visit", "patch", None),
            P("visit", "patch", None, None),
            P("visit", "patch"),
            P(),
            P(),
        ),
        out_specs=P("patch", "visit", None),
        check_vma=False,
    )
```

profile of v0, /device:TPU:62, one launch (start us, length us, event | category | flops | bytes accessed | tf_op | source)
XLA Modules:
  0.0 505.1 jit_solution(5707038578096705376)
XLA Ops:
  6.5 0.8 copy.70
  7.9 0.7 bitcast_add_fusion
  8.9 1.7 reduce_sum.50
  10.7 0.7 copy.77
  11.4 11.7 %all-to-all-start.1 = ((f32[64,1,2]{2,1,0:T(1,128)}), f32[64,1,2]{2,1,0:T(1,128)S(1)}, u32[]{:S(2)}, u32[]{:S(2)}) async-start(f32[64,1,2]{2,1,0:T(1,128)} %copy.77), calls=%async_computation.1 | async-start | bytes 65536 | tf_op jit(solution)/shard_map/all_to_all | solution.py:75
  24.2 0.9 convolution_bitcast_fusion.1
  25.1 0.8 copy.72
  25.9 4.0 all-to-all-done.1
  29.9 7.4 %all-to-all-start = ((f32[64,2,2]{2,1,0:T(2,128)}), f32[64,2,2]{2,1,0:T(2,128)S(1)}, u32[]{:S(2)}, u32[]{:S(2)}) async-start(f32[64,2,2]{2,1,0:T(2,128)} %copy.72), calls=%async_computation | async-start | bytes 131072 | tf_op jit(solution)/shard_map/all_to_all | solution.py:78
  37.4 0.7 copy.82
  38.1 6.2 %all-to-all-done = f32[64,2,2]{2,1,0:T(2,128)S(1)} async-done(((f32[64,2,2]{2,1,0:T(2,128)}), f32[64,2,2]{2,1,0:T(2,128)S(1)}, u32[]{:S(2)}, u32[]{:S(2)}) %all-to-all-start) | async-done | bytes 1056 | tf_op jit(solution)/shard_map/all_to_all | solution.py:78
  44.4 7.4 %all-to-all-start.3 = ((f32[64,2,3]{2,1,0:T(2,128)}), f32[64,2,3]{2,1,0:T(2,128)S(1)}, u32[]{:S(2)}, u32[]{:S(2)}) async-start(f32[64,2,3]{2,1,0:T(2,128)} %copy.82), calls=%async_computation.3 | async-start | bytes 131072 | tf_op jit(solution)/shard_map/all_to_all | solution.py:72
  51.8 8.2 %fusion.31 = f32[64,2,128,128]{3,0,2,1:T(8,128)S(1)} fusion(f32[24,128,128]{2,1,0:T(8,128)} %bitcast.117, f32[64,2,24]{0,2,1:T(8,128)S(1)} %copy.78), kind=kOutput, calls=%fused_computation.38 | convolution fusion | flops 603979776 | bytes 9973760 | tf_op jit(solution)/shard_map/st,tij->sij/dot_general | solution.py:64
  60.0 8.5 %copy.80 = f32[64,2,128,128]{3,2,1,0:T(8,128)} copy(f32[64,2,128,128]{3,0,2,1:T(8,128)S(1)} %fusion.31) | data formatting | bytes 16777216 | tf_op jit(solution)/shard_map/st,tij->sij/dot_general | solution.py:64
  68.5 10.6 %all-to-all-start.2 = ((f32[64,2,128,128]{3,2,1,0:T(8,128)}), f32[64,2,128,128]{3,2,1,0:T(8,128)}, u32[]{:S(2)}, u32[]{:S(2)}) async-start(f32[64,2,128,128]{3,2,1,0:T(8,128)} %copy.80), calls=%async_computation.2 | async-start | bytes 16777216 | tf_op jit(solution)/shard_map/all_to_all | solution.py:65
  82.2 181.3 %all-to-all-done.2 = f32[64,2,128,128]{3,2,1,0:T(8,128)} async-done(((f32[64,2,128,128]{3,2,1,0:T(8,128)}), f32[64,2,128,128]{3,2,1,0:T(8,128)}, u32[]{:S(2)}, u32[]{:S(2)}) %all-to-all-start.2) | async-done | bytes 8388640 | tf_op jit(solution)/shard_map/all_to_all | solution.py:65
  263.5 187.0 %while.14 = (s32[]{:T(128)}, f32[256,256]{1,0:T(8,128)S(1)}, f32[256,256]{1,0:T(8,128)S(1)}, s32[4,32,2]{1,0,2:T(4,128)S(1)}, f32[4,32]{1,0:T(4,128)S(1)}, /*ind...) while((s32[]{:T(128)}, f32[256,256]{1,0:T(8,128)S(1)}, ...), condition=%wide.region_7.8_spmd.clone.clone, body=%wide.region_4.7_spmd.clone.clone.sunk | while | flops 9716891648 | bytes 41520908 | solution.py:122
  263.8 8.8 %convolution_bitcast_fusion.3 = f32[32,3,128,128]{2,3,1,0:T(8,128)S(1)} fusion(f32[4,32,128,128]{3,2,1,0:T(8,128)} %get-tuple-element.295, s32[]{:T(128)S(6)} %copy.131, f32[3,128,128]{2,1,0:T(8,128)S(1)} %get-tuple-element.296), kind=kOutput, calls=%fused_computation.15.clone.1 | convolution fusion | flops 2415919104 | bytes 8585220 | tf_op jit(solution)/shard_map/while/body/eval_jaxpr/bik,nkj->nbij/dot_general | solution.py:29
  272.6 9.9 %fusion.96 = f32[32,3,128,128]{3,2,0,1:T(8,128)S(1)} fusion(f32[32,3,128,128]{2,3,1,0:T(8,128)S(1)} %convolution_bitcast_fusion.3, f32[3,128,128]{2,1,0:T(8,128)S(1)} %get-tuple-element.297), kind=kOutput, calls=%fused_computation.14.clone.1 | convolution fusion | flops 2415919104 | bytes 12779520 | tf_op jit(solution)/shard_map/while/body/eval_jaxpr/nbij,blj->nbil/dot_general | solution.py:30
  282.5 17.0 %fusion.97 = f32[32,1,128,128]{3,1,2,0:T(1,128)S(1)} fusion(f32[32,3,1,1]{1,2,3,0:T(1,128)S(1)} %copy.127, f32[32,3,128,128]{3,2,0,1:T(8,128)S(1)} %fusion.96), kind=kOutput, calls=%fused_computation.2.clone.1 | convolution fusion | flops 18874368 | bytes 8388992 | tf_op jit(solution)/shard_map/while/body/eval_jaxpr/nbil,nb->nil/dot_general | solution.py:31
  299.6 3.9 fusion.99
  303.5 4.9 fusion.100
  308.4 0.7 fusion.101
  309.1 0.7 fusion.102
  310.5 8.7 %convolution_bitcast_fusion.3 = f32[32,3,128,128]{2,3,1,0:T(8,128)S(1)} fusion(f32[4,32,128,128]{3,2,1,0:T(8,128)} %get-tuple-element.295, s32[]{:T(128)S(6)} %copy.131, f32[3,128,128]{2,1,0:T(8,128)S(1)} %get-tuple-element.296), kind=kOutput, calls=%fused_computation.15.clone.1 | convolution fusion | flops 2415919104 | bytes 8585220 | tf_op jit(solution)/shard_map/while/body/eval_jaxpr/bik,nkj->nbij/dot_general | solution.py:29
  319.3 9.9 %fusion.96 = f32[32,3,128,128]{3,2,0,1:T(8,128)S(1)} fusion(f32[32,3,128,128]{2,3,1,0:T(8,128)S(1)} %convolution_bitcast_fusion.3, f32[3,128,128]{2,1,0:T(8,128)S(1)} %get-tuple-element.297), kind=kOutput, calls=%fused_computation.14.clone.1 | convolution fusion | flops 2415919104 | bytes 12779520 | tf_op jit(solution)/shard_map/while/body/eval_jaxpr/nbij,blj->nbil/dot_general | solution.py:30
  329.2 17.0 %fusion.97 = f32[32,1,128,128]{3,1,2,0:T(1,128)S(1)} fusion(f32[32,3,1,1]{1,2,3,0:T(1,128)S(1)} %copy.127, f32[32,3,128,128]{3,2,0,1:T(8,128)S(1)} %fusion.96), kind=kOutput, calls=%fused_computation.2.clone.1 | convolution fusion | flops 18874368 | bytes 8388992 | tf_op jit(solution)/shard_map/while/body/eval_jaxpr/nbil,nb->nil/dot_general | solution.py:31
  346.3 3.9 fusion.99
  350.2 4.9 fusion.100
  355.1 0.7 fusion.101
  355.8 0.7 fusion.102
  357.2 8.7 %convolution_bitcast_fusion.3 = f32[32,3,128,128]{2,3,1,0:T(8,128)S(1)} fusion(f32[4,32,128,128]{3,2,1,0:T(8,128)} %get-tuple-element.295, s32[]{:T(128)S(6)} %copy.131, f32[3,128,128]{2,1,0:T(8,128)S(1)} %get-tuple-element.296), kind=kOutput, calls=%fused_computation.15.clone.1 | convolution fusion | flops 2415919104 | bytes 8585220 | tf_op jit(solution)/shard_map/while/body/eval_jaxpr/bik,nkj->nbij/dot_general | solution.py:29
  366.0 9.9 %fusion.96 = f32[32,3,128,128]{3,2,0,1:T(8,128)S(1)} fusion(f32[32,3,128,128]{2,3,1,0:T(8,128)S(1)} %convolution_bitcast_fusion.3, f32[3,128,128]{2,1,0:T(8,128)S(1)} %get-tuple-element.297), kind=kOutput, calls=%fused_computation.14.clone.1 | convolution fusion | flops 2415919104 | bytes 12779520 | tf_op jit(solution)/shard_map/while/body/eval_jaxpr/nbij,blj->nbil/dot_general | solution.py:30
  375.9 17.0 %fusion.97 = f32[32,1,128,128]{3,1,2,0:T(1,128)S(1)} fusion(f32[32,3,1,1]{1,2,3,0:T(1,128)S(1)} %copy.127, f32[32,3,128,128]{3,2,0,1:T(8,128)S(1)} %fusion.96), kind=kOutput, calls=%fused_computation.2.clone.1 | convolution fusion | flops 18874368 | bytes 8388992 | tf_op jit(solution)/shard_map/while/body/eval_jaxpr/nbil,nb->nil/dot_general | solution.py:31
  393.1 3.9 fusion.99
  397.0 4.9 fusion.100
  401.8 0.7 fusion.101
  402.6 0.7 fusion.102
  404.0 8.7 %convolution_bitcast_fusion.3 = f32[32,3,128,128]{2,3,1,0:T(8,128)S(1)} fusion(f32[4,32,128,128]{3,2,1,0:T(8,128)} %get-tuple-element.295, s32[]{:T(128)S(6)} %copy.131, f32[3,128,128]{2,1,0:T(8,128)S(1)} %get-tuple-element.296), kind=kOutput, calls=%fused_computation.15.clone.1 | convolution fusion | flops 2415919104 | bytes 8585220 | tf_op jit(solution)/shard_map/while/body/eval_jaxpr/bik,nkj->nbij/dot_general | solution.py:29
  412.7 9.9 %fusion.96 = f32[32,3,128,128]{3,2,0,1:T(8,128)S(1)} fusion(f32[32,3,128,128]{2,3,1,0:T(8,128)S(1)} %convolution_bitcast_fusion.3, f32[3,128,128]{2,1,0:T(8,128)S(1)} %get-tuple-element.297), kind=kOutput, calls=%fused_computation.14.clone.1 | convolution fusion | flops 2415919104 | bytes 12779520 | tf_op jit(solution)/shard_map/while/body/eval_jaxpr/nbij,blj->nbil/dot_general | solution.py:30
  422.7 17.0 %fusion.97 = f32[32,1,128,128]{3,1,2,0:T(1,128)S(1)} fusion(f32[32,3,1,1]{1,2,3,0:T(1,128)S(1)} %copy.127, f32[32,3,128,128]{3,2,0,1:T(8,128)S(1)} %fusion.96), kind=kOutput, calls=%fused_computation.2.clone.1 | convolution fusion | flops 18874368 | bytes 8388992 | tf_op jit(solution)/shard_map/while/body/eval_jaxpr/nbil,nb->nil/dot_general | solution.py:31
  439.8 3.9 fusion.99
  443.7 4.9 fusion.100
  448.6 0.7 fusion.101
  449.3 0.7 fusion.102
  450.6 0.7 copy-done.1
  451.4 45.1 %all-reduce.3.cloned.1.call-done = (f32[256,256]{1,0:T(8,128)}, f32[256,256]{1,0:T(8,128)}) async-done(((f32[256,256]{1,0:T(8,128)}, f32[256,256]{1,0:T(8,128)}), (f32[256,256]{1,0:T(8,128)}, f32[256,256]{1,0:T(8,128)})) %all-reduce.3.cloned.1.call-update) | async-done | bytes 524304 | tf_op jit(solution)/shard_map/psum | solution.py:123
  496.6 1.5 divide_bitcast_fusion
  (71 shorter events, 8.4 us)
Async XLA Ops:
  6.5 17.7 %copy-start = (f32[16,3]{0,1:T(4,128)S(1)}, f32[16,3]{0,1:T(4,128)}, u32[]{:S(2)}) copy-start(f32[16,3]{0,1:T(4,128)} %param.14) | copy-start | bytes 580
  11.4 18.4 %all-to-all-start.1 = ((f32[64,1,2]{2,1,0:T(1,128)}), f32[64,1,2]{2,1,0:T(1,128)S(1)}, u32[]{:S(2)}, u32[]{:S(2)}) async-start(f32[64,1,2]{2,1,0:T(1,128)} %copy.77), calls=%async_computation.1 | async-start | bytes 65536 | tf_op jit(solution)/shard_map/all_to_all | solution.py:75
  29.9 14.5 %all-to-all-start = ((f32[64,2,2]{2,1,0:T(2,128)}), f32[64,2,2]{2,1,0:T(2,128)S(1)}, u32[]{:S(2)}, u32[]{:S(2)}) async-start(f32[64,2,2]{2,1,0:T(2,128)} %copy.72), calls=%async_computation | async-start | bytes 131072 | tf_op jit(solution)/shard_map/all_to_all | solution.py:78
  44.4 24.1 %all-to-all-start.3 = ((f32[64,2,3]{2,1,0:T(2,128)}), f32[64,2,3]{2,1,0:T(2,128)S(1)}, u32[]{:S(2)}, u32[]{:S(2)}) async-start(f32[64,2,3]{2,1,0:T(2,128)} %copy.82), calls=%async_computation.3 | async-start | bytes 131072 | tf_op jit(solution)/shard_map/all_to_all | solution.py:72
  68.5 10.7 %copy-start.3 = (f32[3,2,21]{2,1,0:T(2,128)S(1)}, f32[3,2,21]{2,1,0:T(2,128)}, u32[]{:S(2)}) copy-start(f32[3,2,21]{2,1,0:T(2,128)} %param.15) | copy-start | bytes 1516
  68.5 195.0 %all-to-all-start.2 = ((f32[64,2,128,128]{3,2,1,0:T(8,128)}), f32[64,2,128,128]{3,2,1,0:T(8,128)}, u32[]{:S(2)}, u32[]{:S(2)}) async-start(f32[64,2,128,128]{3,2,1,0:T(8,128)} %copy.80), calls=%async_computation.2 | async-start | bytes 16777216 | tf_op jit(solution)/shard_map/all_to_all | solution.py:65
  79.1 417.4 %all-reduce.3.cloned.1.call-start = ((), (), s32[]{:S(2)}) async-start(), calls=%async_computation.4 | async-start | bytes 1048576 | tf_op jit(solution)/shard_map/psum | solution.py:123
  450.6 0.7 copy-start.1
  450.6 0.8 copy-start.2
Sparse Core Ops, SparseCore 0:
  451.5 44.9 all-reduce.2
where the time goes:
time: 511 us; the launch traced here: 505 us
  waiting for transfers between devices  237 us (46%)
  matrix products  191 us (37%)
  starting transfers between devices  37.2 us (7%)
  local copies, waits for them, and re-layouts  14.4 us (3%)
  between operations  13.8 us (3%)
  other arithmetic  11.6 us (2%)
    all_to_all x1, waiting for transfers between devices, body(): lax.all_to_all(packed.reshape(npatch, capacity, pixels, pixels), 'patch',...  181 us
    dot_general x4, matrix products, blur_slots(): jnp.einsum('nbil,nb->nil', smoothed, coeffs, precision=lax.Precision.HIGH...  67.9 us
    psum x1, waiting for transfers between devices, body(): all_num, all_den = lax.psum((numerator, denominator), 'visit')  45.1 us
    dot_general x4, matrix products, blur_slots(): jnp.einsum('nbij,blj->nbil', smoothed, col_mats, precision=lax.Precision....  39.8 us
    dot_general x4, matrix products, blur_slots(): jnp.einsum('bik,nkj->nbij', row_mats, tile_stack, precision=lax.Precision...  35 us
    dot_general x4, matrix products, place_block(): jnp.einsum('naj,nbj->ab', spread, col_pick, precision=lax.Precision.HIGHEST)  19.5 us
    dot_general x4, matrix products, place_block(): jnp.einsum('nai,nij->naj', row_pick, layered, precision=lax.Precision.HIG...  15.6 us
    all_to_all x1, starting transfers between devices, body(): lax.all_to_all(moved_w.reshape(npatch, capacity), 'patch', split_axis=0,...  11.7 us
  transfers between devices with their start and end apart: 5, of which 4 were waited for; matrix products, arithmetic and copies ran while one was open for 5% of the time, Pallas kernels for 0%

commit v1 on v0

v1 whole, which is shorter than its diff:
```python
import functools

import jax
import jax.numpy as jnp
from jax import lax
from jax.experimental import pallas as pl
from jax.experimental.pallas import tpu as pltpu
from jax.sharding import Mesh
from jax.sharding import PartitionSpec as P

PIX = 128
PATCH_PIX = 256
TAPS = 21
MARGIN = TAPS // 2
NB = 3
NX, NZ, NC, NY = 4, 8, 2, 4
STRIP = PATCH_PIX // NY
HALF = 12
F32 = jnp.float32
BF16 = jnp.bfloat16
VMEM_LIMIT = 40 * 1024 * 1024


def split(value):
    high = value.astype(BF16)
    return high, (value - high.astype(F32)).astype(BF16)


def dot(a, b):
    return jnp.dot(a, b, preferred_element_type=F32)


def blur_kernel(first, psf_ref, table_ref, taps_ref, img_ref, var_ref, out_ref, wts_ref,
                col_hi, col_lo, row_hi, row_lo):
    major = lax.broadcasted_iota(jnp.int32, (PIX, PIX), 0)
    minor = lax.broadcasted_iota(jnp.int32, (PIX, PIX), 1)
    for b in range(NB):
        for axis, diff in ((0, minor - major), (1, major - minor)):
            band = jnp.zeros((PIX, PIX), F32)
            for t in range(TAPS):
                band = jnp.where(diff == t - MARGIN, taps_ref[2 * b + axis, t], band)
            hi, lo = split(band)
            place = (slice(None), slice(b * PIX, (b + 1) * PIX))
            if axis:
                col_hi[place], col_lo[place] = hi, lo
            else:
                row_hi[place], row_lo[place] = hi, lo
    for pair in range(HALF // 2):
        x_hi, x_lo = split(img_ref[0, 2 * pair:2 * pair + 2].reshape(2 * PIX, PIX))
        smooth = dot(x_hi, col_hi[...]) + (dot(x_lo, col_hi[...]) + dot(x_hi, col_lo[...]))
        sides = []
        for n in range(2):
            tile = 2 * pair + n
            total = jnp.sum(jnp.sum(var_ref[0, tile], axis=0, keepdims=True), axis=1, keepdims=True)
            weight = 1.0 / (total * (1.0 / (PIX * PIX)))
            wts_ref[tile:tile + 1, :] = jnp.broadcast_to(weight, (1, PIX))
            row = psf_ref[0, first + tile]
            sides.append(jnp.concatenate(
                [smooth[n * PIX:(n + 1) * PIX, b * PIX:(b + 1) * PIX] * (table_ref[row, b] * weight)
                 for b in range(NB)], axis=0))
        q_hi, q_lo = split(jnp.concatenate(sides, axis=1))
        done = dot(row_hi[...], q_hi) + (dot(row_hi[...], q_lo) + dot(row_lo[...], q_hi))
        for n in range(2):
            tile = 2 * pair + n
            out_ref[tile * PIX:(tile + 1) * PIX, :] = done[:, n * PIX:(n + 1) * PIX]


def blur_half(half, psf_index, coeff_table, taps, image, variance):
    smem = pl.BlockSpec(memory_space=pltpu.SMEM)
    tiles = pl.BlockSpec((1, HALF, PIX, PIX), lambda i: (0, half, 0, 0))
    return pl.pallas_call(
        functools.partial(blur_kernel, half * HALF),
        grid=(1,),
        in_specs=[smem, smem, smem, tiles, tiles],
        out_specs=[pl.BlockSpec((HALF * PIX, PIX), lambda i: (0, 0)),
                   pl.BlockSpec((HALF, PIX), lambda i: (0, 0))],
        out_shape=[jax.ShapeDtypeStruct((HALF * PIX, PIX), F32),
                   jax.ShapeDtypeStruct((HALF, PIX), F32)],
        scratch_shapes=[pltpu.VMEM((PIX, NB * PIX), BF16)] * 4,
        compiler_params=pltpu.CompilerParams(vmem_limit_bytes=VMEM_LIMIT),
        cost_estimate=pl.CostEstimate(flops=HALF * 76 * 10**6, bytes_accessed=HALF * 3 * 65536,
                                      transcendentals=0),
        name="blur_half",
    )(psf_index, coeff_table, taps, image, variance)


def place_kernel(fresh, firsts, here_ref, meta_a, meta_b, tiles_a, tiles_b, *refs):
    if fresh:
        mine, theirs, buf, sems = refs
        mine[...] = jnp.zeros(mine.shape, F32)
        theirs[...] = jnp.zeros(theirs.shape, F32)
    else:
        old_mine, old_theirs, mine, theirs, buf, sems = refs
    copies = []
    for n, source in enumerate((tiles_a, tiles_b)):
        copies.append(pltpu.make_async_copy(
            source, buf.at[pl.ds(STRIP + n * HALF * PIX, HALF * PIX)], sems.at[n]))
        copies[-1].start()
    buf[0:STRIP] = jnp.zeros((STRIP, PIX), F32)
    buf[STRIP + 2 * HALF * PIX:] = jnp.zeros((STRIP, PIX), F32)
    if not fresh:
        mine[...] = old_mine[...]
        theirs[...] = old_theirs[...]
    core, strip = here_ref[0], here_ref[1]
    row_of = lax.broadcasted_iota(jnp.int32, (STRIP, PIX), 0)
    lane = lax.broadcasted_iota(jnp.int32, (STRIP, PIX), 1)
    for copy in copies:
        copy.wait()

    def add(canvas, patch, tile_row, skip, col):
        rows = buf[pl.ds(tile_row + skip, STRIP), :]
        rows = pltpu.roll(rows, (col + PIX) & (PIX - 1), 1)
        line = row_of + skip
        inside = (line >= 0) & (line < PIX)
        for side in range(2):
            pixel = lane + (side * PIX - col)
            hit = inside & (pixel >= 0) & (pixel < PIX)
            canvas[patch, side] += jnp.where(hit, rows, 0.0)

    for n, meta in enumerate((meta_a, meta_b)):
        def step(t, carry, n=n, meta=meta):
            for k in range(2):
                at = 6 * (firsts[n] + t) + 3 * k
                patch, row, col = meta[at], meta[at + 1], meta[at + 2]
                skip = strip * STRIP - row
                tile_row = STRIP + (n * HALF + t) * PIX
                touched = (skip > -STRIP) & (skip < PIX)
                own = (patch & 1) == core

                @pl.when(touched & own)
                def _():
                    add(mine, patch >> 1, tile_row, skip, col)

                @pl.when(touched & jnp.logical_not(own))
                def _():
                    add(theirs, patch >> 1, tile_row, skip, col)
            return carry

        lax.fori_loop(0, HALF, step, 0)


def place(here, metas, firsts, tiles, canvas):
    smem = pl.BlockSpec(memory_space=pltpu.SMEM)
    hbm = pl.BlockSpec(memory_space=pl.ANY)
    vmem = pl.BlockSpec(memory_space=pltpu.VMEM)
    shape = jax.ShapeDtypeStruct((NX * NZ, 2, STRIP, PIX), F32)
    fresh = canvas is None
    return pl.pallas_call(
        functools.partial(place_kernel, fresh, firsts),
        in_specs=[smem] * 3 + [hbm] * 2 + ([] if fresh else [vmem] * 2),
        out_specs=[vmem] * 2,
        out_shape=[shape] * 2,
        scratch_shapes=[pltpu.VMEM((2 * STRIP + 2 * HALF * PIX, PIX), F32),
                        pltpu.SemaphoreType.DMA((2,))],
        compiler_params=pltpu.CompilerParams(vmem_limit_bytes=VMEM_LIMIT),
        cost_estimate=pl.CostEstimate(flops=20 * 10**6, bytes_accessed=10 * 10**6, transcendentals=0),
        name="place",
    )(here, *metas, *tiles, *(() if fresh else canvas))


def shift(value, axis, by):
    size = lax.axis_size(axis)
    return lax.ppermute(value, axis, [(i, (i + by) % size) for i in range(size)])


def weight_sums(weights, patches, offsets, strip):
    tile_dev = weights.shape[0]
    npatch = NX * NZ * NC
    pairs = tile_dev * 2
    targets = patches.reshape(pairs)
    matches = (targets[:, None] == jnp.arange(npatch, dtype=jnp.int32)[None, :]).astype(jnp.int32)
    earlier = jnp.sum((jnp.cumsum(matches, axis=0) - matches) * matches, axis=1)
    slot_of = targets * 2 + earlier
    chooser = (jnp.arange(npatch * 2, dtype=jnp.int32)[:, None] == slot_of[None, :]).astype(F32)
    payload = jnp.concatenate(
        [jnp.repeat(weights, 2)[:, None], offsets.reshape(pairs, 2).astype(F32)], axis=1)
    sent = jnp.dot(chooser, payload, precision=lax.Precision.HIGHEST).reshape(npatch, 6)
    got = lax.all_to_all(sent, ("x", "z", "core"), 0, 0, tiled=True)
    every = jnp.stack([got] + [shift(got, "y", k) for k in (1, 2, 3)]).reshape(-1, 3)
    rows = strip * STRIP + jnp.arange(STRIP, dtype=jnp.int32)
    cols = jnp.arange(PATCH_PIX, dtype=jnp.int32)
    row_at = rows[None, :] - every[:, 1:2].astype(jnp.int32)
    col_at = cols[None, :] - every[:, 2:3].astype(jnp.int32)
    row_hit = ((row_at >= 0) & (row_at < PIX)).astype(F32) * every[:, 0:1]
    col_hit = ((col_at >= 0) & (col_at < PIX)).astype(F32)
    return jnp.einsum("na,nb->ab", row_hit, col_hit, precision=lax.Precision.HIGHEST)


def body(image, variance, patches, offsets, psf_index, coeff_table, basis_taps):
    strip = lax.axis_index("y")
    here = jnp.stack([lax.axis_index("core"), strip]).astype(jnp.int32)
    taps = basis_taps.reshape(NB * 2, TAPS)
    meta = jnp.concatenate([patches[0][..., None], offsets[0]], axis=-1).reshape(-1)
    own_a, wts_a = blur_half(0, psf_index, coeff_table, taps, image, variance)
    own_b, wts_b = blur_half(1, psf_index, coeff_table, taps, image, variance)

    meta_left, meta_right, meta_far = (shift(meta, "y", k) for k in (1, -1, 2))
    left_a = shift(own_a, "y", 1)
    right_b = shift(own_b, "y", -1)
    left_a, right_b, next_a, next_b = lax.optimization_barrier((left_a, right_b, own_a, own_b))
    far_a = shift(left_a, "y", 1)
    far_b = shift(right_b, "y", -1)
    left_b = shift(next_b, "y", 1)
    right_a = shift(next_a, "y", -1)

    canvas = place(here, (meta, meta), (0, HALF), (own_a, own_b), None)
    canvas = place(here, (meta_left, meta_right), (0, HALF), (left_a, right_b), canvas)
    canvas = place(here, (meta_left, meta_right), (HALF, 0), (left_b, right_a), canvas)
    mine, theirs = place(here, (meta_far, meta_far), (0, HALF), (far_a, far_b), canvas)

    weights = jnp.concatenate([wts_a[:, 0], wts_b[:, 0]])
    denominator = weight_sums(weights, patches, offsets, strip)

    partial = mine + shift(theirs, "core", 1)
    partial = partial.reshape(NX, NZ * 2 * STRIP, PIX)
    partial = lax.all_to_all(partial, "x", 0, 0, tiled=True).sum(axis=0)
    partial = partial.reshape(NZ, 2 * STRIP, PIX)
    total = lax.all_to_all(partial, "z", 0, 0, tiled=True).sum(axis=0)
    numerator = jnp.concatenate([total[:STRIP], total[STRIP:]], axis=1)
    return (numerator / (denominator + 1.0))[None]


def solution(mesh):
    fine = Mesh(mesh.devices.reshape(NX, NZ, NC, NY), ("x", "z", "core", "y"))
    own = ("x", "z", "core")
    return jax.shard_map(
        body,
        mesh=fine,
        in_specs=(
            P("y", own, None, None),
            P("y", own, None, None),
            P("y", own, None),
            P("y", own, None, None),
            P("y", own),
            P(),
            P(),
        ),
        out_specs=P(own, "y", None),
        check_vma=False,
    )
```

time: 511 us -> 170 us (0.33)
  the two profiles are of different devices: /device:TPU:62 before, /device:TPU:9 now
where the time goes in v1:
time: 170 us
  waiting for transfers between devices  97.6 us (57%)
  starting transfers between devices  34.4 us (20%)
  Pallas kernels  25.7 us (15%)
  local copies, waits for them, and re-layouts  6.87 us (4%)
  other arithmetic  3.61 us (2%)
    ppermute x13, waiting for transfers between devices, shift(): lax.ppermute(value, axis, [(i, (i + by) % size) for i in range(size)])  53.9 us
    all_to_all x1, waiting for transfers between devices, body(): partial = lax.all_to_all(partial, 'x', 0, 0, tiled=True).sum(axis=0)  23.7 us
    pallas_call x4, Pallas kernels, place(): pl.pallas_call(functools.partial(place_kernel, fresh, firsts), in_specs=[...  19.2 us
    ppermute x13, starting transfers between devices, shift(): lax.ppermute(value, axis, [(i, (i + by) % size) for i in range(size)])  14.5 us
    all_to_all x1, waiting for transfers between devices, body(): total = lax.all_to_all(partial, 'z', 0, 0, tiled=True).sum(axis=0)  11.8 us
    all_to_all x1, starting transfers between devices, weight_sums(): got = lax.all_to_all(sent, ('x', 'z', 'core'), 0, 0, tiled=True)  11.4 us
    all_to_all x1, waiting for transfers between devices, weight_sums(): got = lax.all_to_all(sent, ('x', 'z', 'core'), 0, 0, tiled=True)  8.27 us
    pallas_call x2, Pallas kernels, blur_half(): pl.pallas_call(functools.partial(blur_kernel, half * HALF), grid=(1,), in...  6.58 us
  transfers between devices with their start and end apart: 16, of which 8 were waited for; matrix products, arithmetic and copies ran while one was open for 2% of the time, Pallas kernels for 10%

profile of v1, /device:TPU:9, one launch (start us, length us, event | category | flops | bytes accessed | tf_op | source)
XLA Modules:
  0.0 169.9 jit_solution(12997608685355997917)
XLA Ops:
  0.0 0.8 copy.35.table_ref
  0.8 0.7 reshape.39.taps_ref
  1.5 1.4 copy-done
  2.9 1.4 copy-done.2
  4.3 0.7 copy-done.3
  4.9 3.3 %blur_half.2 = (f32[1536,128]{1,0:T(8,128)S(1)}, f32[12,128]{1,0:T(8,128)S(1)}) custom-call(s32[1,24]{1,0:T(1,128)S(1)} %copy-done.3, f32[16,3]{1,0:T(8,128)S(1)} %copy.35.table_ref, f32[6,21]{1,0:T(8,128)S(1)} %reshape.39.taps_ref, f32[1,24,128,128]{3,2,1,0:T(8,128)S(1)} %copy-done, f32[1,24,128,128]{3,2,1,0:T(8,128)S(1)} %copy-done.2), custom_call_target="tpu_custom_call" | custom-call | flops 912000000 | bytes 2359296 | tf_op jit(solution)/shard_map/blur_half/pallas_call | solution.py:71
  8.2 1.4 collective-permute-start.1
  9.6 3.3 %blur_half.3 = (f32[1536,128]{1,0:T(8,128)S(1)}, f32[12,128]{1,0:T(8,128)S(1)}) custom-call(s32[1,24]{1,0:T(1,128)S(1)} %copy-done.3, f32[16,3]{1,0:T(8,128)S(1)} %copy.35.table_ref, f32[6,21]{1,0:T(8,128)S(1)} %reshape.39.taps_ref, f32[1,24,128,128]{3,2,1,0:T(8,128)S(1)} %copy-done.1, f32[1,24,128,128]{3,2,1,0:T(8,128)S(1)} %copy-done.2), custom_call_target="tpu_custom_call" | custom-call | flops 912000000 | bytes 2359296 | tf_op jit(solution)/shard_map/blur_half/pallas_call | solution.py:71
  12.9 0.2 collective-permute-start.2
  13.2 13.4 %collective-permute-done.1.tiles_a = f32[1536,128]{1,0:T(8,128)S(1)} collective-permute-done((f32[1536,128]{1,0:T(8,128)S(1)}, f32[1536,128]{1,0:T(8,128)S(1)}, u32[]{:S(2)}, u32[]{:S(2)}) %collective-permute-start.1) | collective-permute-done | bytes 786464 | tf_op jit(solution)/shard_map/ppermute | solution.py:163
  26.5 4.5 %collective-permute-done.2.tiles_b = f32[1536,128]{1,0:T(8,128)S(1)} collective-permute-done((f32[1536,128]{1,0:T(8,128)S(1)}, f32[1536,128]{1,0:T(8,128)S(1)}, u32[]{:S(2)}, u32[]{:S(2)}) %collective-permute-start.2) | collective-permute-done | bytes 786464 | tf_op jit(solution)/shard_map/ppermute | solution.py:163
  31.1 1.0 collective-permute-start.7
  32.1 0.5 collective-permute-start.8
  32.6 1.0 collective-permute-start.3
  33.6 0.5 collective-permute-start.4
  34.0 0.1 copy.34
  34.1 0.1 reshape.38.meta_a.meta_b
  34.3 1.1 collective-permute-start.5
  35.4 29.8 %collective-permute-done.5.meta_a = s32[144]{0:T(256)S(1)} collective-permute-done((s32[144]{0:T(256)S(1)}, s32[144]{0:T(256)S(1)}, u32[]{:S(2)}, u32[]{:S(2)}) %collective-permute-start.5) | collective-permute-done | bytes 608 | tf_op jit(solution)/shard_map/ppermute | solution.py:163
  65.2 1.0 collective-permute-start.6
  66.2 4.3 %place.4 = (f32[32,2,64,128]{3,2,1,0:T(8,128)S(1)}, f32[32,2,64,128]{3,2,1,0:T(8,128)S(1)}) custom-call(s32[2]{0:T(128)S(1)} %pad_add_fusion.1.here_ref, s32[144]{0:T(256)S(1)} %reshape.38.meta_a.meta_b, s32[144]{0:T(256)S(1)} %reshape.38.meta_a.meta_b, f32[1536,128]{1,0:T(8,128)S(1)} %get-tuple-element.26.tiles_a, f32[1536,128]{1,0:T(8,128)S(1)} %get-tuple-element.25.tiles_b), custom_call_target="tpu_custom_call" | custom-call | flops 20000000 | bytes 10000000 | tf_op jit(solution)/shard_map/place/pallas_call | solution.py:148
  70.5 0.8 collective-permute-start
  71.3 4.5 %place.5 = (f32[32,2,64,128]{3,2,1,0:T(8,128)S(1)}, f32[32,2,64,128]{3,2,1,0:T(8,128)S(1)}) custom-call(s32[2]{0:T(128)S(1)} %pad_add_fusion.1.here_ref, s32[144]{0:T(256)S(1)} %collective-permute-done.5.meta_a, s32[144]{0:T(256)S(1)} %collective-permute-done.6.meta_b, f32[1536,128]{1,0:T(8,128)S(1)} %collective-permute-done.1.tiles_a, ...), custom_call_target="tpu_custom_call" | custom-call | flops 20000000 | bytes 10000000 | tf_op jit(solution)/shard_map/place/pallas_call | solution.py:148
  75.9 5.2 %place.6 = (f32[32,2,64,128]{3,2,1,0:T(8,128)S(1)}, f32[32,2,64,128]{3,2,1,0:T(8,128)S(1)}) custom-call(s32[2]{0:T(128)S(1)} %pad_add_fusion.1.here_ref, s32[144]{0:T(256)S(1)} %collective-permute-done.5.meta_a, s32[144]{0:T(256)S(1)} %collective-permute-done.6.meta_b, f32[1536,128]{1,0:T(8,128)} %collective-permute-done.7.tiles_a, ...), custom_call_target="tpu_custom_call" | custom-call | flops 20000000 | bytes 10000000 | tf_op jit(solution)/shard_map/place/pallas_call | solution.py:148
  81.1 5.2 %place.7 = (f32[32,2,64,128]{3,2,1,0:T(8,128)S(1)}, f32[32,2,64,128]{3,2,1,0:T(8,128)S(1)}) custom-call(s32[2]{0:T(128)S(1)} %pad_add_fusion.1.here_ref, s32[144]{0:T(256)S(1)} %collective-permute-done.meta_a.meta_b, s32[144]{0:T(256)S(1)} %collective-permute-done.meta_a.meta_b, f32[1536,128]{1,0:T(8,128)} %collective-permute-done.3.tiles_a, ...), custom_call_target="tpu_custom_call" | custom-call | flops 20000000 | bytes 10000000 | tf_op jit(solution)/shard_map/place/pallas_call | solution.py:148
  86.3 4.0 %collective-permute-start.9 = (f32[32,2,64,128]{3,2,1,0:T(8,128)S(1)}, f32[32,2,64,128]{3,2,1,0:T(8,128)S(1)}, u32[]{:S(2)}, u32[]{:S(2)}) collective-permute-start(f32[32,2,64,128]{3,2,1,0:T(8,128)S(1)} %get-tuple-element.34), channel_id=1, source_target_pairs={{0,4},{4,0},{1,5},{5,1},{2,6},{6,2},{3,7},{7,3},{8,12},{12,8},{9,1... | collective-permute-start | bytes 6291464 | tf_op jit(solution)/shard_map/ppermute | solution.py:163
  90.3 3.8 %collective-permute-done.9 = f32[32,2,64,128]{3,2,1,0:T(8,128)S(1)} collective-permute-done((f32[32,2,64,128]{3,2,1,0:T(8,128)S(1)}, f32[32,2,64,128]{3,2,1,0:T(8,128)S(1)}, u32[]{:S(2)}, u32[]{:S(2)}) %collective-permute-start.9) | collective-permute-done | bytes 2097184 | tf_op jit(solution)/shard_map/ppermute | solution.py:163
  94.1 1.7 %add.26 = f32[32,2,64,128]{3,2,1,0:T(8,128)} add(f32[32,2,64,128]{3,2,1,0:T(8,128)S(1)} %get-tuple-element.33, f32[32,2,64,128]{3,2,1,0:T(8,128)S(1)} %collective-permute-done.9) | non-fusion elementwise | flops 524288 | bytes 6291456 | tf_op jit(solution)/shard_map/add | solution.py:214
  95.9 4.9 %all-to-all-start = ((f32[4,1024,128]{2,1,0:T(8,128)}), f32[4,1024,128]{2,1,0:T(8,128)S(1)}, u32[]{:S(2)}, u32[]{:S(2)}) async-start(f32[4,1024,128]{2,1,0:T(8,128)} %bitcast.5), calls=%async_computation | async-start | bytes 4194304 | tf_op jit(solution)/shard_map/all_to_all | solution.py:216
  100.9 0.1 slice_reduce_fusion.1
  101.0 0.1 slice_reduce_fusion.2
  101.3 0.1 broadcast_in_dim_reshape.4
  101.8 0.2 select_reduce_fusion
  102.0 0.2 fusion.21
  102.2 0.7 all_to_all.16
  102.9 23.7 %all-to-all-done = f32[4,1024,128]{2,1,0:T(8,128)S(1)} async-done(((f32[4,1024,128]{2,1,0:T(8,128)}), f32[4,1024,128]{2,1,0:T(8,128)S(1)}, u32[]{:S(2)}, u32[]{:S(2)}) %all-to-all-start) | async-done | bytes 2097184 | tf_op jit(solution)/shard_map/all_to_all | solution.py:216
  126.6 11.4 %all-to-all-start.2 = ((f32[64,1,6]{2,1,0:T(1,128)}), f32[64,1,6]{2,1,0:T(1,128)S(1)}, u32[]{:S(2)}, u32[]{:S(2)}) async-start(f32[64,1,6]{2,1,0:T(1,128)} %bitcast.7), calls=%async_computation.2 | async-start | bytes 65536 | tf_op jit(solution)/shard_map/all_to_all | solution.py:178
  138.0 0.9 reduce_sum.27
  139.0 8.3 %all-to-all-done.2 = f32[64,1,6]{2,1,0:T(1,128)S(1)} async-done(((f32[64,1,6]{2,1,0:T(1,128)}), f32[64,1,6]{2,1,0:T(1,128)S(1)}, u32[]{:S(2)}, u32[]{:S(2)}) %all-to-all-start.2) | async-done | bytes 1568 | tf_op jit(solution)/shard_map/all_to_all | solution.py:178
  147.2 3.5 %all-to-all-start.1 = ((f32[8,128,128]{2,1,0:T(8,128)}), f32[8,128,128]{2,1,0:T(8,128)S(1)}, u32[]{:S(2)}, u32[]{:S(2)}) async-start(f32[8,128,128]{2,1,0:T(8,128)} %bitcast.6), calls=%async_computation.1 | async-start | bytes 1048576 | tf_op jit(solution)/shard_map/all_to_all | solution.py:218
  150.7 1.2 collective-permute-start.10
  151.9 1.9 %collective-permute-start.12 = (f32[64,6]{1,0:T(8,128)S(1)}, f32[64,6]{1,0:T(8,128)S(1)}, u32[]{:S(2)}, u32[]{:S(2)}) collective-permute-start(f32[64,6]{1,0:T(8,128)S(1)} %bitcast.22), channel_id=1, source_target_pairs={{0,3},{1,0},{2,1},{3,2},{4,7},{5,4},{6,5},{7,6},{8,11},{9,8},{10,9... | collective-permute-start | bytes 4616 | tf_op jit(solution)/shard_map/ppermute | solution.py:163
  153.8 2.4 %collective-permute-done.11 = f32[64,6]{1,0:T(8,128)S(1)} collective-permute-done((f32[64,6]{1,0:T(8,128)S(1)}, f32[64,6]{1,0:T(8,128)S(1)}, u32[]{:S(2)}, u32[]{:S(2)}) %collective-permute-start.11) | collective-permute-done | bytes 1568 | tf_op jit(solution)/shard_map/ppermute | solution.py:163
  156.2 0.1 reshape.43
  156.3 0.1 slice_reduce_fusion
  156.5 0.4 fusion.8
  156.8 11.8 %all-to-all-done.1 = f32[8,128,128]{2,1,0:T(8,128)S(1)} async-done(((f32[8,128,128]{2,1,0:T(8,128)}), f32[8,128,128]{2,1,0:T(8,128)S(1)}, u32[]{:S(2)}, u32[]{:S(2)}) %all-to-all-start.1) | async-done | bytes 524320 | tf_op jit(solution)/shard_map/all_to_all | solution.py:218
  168.6 1.3 fusion.1
  (34 shorter events, 0.9 us)
Async XLA Ops:
  1.4 1.4 copy-start
  2.9 1.4 copy-start.2
  4.3 0.7 copy-start.3
  4.9 4.7 %copy-start.1 = (f32[1,24,128,128]{3,2,1,0:T(8,128)S(1)}, f32[1,24,128,128]{3,2,1,0:T(8,128)}, u32[]{:S(2)}) copy-start(f32[1,24,128,128]{3,2,1,0:T(8,128)} %img_ref.3) | copy-start | bytes 4718596
  8.2 25.8 %copy-start.4 = (s32[1,24,2,2]{1,3,2,0:T(2,128)S(1)}, s32[1,24,2,2]{1,3,2,0:T(2,128)}, u32[]{:S(2)}) copy-start(s32[1,24,2,2]{1,3,2,0:T(2,128)} %param.10) | copy-start | bytes 1156
  8.2 25.8 %copy-start.5 = (s32[1,24,2]{1,2,0:T(2,128)S(1)}, s32[1,24,2]{1,2,0:T(2,128)}, u32[]{:S(2)}) copy-start(s32[1,24,2]{1,2,0:T(2,128)} %param.9) | copy-start | bytes 580
  8.2 18.3 %collective-permute-start.1 = (f32[1536,128]{1,0:T(8,128)S(1)}, f32[1536,128]{1,0:T(8,128)S(1)}, u32[]{:S(2)}, u32[]{:S(2)}) collective-permute-start(f32[1536,128]{1,0:T(8,128)S(1)} %get-tuple-element.26.tiles_a), channel_id=1, source_target_pairs={{0,1},{1,2},{2,3},{3,0},{4,5},{5,6},{6,7},{7,4},{8,9},{9,10},{10,1... | collective-permute-start | bytes 2359304 | tf_op jit(solution)/shard_map/ppermute | solution.py:163
  12.9 18.2 %collective-permute-start.2 = (f32[1536,128]{1,0:T(8,128)S(1)}, f32[1536,128]{1,0:T(8,128)S(1)}, u32[]{:S(2)}, u32[]{:S(2)}) collective-permute-start(f32[1536,128]{1,0:T(8,128)S(1)} %get-tuple-element.25.tiles_b), channel_id=1, source_target_pairs={{0,3},{1,0},{2,1},{3,2},{4,7},{5,4},{6,5},{7,6},{8,11},{9,8},{10,9... | collective-permute-start | bytes 2359304 | tf_op jit(solution)/shard_map/ppermute | solution.py:163
  31.1 44.8 %collective-permute-start.7 = (f32[1536,128]{1,0:T(8,128)S(1)}, f32[1536,128]{1,0:T(8,128)}, u32[]{:S(2)}, u32[]{:S(2)}) collective-permute-start(f32[1536,128]{1,0:T(8,128)S(1)} %get-tuple-element.25.tiles_b), channel_id=1, source_target_pairs={{0,1},{1,2},{2,3},{3,0},{4,5},{5,6},{6,7},{7,4},{8,9},{9,10},{10,1... | collective-permute-start | bytes 2359304 | tf_op jit(solution)/shard_map/ppermute | solution.py:163
  32.1 43.8 %collective-permute-start.8 = (f32[1536,128]{1,0:T(8,128)S(1)}, f32[1536,128]{1,0:T(8,128)}, u32[]{:S(2)}, u32[]{:S(2)}) collective-permute-start(f32[1536,128]{1,0:T(8,128)S(1)} %get-tuple-element.26.tiles_a), channel_id=1, source_target_pairs={{0,3},{1,0},{2,1},{3,2},{4,7},{5,4},{6,5},{7,6},{8,11},{9,8},{10,9... | collective-permute-start | bytes 2359304 | tf_op jit(solution)/shard_map/ppermute | solution.py:163
  32.6 48.6 %collective-permute-start.3 = (f32[1536,128]{1,0:T(8,128)S(1)}, f32[1536,128]{1,0:T(8,128)}, u32[]{:S(2)}, u32[]{:S(2)}) collective-permute-start(f32[1536,128]{1,0:T(8,128)S(1)} %collective-permute-done.1.tiles_a), channel_id=1, source_target_pairs={{0,1},{1,2},{2,3},{3,0},{4,5},{5,6},{6,7},{7,4},{8,9},{9,10},{10,1... | collective-permute-start | bytes 2359304 | tf_op jit(solution)/shard_map/ppermute | solution.py:163
  33.6 47.6 %collective-permute-start.4 = (f32[1536,128]{1,0:T(8,128)S(1)}, f32[1536,128]{1,0:T(8,128)}, u32[]{:S(2)}, u32[]{:S(2)}) collective-permute-start(f32[1536,128]{1,0:T(8,128)S(1)} %collective-permute-done.2.tiles_b), channel_id=1, source_target_pairs={{0,3},{1,0},{2,1},{3,2},{4,7},{5,4},{6,5},{7,6},{8,11},{9,8},{10,9... | collective-permute-start | bytes 2359304 | tf_op jit(solution)/shard_map/ppermute | solution.py:163
  34.3 31.0 %collective-permute-start.5 = (s32[144]{0:T(256)S(1)}, s32[144]{0:T(256)S(1)}, u32[]{:S(2)}, u32[]{:S(2)}) collective-permute-start(s32[144]{0:T(256)S(1)} %reshape.38.meta_a.meta_b), channel_id=1, source_target_pairs={{0,1},{1,2},{2,3},{3,0},{4,5},{5,6},{6,7},{7,4},{8,9},{9,10},{10,1... | collective-permute-start | bytes 1736 | tf_op jit(solution)/shard_map/ppermute | solution.py:163
  65.2 5.3 %collective-permute-start.6 = (s32[144]{0:T(256)S(1)}, s32[144]{0:T(256)S(1)}, u32[]{:S(2)}, u32[]{:S(2)}) collective-permute-start(s32[144]{0:T(256)S(1)} %reshape.38.meta_a.meta_b), channel_id=1, source_target_pairs={{0,3},{1,0},{2,1},{3,2},{4,7},{5,4},{6,5},{7,6},{8,11},{9,8},{10,9... | collective-permute-start | bytes 1736 | tf_op jit(solution)/shard_map/ppermute | solution.py:163
  70.5 10.6 %collective-permute-start = (s32[144]{0:T(256)S(1)}, s32[144]{0:T(256)S(1)}, u32[]{:S(2)}, u32[]{:S(2)}) collective-permute-start(s32[144]{0:T(256)S(1)} %reshape.38.meta_a.meta_b), channel_id=1, source_target_pairs={{0,2},{1,3},{2,0},{3,1},{4,6},{5,7},{6,4},{7,5},{8,10},{9,11},{10,... | collective-permute-start | bytes 1736 | tf_op jit(solution)/shard_map/ppermute | solution.py:163
  86.3 7.8 %collective-permute-start.9 = (f32[32,2,64,128]{3,2,1,0:T(8,128)S(1)}, f32[32,2,64,128]{3,2,1,0:T(8,128)S(1)}, u32[]{:S(2)}, u32[]{:S(2)}) collective-permute-start(f32[32,2,64,128]{3,2,1,0:T(8,128)S(1)} %get-tuple-element.34), channel_id=1, source_target_pairs={{0,4},{4,0},{1,5},{5,1},{2,6},{6,2},{3,7},{7,3},{8,12},{12,8},{9,1... | collective-permute-start | bytes 6291464 | tf_op jit(solution)/shard_map/ppermute | solution.py:163
  95.9 30.7 %all-to-all-start = ((f32[4,1024,128]{2,1,0:T(8,128)}), f32[4,1024,128]{2,1,0:T(8,128)S(1)}, u32[]{:S(2)}, u32[]{:S(2)}) async-start(f32[4,1024,128]{2,1,0:T(8,128)} %bitcast.5), calls=%async_computation | async-start | bytes 4194304 | tf_op jit(solution)/shard_map/all_to_all | solution.py:216
  126.6 20.7 %all-to-all-start.2 = ((f32[64,1,6]{2,1,0:T(1,128)}), f32[64,1,6]{2,1,0:T(1,128)S(1)}, u32[]{:S(2)}, u32[]{:S(2)}) async-start(f32[64,1,6]{2,1,0:T(1,128)} %bitcast.7), calls=%async_computation.2 | async-start | bytes 65536 | tf_op jit(solution)/shard_map/all_to_all | solution.py:178
  147.2 21.4 %all-to-all-start.1 = ((f32[8,128,128]{2,1,0:T(8,128)}), f32[8,128,128]{2,1,0:T(8,128)S(1)}, u32[]{:S(2)}, u32[]{:S(2)}) async-start(f32[8,128,128]{2,1,0:T(8,128)} %bitcast.6), calls=%async_computation.1 | async-start | bytes 1048576 | tf_op jit(solution)/shard_map/all_to_all | solution.py:218
  150.7 3.0 %collective-permute-start.10 = (f32[64,6]{1,0:T(8,128)S(1)}, f32[64,6]{1,0:T(8,128)S(1)}, u32[]{:S(2)}, u32[]{:S(2)}) collective-permute-start(f32[64,6]{1,0:T(8,128)S(1)} %bitcast.20), channel_id=1, source_target_pairs={{0,1},{1,2},{2,3},{3,0},{4,5},{5,6},{6,7},{7,4},{8,9},{9,10},{10,1... | collective-permute-start | bytes 4616 | tf_op jit(solution)/shard_map/ppermute | solution.py:163
  151.9 4.3 %collective-permute-start.11 = (f32[64,6]{1,0:T(8,128)S(1)}, f32[64,6]{1,0:T(8,128)S(1)}, u32[]{:S(2)}, u32[]{:S(2)}) collective-permute-start(f32[64,6]{1,0:T(8,128)S(1)} %bitcast.21), channel_id=1, source_target_pairs={{0,2},{1,3},{2,0},{3,1},{4,6},{5,7},{6,4},{7,5},{8,10},{9,11},{10,... | collective-permute-start | bytes 4616 | tf_op jit(solution)/shard_map/ppermute | solution.py:163
  151.9 4.3 %collective-permute-start.12 = (f32[64,6]{1,0:T(8,128)S(1)}, f32[64,6]{1,0:T(8,128)S(1)}, u32[]{:S(2)}, u32[]{:S(2)}) collective-permute-start(f32[64,6]{1,0:T(8,128)S(1)} %bitcast.22), channel_id=1, source_target_pairs={{0,3},{1,0},{2,1},{3,2},{4,7},{5,4},{6,5},{7,6},{8,11},{9,8},{10,9... | collective-permute-start | bytes 4616 | tf_op jit(solution)/shard_map/ppermute | solution.py:163

commit v2 on v1

v2 whole, which is shorter than its diff:
```python
import functools

import jax
import jax.numpy as jnp
from jax import lax
from jax.experimental import pallas as pl
from jax.experimental.pallas import tpu as pltpu
from jax.sharding import Mesh
from jax.sharding import PartitionSpec as P

PIX = 128
PATCH_PIX = 256
TAPS = 21
MARGIN = TAPS // 2
NB = 3
NX, NZ, NC, NY = 4, 8, 2, 4
STRIP = PATCH_PIX // NY
HALF = 12
STEP = 6
UNROLL = 3
META = 8
F32 = jnp.float32
BF16 = jnp.bfloat16
BLUR_LIMIT = 56 * 1024 * 1024
PLACE_LIMIT = 24 * 1024 * 1024
ADD_LIMIT = 8 * 1024 * 1024


def split(value):
    high = value.astype(BF16)
    return high, (value - high.astype(F32)).astype(BF16)


def dot(a, b):
    return jnp.dot(a, b, preferred_element_type=F32)


def blur_kernel(first, psf_ref, table_ref, taps_ref, patch_ref, offset_ref, img_ref, var_ref, out_ref, wts_ref,
                col_hi, col_lo, row_hi, row_lo):
    now = pl.program_id(0)

    @pl.when(now == 0)
    def _():
        major = lax.broadcasted_iota(jnp.int32, (PIX, PIX), 0)
        minor = lax.broadcasted_iota(jnp.int32, (PIX, PIX), 1)
        for b in range(NB):
            for axis, diff in ((0, minor - major), (1, major - minor)):
                band = jnp.zeros((PIX, PIX), F32)
                for t in range(TAPS):
                    band = jnp.where(diff == t - MARGIN, taps_ref[b, axis, t], band)
                hi, lo = split(band)
                place = (slice(None), slice(b * PIX, (b + 1) * PIX))
                if axis:
                    col_hi[place], col_lo[place] = hi, lo
                else:
                    row_hi[place], row_lo[place] = hi, lo
        lane = lax.broadcasted_iota(jnp.int32, (META, PIX), 1)
        facts = jnp.zeros((META, PIX), jnp.int32)
        for n in range(HALF):
            for k in range(2):
                values = (patch_ref[0, k, first + n], offset_ref[0, k, 0, first + n], offset_ref[0, k, 1, first + n])
                for m, value in enumerate(values):
                    facts = jnp.where(lane == 6 * n + 3 * k + m, value, facts)
        out_ref[0:META, :] = facts.astype(F32)

    for pair in range(STEP // 2):
        x_hi, x_lo = split(img_ref[0, 2 * pair:2 * pair + 2].reshape(2 * PIX, PIX))
        smooth = dot(x_hi, col_hi[...]) + (dot(x_lo, col_hi[...]) + dot(x_hi, col_lo[...]))
        sides = []
        for n in range(2):
            tile = now * STEP + 2 * pair + n
            total = jnp.sum(jnp.sum(var_ref[0, 2 * pair + n], axis=0, keepdims=True), axis=1, keepdims=True)
            weight = 1.0 / (total * (1.0 / (PIX * PIX)))
            wts_ref[pl.ds(tile, 1), :] = jnp.broadcast_to(weight, (1, PIX))
            row = psf_ref[0, first + tile]
            sides.append(jnp.concatenate(
                [smooth[n * PIX:(n + 1) * PIX, b * PIX:(b + 1) * PIX] * (table_ref[b, row] * weight)
                 for b in range(NB)], axis=0))
        q_hi, q_lo = split(jnp.concatenate(sides, axis=1))
        done = dot(row_hi[...], q_hi) + (dot(row_hi[...], q_lo) + dot(row_lo[...], q_hi))
        for n in range(2):
            tile = now * STEP + 2 * pair + n
            out_ref[pl.ds(META + tile * PIX, PIX), :] = done[:, n * PIX:(n + 1) * PIX]


def blur_half(half, psf_index, table, taps, patches, offsets, image, variance):
    smem = pl.BlockSpec(memory_space=pltpu.SMEM)
    tiles = pl.BlockSpec((1, STEP, PIX, PIX), lambda i: (0, half * HALF // STEP + i, 0, 0))
    rows = META + HALF * PIX
    return pl.pallas_call(
        functools.partial(blur_kernel, half * HALF),
        grid=(HALF // STEP,),
        in_specs=[smem] * 5 + [tiles, tiles],
        out_specs=[pl.BlockSpec((rows, PIX), lambda i: (0, 0)),
                   pl.BlockSpec((HALF, PIX), lambda i: (0, 0))],
        out_shape=[jax.ShapeDtypeStruct((rows, PIX), F32),
                   jax.ShapeDtypeStruct((HALF, PIX), F32)],
        scratch_shapes=[pltpu.VMEM((PIX, NB * PIX), BF16)] * 4,
        compiler_params=pltpu.CompilerParams(vmem_limit_bytes=BLUR_LIMIT),
        cost_estimate=pl.CostEstimate(flops=HALF * 76 * 10**6, bytes_accessed=HALF * 3 * 65536,
                                      transcendentals=0),
        name="blur_half",
    )(psf_index, table, taps, patches, offsets, image, variance)


def halves_kernel(*refs):
    for n in range(4):
        rows = refs[4 + n].shape[0] - META
        start = META if n % 2 == 0 else META + rows
        refs[4 + n][0:META] = refs[n][0:META]
        refs[4 + n][META:] = refs[n][start:start + rows]


def halves(*arrays):
    vmem = pl.BlockSpec(memory_space=pltpu.VMEM)
    rows = META + HALF * PIX // 2
    return pl.pallas_call(
        halves_kernel,
        in_specs=[vmem] * 4,
        out_specs=[vmem] * 4,
        out_shape=[jax.ShapeDtypeStruct((rows, PIX), F32)] * 4,
        compiler_params=pltpu.CompilerParams(vmem_limit_bytes=ADD_LIMIT),
        name="halves",
    )(*arrays)


def place_kernel(runs, olds, both, last, here_ref, *refs):
    count = len(runs)
    tiles, old, refs = refs[:count], refs[count:count + olds], refs[count + olds:]
    outs, (canvas, buf, facts, meta_ref, sems) = refs[:10], refs[-5:]
    copies, starts, at = [], [], STRIP
    for n, source in enumerate(tiles):
        copies.append(pltpu.make_async_copy(source, buf.at[pl.ds(at, source.shape[0])], sems.at[n]))
        copies[-1].start()
        buf[at - STRIP:at] = jnp.zeros((STRIP, PIX), F32)
        starts.append(at + META)
        at += source.shape[0] + STRIP
    buf[at - STRIP:at] = jnp.zeros((STRIP, PIX), F32)
    if old:
        canvas[...] = old[0][...] + old[1][...] if len(old) > 1 else old[0][...]
    else:
        canvas[...] = jnp.zeros(canvas.shape, F32)
    my_x, core, my_y = here_ref[0], here_ref[1], here_ref[2]
    for n, copy in enumerate(copies):
        copy.wait()
        facts[n * META:(n + 1) * META] = buf[starts[n] - META:starts[n]].astype(jnp.int32)
    to_scalars = pltpu.make_async_copy(facts, meta_ref, sems.at[count])
    to_scalars.start()
    to_scalars.wait()
    row_of = lax.broadcasted_iota(jnp.int32, (8, PIX), 0)
    lane = lax.broadcasted_iota(jnp.int32, (8, PIX), 1)

    def add(items):
        moved = [pltpu.roll(buf[pl.ds(tile_row + skip, STRIP), :], (col + PIX) & (PIX - 1), 1)
                 for _, tile_row, skip, col in items]
        for (at, _, skip, col), strip in zip(items, moved):
            sides = [(lane >= col - n * PIX) & (lane < col - n * PIX + PIX) for n in range(2)]
            for g in range(0, STRIP, 8):
                line = row_of + (skip + g)
                inside = (line >= 0) & (line < PIX)
                for n in range(2):
                    canvas[at, n, g:g + 8] += jnp.where(inside & sides[n], strip[g:g + 8], 0.0)

    def bounded(skip):
        return jnp.clip(skip, -STRIP, PIX)

    def pair_of(index, entry):
        patch, row, col = (meta_ref[index * META, entry + n] for n in range(3))
        return patch, (patch >> 1) & (NZ - 1), patch >> 4, row, col

    def along_y(t, carry, index, entry, base):
        items = []
        for n in range(UNROLL):
            for k in range(2):
                patch, column, owner, row, col = pair_of(index, entry + 6 * (UNROLL * t + n) + 3 * k)
                at = ((owner - my_x) & (NX - 1)) * NZ + column
                skip = bounded(my_y * STRIP - row)
                other = (patch & 1) != core
                if both:
                    at = at + jnp.where(other, 2 * NX * NZ, 0)
                else:
                    skip = jnp.where(other, PIX, skip)
                items.append((at, base + (UNROLL * t + n) * PIX, skip, col))
        add(items)
        return carry

    def along_x(t, carry, index, entry, base):
        for k in range(2):
            patch, column, owner, row, col = pair_of(index, entry + 6 * t + 3 * k)
            other = (patch & 1) != core
            top = jnp.maximum(row, 0) // STRIP

            @pl.when((owner == my_x) if both else (owner == my_x) & jnp.logical_not(other))
            def _():
                items = []
                for n in range(3):
                    strip = top + n
                    skip = jnp.where(strip < NY, bounded(strip * STRIP - row), PIX)
                    at = (NX + ((strip - my_y) & (NY - 1))) * NZ + column
                    if both:
                        at = at + jnp.where(other, 2 * NX * NZ, 0)
                    items.append((at, base + t * PIX, skip, col))
                add(items)
        return carry

    for index, (group, tile, size) in enumerate(runs):
        given = dict(index=index, entry=6 * tile, base=starts[index])
        if group == 0:
            lax.fori_loop(0, size // UNROLL, functools.partial(along_y, **given), 0)
        else:
            lax.fori_loop(0, size, functools.partial(along_x, **given), 0)
    if last:
        half = NZ // 2
        for group in range(2):
            own, right, far, left = (group * NX * NZ + n * NZ for n in range(4))
            to_right, to_left, right_low, left_high, stay = outs[5 * group:5 * group + 5]
            to_right[:half] = canvas[far:far + half]
            to_right[half:] = canvas[right + half:right + NZ]
            to_left[:half] = canvas[far + half:far + NZ]
            to_left[half:] = canvas[left:left + half]
            right_low[...] = canvas[right:right + half]
            left_high[...] = canvas[left + half:left + NZ]
            stay[...] = canvas[own:own + NZ]
    elif both:
        refs[0][...] = canvas[:2 * NX * NZ]
        refs[1][...] = canvas[2 * NX * NZ:]
    else:
        refs[0][...] = canvas[...]


def place(here, arrays, old=(), both=False, last=False, cost=4):
    smem = pl.BlockSpec(memory_space=pltpu.SMEM)
    hbm = pl.BlockSpec(memory_space=pl.ANY)
    vmem = pl.BlockSpec(memory_space=pltpu.VMEM)
    size = 2 * NX * NZ
    shape = jax.ShapeDtypeStruct((size, 2, STRIP, PIX), F32)
    whole = jax.ShapeDtypeStruct((NZ, 2, STRIP, PIX), F32)
    half = jax.ShapeDtypeStruct((NZ // 2, 2, STRIP, PIX), F32)
    count = len(arrays)
    rows = sum(a.shape[0] + STRIP for _, _, a in arrays) + STRIP
    runs = tuple((group, tile, a.shape[0] // PIX) for group, tile, a in arrays)
    outs = [whole, whole, half, half, whole] * 2 if last else [shape] * (2 if both else 1)
    return pl.pallas_call(
        functools.partial(place_kernel, runs, len(old), both, last),
        in_specs=[smem] + [hbm] * count + [vmem] * len(old),
        out_specs=[vmem] * len(outs),
        out_shape=outs,
        scratch_shapes=[pltpu.VMEM((size * (2 if both else 1), 2, STRIP, PIX), F32),
                        pltpu.VMEM((rows, PIX), F32),
                        pltpu.VMEM((count * META, PIX), jnp.int32),
                        pltpu.SMEM((count * META, PIX), jnp.int32),
                        pltpu.SemaphoreType.DMA((count + 1,))],
        compiler_params=pltpu.CompilerParams(vmem_limit_bytes=PLACE_LIMIT),
        cost_estimate=pl.CostEstimate(flops=10**6, bytes_accessed=cost * 3690000, transcendentals=0),
        name="place",
    )(here, *(a for _, _, a in arrays), *old)


def add_kernel(*refs):
    number = len(refs) // 3
    for n in range(number):
        refs[2 * number + n][...] = refs[n][...] + refs[number + n][0:refs[n].shape[0]]


def add_received(mine, received):
    vmem = pl.BlockSpec(memory_space=pltpu.VMEM)
    return pl.pallas_call(
        add_kernel,
        in_specs=[vmem] * (2 * len(mine)),
        out_specs=[vmem] * len(mine),
        out_shape=[jax.ShapeDtypeStruct(a.shape, F32) for a in mine],
        compiler_params=pltpu.CompilerParams(vmem_limit_bytes=ADD_LIMIT),
        name="add_received",
    )(*mine, *received)


def join_kernel(stay_a, stay_b, *refs):
    out = refs[-1]
    half = NZ // 2
    low = stay_a[:half] + stay_b[:half]
    high = stay_a[half:] + stay_b[half:]
    for from_left, from_right, left_last, right_last in (refs[0:4], refs[4:8]):
        low = low + (from_right[half:] + left_last[...])
        high = high + (from_left[half:] + right_last[...])
    out[:half] = low
    out[half:] = high


def join(stay_a, stay_b, *received):
    vmem = pl.BlockSpec(memory_space=pltpu.VMEM)
    return pl.pallas_call(
        join_kernel,
        in_specs=[vmem] * 10,
        out_specs=vmem,
        out_shape=jax.ShapeDtypeStruct(stay_a.shape, F32),
        compiler_params=pltpu.CompilerParams(vmem_limit_bytes=ADD_LIMIT),
        name="join",
    )(stay_a, stay_b, *received)


def shift(value, axis, by):
    size = lax.axis_size(axis)
    return lax.ppermute(value, axis, [(i, (i + by) % size) for i in range(size)])


def pairs_of_patch(weights, patches, offsets):
    tile_dev = weights.shape[0]
    npatch = NX * NZ * NC
    pairs = tile_dev * 2
    targets = patches.reshape(pairs)
    matches = (targets[:, None] == jnp.arange(npatch, dtype=jnp.int32)[None, :]).astype(jnp.int32)
    earlier = jnp.sum((jnp.cumsum(matches, axis=0) - matches) * matches, axis=1)
    slot_of = targets * 2 + earlier
    chooser = (jnp.arange(npatch * 2, dtype=jnp.int32)[:, None] == slot_of[None, :]).astype(F32)
    payload = jnp.concatenate(
        [jnp.repeat(weights, 2)[:, None], offsets.reshape(pairs, 2).astype(F32)], axis=1)
    sent = jnp.dot(chooser, payload, precision=lax.Precision.HIGHEST).reshape(NX, NZ, NC, 1, 6)
    sent = jnp.broadcast_to(sent, (NX, NZ, NC, NY, 6)).reshape(-1, 6)
    return lax.all_to_all(sent, ("x", "z", "core", "y"), 0, 0, tiled=True)


def weight_sums(got, strip):
    every = got.reshape(-1, 3)
    rows = strip * STRIP + jnp.arange(STRIP, dtype=jnp.int32)
    cols = jnp.arange(PATCH_PIX, dtype=jnp.int32)
    row_at = rows[None, :] - every[:, 1:2].astype(jnp.int32)
    col_at = cols[None, :] - every[:, 2:3].astype(jnp.int32)
    row_hit = ((row_at >= 0) & (row_at < PIX)).astype(F32) * every[:, 0:1]
    col_hit = ((col_at >= 0) & (col_at < PIX)).astype(F32)
    return jnp.einsum("na,nb->ab", row_hit, col_hit, precision=lax.Precision.HIGHEST)


def body(image, variance, patches, offsets, psf_index, coeff_table, basis_taps):
    strip = lax.axis_index("y")
    here = jnp.stack([lax.axis_index("x"), lax.axis_index("core"), strip]).astype(jnp.int32)
    table = coeff_table.T
    patch_of, offset_of = patches.transpose(0, 2, 1), offsets.transpose(0, 2, 3, 1)
    own_y, wts_y = blur_half(0, psf_index, table, basis_taps, patch_of, offset_of, image, variance)
    own_x, wts_x = blur_half(1, psf_index, table, basis_taps, patch_of, offset_of, image, variance)

    left_y, right_y = shift(own_y, "y", 1), shift(own_y, "y", -1)
    left_x, right_x = shift(own_x, "x", 1), shift(own_x, "x", -1)
    weights = jnp.concatenate([wts_y[:, 0], wts_x[:, 0]])
    pairs = pairs_of_patch(weights, patches, offsets)
    left_y, right_y, left_x, right_x, pairs = lax.optimization_barrier((left_y, right_y, left_x, right_x, pairs))

    low_y, high_y, low_x, high_x = halves(left_y, right_y, left_x, right_x)
    far = [(0, 0, shift(low_y, "y", 1)), (0, HALF // 2, shift(high_y, "y", -1)),
           (1, 0, shift(low_x, "x", 1)), (1, HALF // 2, shift(high_x, "x", -1))]
    mine, theirs = place(here, [(0, 0, own_y), (0, 0, left_y), (0, 0, right_y),
                                (1, 0, own_x), (1, 0, left_x), (1, 0, right_x)], both=True, cost=12)
    far_arrays, mine, theirs = lax.optimization_barrier(([a for _, _, a in far], mine, theirs))

    received = shift(theirs, "core", 1)
    far = [(group, tile, a) for (group, tile, _), a in zip(far, far_arrays)]
    sib = [(group, tile, shift(a, "core", 1)) for group, tile, a in far]
    denominator = weight_sums(pairs, strip)
    mine, = place(here, far, (mine,))
    ready = place(here, sib, (mine, received), last=True)

    right_a, left_a, low_a, high_a, stay_a, right_b, left_b, low_b, high_b, stay_b = ready
    from_left_a, from_right_a = shift(right_a, "x", 1), shift(left_a, "x", -1)
    from_left_b, from_right_b = shift(right_b, "y", 1), shift(left_b, "y", -1)
    from_left_a, from_right_a, from_left_b, from_right_b = lax.optimization_barrier(
        (from_left_a, from_right_a, from_left_b, from_right_b))
    low_a, low_b, high_a, high_b = add_received(
        (low_a, low_b, high_a, high_b),
        (from_left_a, from_left_b, from_right_a, from_right_b))
    partial = join(stay_a, stay_b,
                   from_left_a, from_right_a, shift(low_a, "x", 1), shift(high_a, "x", -1),
                   from_left_b, from_right_b, shift(low_b, "y", 1), shift(high_b, "y", -1))
    partial = partial.reshape(NZ, 2 * STRIP, PIX)
    total = lax.all_to_all(partial, "z", 0, 0, tiled=True).sum(axis=0)
    numerator = jnp.concatenate([total[:STRIP], total[STRIP:]], axis=1)
    return (numerator / (denominator + 1.0))[None]


def solution(mesh):
    fine = Mesh(mesh.devices.reshape(NX, NZ, NC, NY), ("x", "z", "core", "y"))
    own = ("x", "z", "core")
    return jax.shard_map(
        body,
        mesh=fine,
        in_specs=(
            P("y", own, None, None),
            P("y", own, None, None),
            P("y", own, None),
            P("y", own, None, None),
            P("y", own),
            P(),
            P(),
        ),
        out_specs=P(own, "y", None),
        check_vma=False,
    )
```

time: 170 us -> 127 us (0.75)
  the two profiles are of different devices: /device:TPU:9 before, /device:TPU:24 now
where the time goes in v2:
time: 127 us
  waiting for transfers between devices  38.6 us (30%)
  Pallas kernels  28.8 us (23%)
  starting transfers between devices  27.9 us (22%)
  blocking collectives  24.2 us (19%)
  local copies, waits for them, and re-layouts  4.81 us (4%)
  matrix products  1.44 us (1%)
    ppermute x21, waiting for transfers between devices, shift(): lax.ppermute(value, axis, [(i, (i + by) % size) for i in range(size)])  24.5 us
    ppermute x21, starting transfers between devices, shift(): lax.ppermute(value, axis, [(i, (i + by) % size) for i in range(size)])  24.4 us
    all_to_all x1, blocking collectives, pairs_of_patch(): return lax.all_to_all(sent, ('x', 'z', 'core', 'y'), 0, 0, tiled=True)  24.2 us
    pallas_call x3, Pallas kernels, place(): pl.pallas_call(functools.partial(place_kernel, runs, len(old), both, last...  15.5 us
    all_to_all x1, waiting for transfers between devices, body(): total = lax.all_to_all(partial, 'z', 0, 0, tiled=True).sum(axis=0)  14.1 us
    pallas_call x2, Pallas kernels, blur_half(): pl.pallas_call(functools.partial(blur_kernel, half * HALF), grid=(HALF //...  11.1 us
    all_to_all x1, starting transfers between devices, body(): total = lax.all_to_all(partial, 'z', 0, 0, tiled=True).sum(axis=0)  3.49 us
  transfers between devices with their start and end apart: 22, of which 12 were waited for; matrix products, arithmetic and copies ran while one was open for 3% of the time, Pallas kernels for 13%

profile of v2, /device:TPU:24, one launch (start us, length us, event | category | flops | bytes accessed | tf_op | source)
XLA Modules:
  0.0 126.8 jit_solution(15926316391814645450)
XLA Ops:
  0.0 5.6 %blur_half.2 = (f32[1544,128]{1,0:T(8,128)}, f32[12,128]{1,0:T(8,128)}) custom-call(s32[1,24]{1,0:T(1,128)} %psf_ref.3, f32[3,16]{1,0:T(4,128)} %bitcast.21, f32[3,2,21]{2,1,0:T(2,128)} %taps_ref.3, s32[1,2,24]{2,1,0:T(2,128)} %bitcast.19, s32[1,2,2,24]{3,2,1,0:T(2,128)} %bitcast.17, f32[1,24,128,128]{3,2,1,0:T(8,128)} %img_ref.3, f32[1,24,128,128]{3,2,1,0:T(8,128)} %var_ref.3), custom_call_target="tpu_custom_call" | custom-call | flops 912000000 | bytes 2359296 | tf_op jit(solution)/shard_map/blur_half/pallas_call | solution.py:90
  5.6 2.0 %collective-permute-start = (f32[1544,128]{1,0:T(8,128)}, f32[1544,128]{1,0:T(8,128)S(1)}, u32[]{:S(2)}, u32[]{:S(2)}) collective-permute-start(f32[1544,128]{1,0:T(8,128)} %get-tuple-element.44.refs_0_), channel_id=1, source_target_pairs={{0,1},{1,2},{2,3},{3,0},{4,5},{5,6},{6,7},{7,4},{8,9},{9,10},{10,1... | collective-permute-start | bytes 2371592 | tf_op jit(solution)/shard_map/ppermute | solution.py:303
  7.6 5.5 %blur_half.3 = (f32[1544,128]{1,0:T(8,128)}, f32[12,128]{1,0:T(8,128)}) custom-call(s32[1,24]{1,0:T(1,128)} %psf_ref.3, f32[3,16]{1,0:T(4,128)} %bitcast.22, f32[3,2,21]{2,1,0:T(2,128)} %taps_ref.3, s32[1,2,24]{2,1,0:T(2,128)} %bitcast.20, s32[1,2,2,24]{3,2,1,0:T(2,128)} %bitcast.18, f32[1,24,128,128]{3,2,1,0:T(8,128)} %img_ref.3, f32[1,24,128,128]{3,2,1,0:T(8,128)} %var_ref.3), custom_call_target="tpu_custom_call" | custom-call | flops 912000000 | bytes 2359296 | tf_op jit(solution)/shard_map/blur_half/pallas_call | solution.py:90
  13.1 1.5 %collective-permute-start.2 = (f32[1544,128]{1,0:T(8,128)}, f32[1544,128]{1,0:T(8,128)S(1)}, u32[]{:S(2)}, u32[]{:S(2)}) collective-permute-start(f32[1544,128]{1,0:T(8,128)} %get-tuple-element.45.refs_3_), channel_id=1, source_target_pairs={{0,64},{64,128},{128,192},{192,0},{1,65},{65,129},{129,193},{193,1... | collective-permute-start | bytes 2371592 | tf_op jit(solution)/shard_map/ppermute | solution.py:303
  14.6 1.7 %collective-permute-start.3 = (f32[1544,128]{1,0:T(8,128)}, f32[1544,128]{1,0:T(8,128)S(1)}, u32[]{:S(2)}, u32[]{:S(2)}) collective-permute-start(f32[1544,128]{1,0:T(8,128)} %get-tuple-element.45.refs_3_), channel_id=1, source_target_pairs={{0,192},{64,0},{128,64},{192,128},{1,193},{65,1},{129,65},{193,129... | collective-permute-start | bytes 2371592 | tf_op jit(solution)/shard_map/ppermute | solution.py:303
  16.4 0.8 slice_reduce_fusion.1
  17.2 0.8 slice_reduce_fusion.2
  18.5 0.1 convert_element_type.20
  18.7 0.2 select_reduce_fusion
  18.9 0.2 fusion.21
  19.2 24.2 %all_to_all.17 = f32[256,1,6]{2,1,0:T(1,128)S(1)} all-to-all(f32[256,1,6]{2,1,0:T(1,128)S(1)} %bitcast.16), channel_id=1, replica_groups=mesh['x'=4,'z'=8,'core'=2,'y'=4] {'x','z','core','y'}, dimensions={0} | all-to-all | bytes 12288 | tf_op jit(solution)/shard_map/all_to_all | solution.py:319
  43.4 1.3 halves.1
  44.7 2.6 %collective-permute-start.4 = (f32[776,128]{1,0:T(8,128)}, f32[776,128]{1,0:T(8,128)}, u32[]{:S(2)}, u32[]{:S(2)}) collective-permute-start(f32[776,128]{1,0:T(8,128)} %get-tuple-element.52), channel_id=1, source_target_pairs={{0,1},{1,2},{2,3},{3,0},{4,5},{5,6},{6,7},{7,4},{8,9},{9,10},{10,1... | collective-permute-start | bytes 1191944 | tf_op jit(solution)/shard_map/ppermute | solution.py:303
  47.2 0.6 collective-permute-start.6
  47.8 2.7 %collective-permute-start.7 = (f32[776,128]{1,0:T(8,128)}, f32[776,128]{1,0:T(8,128)}, u32[]{:S(2)}, u32[]{:S(2)}) collective-permute-start(f32[776,128]{1,0:T(8,128)} %get-tuple-element.55), channel_id=1, source_target_pairs={{0,192},{64,0},{128,64},{192,128},{1,193},{65,1},{129,65},{193,129... | collective-permute-start | bytes 1191944 | tf_op jit(solution)/shard_map/ppermute | solution.py:303
  50.6 1.1 copy-done
  51.7 1.1 copy-done.1
  52.8 7.3 %place.3 = (f32[64,2,64,128]{3,2,1,0:T(8,128)S(1)}, f32[64,2,64,128]{3,2,1,0:T(8,128)S(1)}) custom-call(s32[3]{0:T(128)S(1)} %pad_add_fusion.here_ref, f32[1544,128]{1,0:T(8,128)S(1)} %copy-done, f32[1544,128]{1,0:T(8,128)S(1)} %collective-permute-done.refs_0_.refs_1_, f32[1544,128]{1,0:T(8,128)S(1)} %collective-permute-done.1.refs_1_.refs_2_, ...), custom_call_target="tpu_custom_call" | custom-call | flops 1000000 | bytes 44280000 | tf_op jit(solution)/shard_map/place/pallas_call | solution.py:243
  60.3 0.5 collective-permute-start.10
  60.8 0.1 collective-permute-start.11
  60.9 0.4 collective-permute-start.8
  61.3 0.1 collective-permute-start.9
  61.4 4.1 %place.4.refs_4_ = f32[64,2,64,128]{3,2,1,0:T(8,128)S(1)} custom-call(s32[3]{0:T(128)S(1)} %pad_add_fusion.here_ref, f32[776,128]{1,0:T(8,128)} %collective-permute-done.4.refs_0_, f32[776,128]{1,0:T(8,128)} %collective-permute-done.5.refs_1_, f32[776,128]{1,0:T(8,128)} %collective-permute-done.6.refs_2_, f32[776,128]{1,0:T(8,128)} %collective-permute-done.7.refs_3_, ...), custom_call_target="tpu_custom_call" | custom-call | flops 1000000 | bytes 14760000 | tf_op jit(solution)/shard_map/place/pallas_call | solution.py:243
  65.5 1.9 %collective-permute-done.10.refs_2_ = f32[776,128]{1,0:T(8,128)S(1)} collective-permute-done((f32[776,128]{1,0:T(8,128)}, f32[776,128]{1,0:T(8,128)S(1)}, u32[]{:S(2)}, u32[]{:S(2)}) %collective-permute-start.10) | collective-permute-done | bytes 397344 | tf_op jit(solution)/shard_map/ppermute | solution.py:303
  67.4 1.0 collective-permute-done.11.refs_3_
  68.4 0.6 collective-permute-done.8.refs_0_
  69.0 0.6 collective-permute-done.9.refs_1_
  69.5 0.2 collective-permute-done.12.refs_5_
  69.7 4.1 %place.5 = (f32[8,2,64,128]{3,2,1,0:T(8,128)S(1)}, f32[8,2,64,128]{3,2,1,0:T(8,128)S(1)}, f32[4,2,64,128]{3,2,1,0:T(8,128)S(1)}, f32[4,2,64,128]{3,2,1,0:T(8,128...) custom-call(s32[3]{0:T(128)S(1)} %pad_add_fusion.here_ref, ...), custom_call_target="tpu_custom_call" | custom-call | flops 1000000 | bytes 14760000 | tf_op jit(solution)/shard_map/place/pallas_call | solution.py:243
  73.8 3.2 %collective-permute-start.14 = (f32[8,2,64,128]{3,2,1,0:T(8,128)S(1)}, f32[8,2,64,128]{3,2,1,0:T(8,128)S(1)}, u32[]{:S(2)}, u32[]{:S(2)}) collective-permute-start(f32[8,2,64,128]{3,2,1,0:T(8,128)S(1)} %get-tuple-element.67), channel_id=1, source_target_pairs={{0,192},{64,0},{128,64},{192,128},{1,193},{65,1},{129,65},{193,129... | collective-permute-start | bytes 1572872 | tf_op jit(solution)/shard_map/ppermute | solution.py:303
  77.1 3.5 %collective-permute-start.15 = (f32[8,2,64,128]{3,2,1,0:T(8,128)S(1)}, f32[8,2,64,128]{3,2,1,0:T(8,128)S(1)}, u32[]{:S(2)}, u32[]{:S(2)}) collective-permute-start(f32[8,2,64,128]{3,2,1,0:T(8,128)S(1)} %get-tuple-element.68), channel_id=1, source_target_pairs={{0,1},{1,2},{2,3},{3,0},{4,5},{5,6},{6,7},{7,4},{8,9},{9,10},{10,1... | collective-permute-start | bytes 1572872 | tf_op jit(solution)/shard_map/ppermute | solution.py:303
  80.6 8.8 %collective-permute-done.13.refs_4_.refs_0_ = f32[8,2,64,128]{3,2,1,0:T(8,128)S(1)} collective-permute-done((f32[8,2,64,128]{3,2,1,0:T(8,128)S(1)}, f32[8,2,64,128]{3,2,1,0:T(8,128)S(1)}, u32[]{:S(2)}, u32[]{:S(2)}) %collective-permute-start.13) | collective-permute-done | bytes 524320 | tf_op jit(solution)/shard_map/ppermute | solution.py:303
  89.4 2.2 %collective-permute-done.15.refs_5_.refs_4_ = f32[8,2,64,128]{3,2,1,0:T(8,128)S(1)} collective-permute-done((f32[8,2,64,128]{3,2,1,0:T(8,128)S(1)}, f32[8,2,64,128]{3,2,1,0:T(8,128)S(1)}, u32[]{:S(2)}, u32[]{:S(2)}) %collective-permute-start.15) | collective-permute-done | bytes 524320 | tf_op jit(solution)/shard_map/ppermute | solution.py:303
  91.6 3.4 %collective-permute-done.16.refs_7_.refs_5_ = f32[8,2,64,128]{3,2,1,0:T(8,128)S(1)} collective-permute-done((f32[8,2,64,128]{3,2,1,0:T(8,128)S(1)}, f32[8,2,64,128]{3,2,1,0:T(8,128)S(1)}, u32[]{:S(2)}, u32[]{:S(2)}) %collective-permute-start.16) | collective-permute-done | bytes 524320 | tf_op jit(solution)/shard_map/ppermute | solution.py:303
  95.0 0.1 add_received.1
  95.2 3.2 %collective-permute-start.18 = (f32[4,2,64,128]{3,2,1,0:T(8,128)S(1)}, f32[4,2,64,128]{3,2,1,0:T(8,128)S(1)}, u32[]{:S(2)}, u32[]{:S(2)}) collective-permute-start(f32[4,2,64,128]{3,2,1,0:T(8,128)S(1)} %get-tuple-element.79), channel_id=1, source_target_pairs={{0,192},{64,0},{128,64},{192,128},{1,193},{65,1},{129,65},{193,129... | collective-permute-start | bytes 786440 | tf_op jit(solution)/shard_map/ppermute | solution.py:303
  98.4 0.3 collective-permute-start.19
  98.7 1.7 %collective-permute-start.20 = (f32[4,2,64,128]{3,2,1,0:T(8,128)S(1)}, f32[4,2,64,128]{3,2,1,0:T(8,128)S(1)}, u32[]{:S(2)}, u32[]{:S(2)}) collective-permute-start(f32[4,2,64,128]{3,2,1,0:T(8,128)S(1)} %get-tuple-element.81), channel_id=1, source_target_pairs={{0,3},{1,0},{2,1},{3,2},{4,7},{5,4},{6,5},{7,6},{8,11},{9,8},{10,9... | collective-permute-start | bytes 786440 | tf_op jit(solution)/shard_map/ppermute | solution.py:303
  100.5 2.6 %collective-permute-done.17.refs_2_ = f32[4,2,64,128]{3,2,1,0:T(8,128)S(1)} collective-permute-done((f32[4,2,64,128]{3,2,1,0:T(8,128)S(1)}, f32[4,2,64,128]{3,2,1,0:T(8,128)S(1)}, u32[]{:S(2)}, u32[]{:S(2)}) %collective-permute-start.17) | collective-permute-done | bytes 262176 | tf_op jit(solution)/shard_map/ppermute | solution.py:303
  103.1 1.7 %collective-permute-done.19.refs_6_ = f32[4,2,64,128]{3,2,1,0:T(8,128)S(1)} collective-permute-done((f32[4,2,64,128]{3,2,1,0:T(8,128)S(1)}, f32[4,2,64,128]{3,2,1,0:T(8,128)S(1)}, u32[]{:S(2)}, u32[]{:S(2)}) %collective-permute-start.19) | collective-permute-done | bytes 262176 | tf_op jit(solution)/shard_map/ppermute | solution.py:303
  104.8 1.5 %collective-permute-done.20.refs_7_ = f32[4,2,64,128]{3,2,1,0:T(8,128)S(1)} collective-permute-done((f32[4,2,64,128]{3,2,1,0:T(8,128)S(1)}, f32[4,2,64,128]{3,2,1,0:T(8,128)S(1)}, u32[]{:S(2)}, u32[]{:S(2)}) %collective-permute-start.20) | collective-permute-done | bytes 262176 | tf_op jit(solution)/shard_map/ppermute | solution.py:303
  106.3 0.9 join.1
  107.2 3.5 %all-to-all-start.1 = ((f32[8,128,128]{2,1,0:T(8,128)}), f32[8,128,128]{2,1,0:T(8,128)S(1)}, u32[]{:S(2)}, u32[]{:S(2)}) async-start(f32[8,128,128]{2,1,0:T(8,128)} %bitcast.8), calls=%async_computation.1 | async-start | bytes 1048576 | tf_op jit(solution)/shard_map/all_to_all | solution.py:373
  110.8 0.1 reshape.32
  110.9 0.1 slice_reduce_fusion
  111.0 0.4 fusion.8
  111.4 14.1 %all-to-all-done.1 = f32[8,128,128]{2,1,0:T(8,128)S(1)} async-done(((f32[8,128,128]{2,1,0:T(8,128)}), f32[8,128,128]{2,1,0:T(8,128)S(1)}, u32[]{:S(2)}, u32[]{:S(2)}) %all-to-all-start.1) | async-done | bytes 524320 | tf_op jit(solution)/shard_map/all_to_all | solution.py:373
  125.5 1.3 fusion.1
  (38 shorter events, 1.3 us)
Async XLA Ops:
  0.0 16.3 %copy-start.3 = (s32[1,24,2]{1,2,0:T(2,128)S(1)}, s32[1,24,2]{1,2,0:T(2,128)}, u32[]{:S(2)}) copy-start(s32[1,24,2]{1,2,0:T(2,128)} %param.9) | copy-start | bytes 580
  0.0 16.4 %copy-start.2 = (s32[1,24,2,2]{1,3,2,0:T(2,128)S(1)}, s32[1,24,2,2]{1,3,2,0:T(2,128)}, u32[]{:S(2)}) copy-start(s32[1,24,2,2]{1,3,2,0:T(2,128)} %param.10) | copy-start | bytes 1156
  5.6 37.9 %collective-permute-start = (f32[1544,128]{1,0:T(8,128)}, f32[1544,128]{1,0:T(8,128)S(1)}, u32[]{:S(2)}, u32[]{:S(2)}) collective-permute-start(f32[1544,128]{1,0:T(8,128)} %get-tuple-element.44.refs_0_), channel_id=1, source_target_pairs={{0,1},{1,2},{2,3},{3,0},{4,5},{5,6},{6,7},{7,4},{8,9},{9,10},{10,1... | collective-permute-start | bytes 2371592 | tf_op jit(solution)/shard_map/ppermute | solution.py:303
  7.5 35.9 %collective-permute-start.1 = (f32[1544,128]{1,0:T(8,128)}, f32[1544,128]{1,0:T(8,128)S(1)}, u32[]{:S(2)}, u32[]{:S(2)}) collective-permute-start(f32[1544,128]{1,0:T(8,128)} %get-tuple-element.44.refs_0_), channel_id=1, source_target_pairs={{0,3},{1,0},{2,1},{3,2},{4,7},{5,4},{6,5},{7,6},{8,11},{9,8},{10,9... | collective-permute-start | bytes 2371592 | tf_op jit(solution)/shard_map/ppermute | solution.py:303
  13.1 30.3 %collective-permute-start.2 = (f32[1544,128]{1,0:T(8,128)}, f32[1544,128]{1,0:T(8,128)S(1)}, u32[]{:S(2)}, u32[]{:S(2)}) collective-permute-start(f32[1544,128]{1,0:T(8,128)} %get-tuple-element.45.refs_3_), channel_id=1, source_target_pairs={{0,64},{64,128},{128,192},{192,0},{1,65},{65,129},{129,193},{193,1... | collective-permute-start | bytes 2371592 | tf_op jit(solution)/shard_map/ppermute | solution.py:303
  14.6 28.8 %collective-permute-start.3 = (f32[1544,128]{1,0:T(8,128)}, f32[1544,128]{1,0:T(8,128)S(1)}, u32[]{:S(2)}, u32[]{:S(2)}) collective-permute-start(f32[1544,128]{1,0:T(8,128)} %get-tuple-element.45.refs_3_), channel_id=1, source_target_pairs={{0,192},{64,0},{128,64},{192,128},{1,193},{65,1},{129,65},{193,129... | collective-permute-start | bytes 2371592 | tf_op jit(solution)/shard_map/ppermute | solution.py:303
  44.7 15.4 %collective-permute-start.4 = (f32[776,128]{1,0:T(8,128)}, f32[776,128]{1,0:T(8,128)}, u32[]{:S(2)}, u32[]{:S(2)}) collective-permute-start(f32[776,128]{1,0:T(8,128)} %get-tuple-element.52), channel_id=1, source_target_pairs={{0,1},{1,2},{2,3},{3,0},{4,5},{5,6},{6,7},{7,4},{8,9},{9,10},{10,1... | collective-permute-start | bytes 1191944 | tf_op jit(solution)/shard_map/ppermute | solution.py:303
  47.2 12.9 %collective-permute-start.5 = (f32[776,128]{1,0:T(8,128)}, f32[776,128]{1,0:T(8,128)}, u32[]{:S(2)}, u32[]{:S(2)}) collective-permute-start(f32[776,128]{1,0:T(8,128)} %get-tuple-element.53), channel_id=1, source_target_pairs={{0,3},{1,0},{2,1},{3,2},{4,7},{5,4},{6,5},{7,6},{8,11},{9,8},{10,9... | collective-permute-start | bytes 1191944 | tf_op jit(solution)/shard_map/ppermute | solution.py:303
  47.2 12.9 %collective-permute-start.6 = (f32[776,128]{1,0:T(8,128)}, f32[776,128]{1,0:T(8,128)}, u32[]{:S(2)}, u32[]{:S(2)}) collective-permute-start(f32[776,128]{1,0:T(8,128)} %get-tuple-element.54), channel_id=1, source_target_pairs={{0,64},{64,128},{128,192},{192,0},{1,65},{65,129},{129,193},{193,1... | collective-permute-start | bytes 1191944 | tf_op jit(solution)/shard_map/ppermute | solution.py:303
  47.8 12.3 %collective-permute-start.7 = (f32[776,128]{1,0:T(8,128)}, f32[776,128]{1,0:T(8,128)}, u32[]{:S(2)}, u32[]{:S(2)}) collective-permute-start(f32[776,128]{1,0:T(8,128)} %get-tuple-element.55), channel_id=1, source_target_pairs={{0,192},{64,0},{128,64},{192,128},{1,193},{65,1},{129,65},{193,129... | collective-permute-start | bytes 1191944 | tf_op jit(solution)/shard_map/ppermute | solution.py:303
  50.6 1.1 copy-start
  51.7 1.1 copy-start.1
  60.2 9.5 %collective-permute-start.12 = (f32[64,2,64,128]{3,2,1,0:T(8,128)S(1)}, f32[64,2,64,128]{3,2,1,0:T(8,128)S(1)}, u32[]{:S(2)}, u32[]{:S(2)}) collective-permute-start(f32[64,2,64,128]{3,2,1,0:T(8,128)S(1)} %get-tuple-element.63), channel_id=1, source_target_pairs={{0,4},{4,0},{1,5},{5,1},{2,6},{6,2},{3,7},{7,3},{8,12},{12,8},{9,1... | collective-permute-start | bytes 12582920 | tf_op jit(solution)/shard_map/ppermute | solution.py:303
  60.3 7.2 %collective-permute-start.10 = (f32[776,128]{1,0:T(8,128)}, f32[776,128]{1,0:T(8,128)S(1)}, u32[]{:S(2)}, u32[]{:S(2)}) collective-permute-start(f32[776,128]{1,0:T(8,128)} %collective-permute-done.6.refs_2_), channel_id=1, source_target_pairs={{0,4},{4,0},{1,5},{5,1},{2,6},{6,2},{3,7},{7,3},{8,12},{12,8},{9,1... | collective-permute-start | bytes 1191944 | tf_op jit(solution)/shard_map/ppermute | solution.py:303
  60.8 7.6 %collective-permute-start.11 = (f32[776,128]{1,0:T(8,128)}, f32[776,128]{1,0:T(8,128)S(1)}, u32[]{:S(2)}, u32[]{:S(2)}) collective-permute-start(f32[776,128]{1,0:T(8,128)} %collective-permute-done.7.refs_3_), channel_id=1, source_target_pairs={{0,4},{4,0},{1,5},{5,1},{2,6},{6,2},{3,7},{7,3},{8,12},{12,8},{9,1... | collective-permute-start | bytes 1191944 | tf_op jit(solution)/shard_map/ppermute | solution.py:303
  60.9 8.1 %collective-permute-start.8 = (f32[776,128]{1,0:T(8,128)}, f32[776,128]{1,0:T(8,128)S(1)}, u32[]{:S(2)}, u32[]{:S(2)}) collective-permute-start(f32[776,128]{1,0:T(8,128)} %collective-permute-done.4.refs_0_), channel_id=1, source_target_pairs={{0,4},{4,0},{1,5},{5,1},{2,6},{6,2},{3,7},{7,3},{8,12},{12,8},{9,1... | collective-permute-start | bytes 1191944 | tf_op jit(solution)/shard_map/ppermute | solution.py:303
  61.3 8.3 %collective-permute-start.9 = (f32[776,128]{1,0:T(8,128)}, f32[776,128]{1,0:T(8,128)S(1)}, u32[]{:S(2)}, u32[]{:S(2)}) collective-permute-start(f32[776,128]{1,0:T(8,128)} %collective-permute-done.5.refs_1_), channel_id=1, source_target_pairs={{0,4},{4,0},{1,5},{5,1},{2,6},{6,2},{3,7},{7,3},{8,12},{12,8},{9,1... | collective-permute-start | bytes 1191944 | tf_op jit(solution)/shard_map/ppermute | solution.py:303
  73.8 15.6 %collective-permute-start.13 = (f32[8,2,64,128]{3,2,1,0:T(8,128)S(1)}, f32[8,2,64,128]{3,2,1,0:T(8,128)S(1)}, u32[]{:S(2)}, u32[]{:S(2)}) collective-permute-start(f32[8,2,64,128]{3,2,1,0:T(8,128)S(1)} %get-tuple-element.66), channel_id=1, source_target_pairs={{0,64},{64,128},{128,192},{192,0},{1,65},{65,129},{129,193},{193,1... | collective-permute-start | bytes 1572872 | tf_op jit(solution)/shard_map/ppermute | solution.py:303
  73.8 15.5 %collective-permute-start.14 = (f32[8,2,64,128]{3,2,1,0:T(8,128)S(1)}, f32[8,2,64,128]{3,2,1,0:T(8,128)S(1)}, u32[]{:S(2)}, u32[]{:S(2)}) collective-permute-start(f32[8,2,64,128]{3,2,1,0:T(8,128)S(1)} %get-tuple-element.67), channel_id=1, source_target_pairs={{0,192},{64,0},{128,64},{192,128},{1,193},{65,1},{129,65},{193,129... | collective-permute-start | bytes 1572872 | tf_op jit(solution)/shard_map/ppermute | solution.py:303
  77.1 14.5 %collective-permute-start.15 = (f32[8,2,64,128]{3,2,1,0:T(8,128)S(1)}, f32[8,2,64,128]{3,2,1,0:T(8,128)S(1)}, u32[]{:S(2)}, u32[]{:S(2)}) collective-permute-start(f32[8,2,64,128]{3,2,1,0:T(8,128)S(1)} %get-tuple-element.68), channel_id=1, source_target_pairs={{0,1},{1,2},{2,3},{3,0},{4,5},{5,6},{6,7},{7,4},{8,9},{9,10},{10,1... | collective-permute-start | bytes 1572872 | tf_op jit(solution)/shard_map/ppermute | solution.py:303
  80.6 14.4 %collective-permute-start.16 = (f32[8,2,64,128]{3,2,1,0:T(8,128)S(1)}, f32[8,2,64,128]{3,2,1,0:T(8,128)S(1)}, u32[]{:S(2)}, u32[]{:S(2)}) collective-permute-start(f32[8,2,64,128]{3,2,1,0:T(8,128)S(1)} %get-tuple-element.69), channel_id=1, source_target_pairs={{0,3},{1,0},{2,1},{3,2},{4,7},{5,4},{6,5},{7,6},{8,11},{9,8},{10,9... | collective-permute-start | bytes 1572872 | tf_op jit(solution)/shard_map/ppermute | solution.py:303
  95.1 8.0 %collective-permute-start.17 = (f32[4,2,64,128]{3,2,1,0:T(8,128)S(1)}, f32[4,2,64,128]{3,2,1,0:T(8,128)S(1)}, u32[]{:S(2)}, u32[]{:S(2)}) collective-permute-start(f32[4,2,64,128]{3,2,1,0:T(8,128)S(1)} %get-tuple-element.78), channel_id=1, source_target_pairs={{0,64},{64,128},{128,192},{192,0},{1,65},{65,129},{129,193},{193,1... | collective-permute-start | bytes 786440 | tf_op jit(solution)/shard_map/ppermute | solution.py:303
  95.2 7.9 %collective-permute-start.18 = (f32[4,2,64,128]{3,2,1,0:T(8,128)S(1)}, f32[4,2,64,128]{3,2,1,0:T(8,128)S(1)}, u32[]{:S(2)}, u32[]{:S(2)}) collective-permute-start(f32[4,2,64,128]{3,2,1,0:T(8,128)S(1)} %get-tuple-element.79), channel_id=1, source_target_pairs={{0,192},{64,0},{128,64},{192,128},{1,193},{65,1},{129,65},{193,129... | collective-permute-start | bytes 786440 | tf_op jit(solution)/shard_map/ppermute | solution.py:303
  98.4 6.4 %collective-permute-start.19 = (f32[4,2,64,128]{3,2,1,0:T(8,128)S(1)}, f32[4,2,64,128]{3,2,1,0:T(8,128)S(1)}, u32[]{:S(2)}, u32[]{:S(2)}) collective-permute-start(f32[4,2,64,128]{3,2,1,0:T(8,128)S(1)} %get-tuple-element.80), channel_id=1, source_target_pairs={{0,1},{1,2},{2,3},{3,0},{4,5},{5,6},{6,7},{7,4},{8,9},{9,10},{10,1... | collective-permute-start | bytes 786440 | tf_op jit(solution)/shard_map/ppermute | solution.py:303
  98.7 7.6 %collective-permute-start.20 = (f32[4,2,64,128]{3,2,1,0:T(8,128)S(1)}, f32[4,2,64,128]{3,2,1,0:T(8,128)S(1)}, u32[]{:S(2)}, u32[]{:S(2)}) collective-permute-start(f32[4,2,64,128]{3,2,1,0:T(8,128)S(1)} %get-tuple-element.81), channel_id=1, source_target_pairs={{0,3},{1,0},{2,1},{3,2},{4,7},{5,4},{6,5},{7,6},{8,11},{9,8},{10,9... | collective-permute-start | bytes 786440 | tf_op jit(solution)/shard_map/ppermute | solution.py:303
  107.2 18.2 %all-to-all-start.1 = ((f32[8,128,128]{2,1,0:T(8,128)}), f32[8,128,128]{2,1,0:T(8,128)S(1)}, u32[]{:S(2)}, u32[]{:S(2)}) async-start(f32[8,128,128]{2,1,0:T(8,128)} %bitcast.8), calls=%async_computation.1 | async-start | bytes 1048576 | tf_op jit(solution)/shard_map/all_to_all | solution.py:373

commit v3 on v1

v3 whole, which is shorter than its diff:
```python
import functools

import jax
import jax.numpy as jnp
from jax import lax
from jax.experimental import pallas as pl
from jax.experimental.pallas import tpu as pltpu
from jax.sharding import Mesh
from jax.sharding import PartitionSpec as P

PIX = 128
PATCH_PIX = 256
TAPS = 21
MARGIN = TAPS // 2
NB = 3
NX, NZ, NC, NY = 4, 8, 2, 4
RING = 4
STRIP = PATCH_PIX // NY
TILES = 24
HALF = 12
UNROLL = 3
META = 8
PATCH, ROW, COL, RANK, WEIGHT = range(5)
GROUP_ROWS = META + HALF * PIX
ENTRIES = NZ * NC
ENTRY_ROWS = 2 * STRIP
SLOTS = 32
F32 = jnp.float32
BF16 = jnp.bfloat16
BLUR_LIMIT = 56 * 1024 * 1024
PLACE_LIMIT = 24 * 1024 * 1024
ADD_LIMIT = 12 * 1024 * 1024


def split(value):
    high = value.astype(BF16)
    return high, (value - high.astype(F32)).astype(BF16)


def dot(a, b):
    return jnp.dot(a, b, preferred_element_type=F32)


def blur_kernel(first, psf_ref, table_ref, taps_ref, patch_ref, offset_ref, img_ref, var_ref, out_ref,
                col_hi, col_lo, rows):
    major = lax.broadcasted_iota(jnp.int32, (PIX, PIX), 0)
    minor = lax.broadcasted_iota(jnp.int32, (PIX, PIX), 1)
    for b in range(NB):
        lanes = slice(b * PIX, (b + 1) * PIX)
        for axis, diff in ((0, minor - major), (1, major - minor)):
            band = jnp.zeros((PIX, PIX), F32)
            for t in range(TAPS):
                band = jnp.where(diff == t - MARGIN, taps_ref[b, axis, t], band)
            hi, lo = split(band)
            if axis:
                col_hi[:PIX, lanes], col_hi[PIX:, lanes], col_lo[:, lanes] = hi, hi, lo
            else:
                rows[:PIX, lanes], rows[PIX:, lanes] = hi, lo

    x_hi, x_lo = split(img_ref[0].reshape(HALF * PIX, PIX))
    smooth = dot(jnp.concatenate([x_hi, x_lo], axis=1), col_hi[...]) + dot(x_hi, col_lo[...])
    weights = []
    for n in range(HALF):
        total = jnp.sum(jnp.sum(var_ref[0, n], axis=0, keepdims=True), axis=1, keepdims=True)
        weights.append(1.0 / (total * (1.0 / (PIX * PIX))))
    for pair in range(HALF // 2):
        sides = []
        for n in (2 * pair, 2 * pair + 1):
            row = psf_ref[0, first + n]
            sides.append(jnp.concatenate(
                [smooth[n * PIX:(n + 1) * PIX, b * PIX:(b + 1) * PIX] * (table_ref[b, row] * weights[n])
                 for b in range(NB)], axis=0))
        q_hi, q_lo = split(jnp.concatenate(sides, axis=1))
        both = dot(rows[...], q_hi)
        done = both[:PIX] + (both[PIX:] + dot(rows[:PIX], q_lo))
        for n in range(2):
            at = META + (2 * pair + n) * PIX
            out_ref[at:at + PIX, :] = done[:, n * PIX:(n + 1) * PIX]

    lane = lax.broadcasted_iota(jnp.int32, (META, PIX), 1)
    kind = lax.broadcasted_iota(jnp.int32, (META, PIX), 0)
    patch, facts = jnp.zeros((META, PIX), jnp.int32), jnp.zeros((META, PIX), jnp.int32)
    for t in range(TILES):
        for k in range(2):
            here = lane == 2 * t + k
            patch = jnp.where(here, patch_ref[0, k, t], patch)
            place = jnp.where(kind == ROW, offset_ref[0, k, 0, t], offset_ref[0, k, 1, t])
            facts = jnp.where(here, place, facts)
    rank = jnp.zeros((META, PIX), jnp.int32)
    for t in range(TILES):
        for k in range(2):
            rank += jnp.where((patch == patch_ref[0, k, t]) & (lane > 2 * t + k), 1, 0)
    facts = jnp.where(kind == PATCH, patch, jnp.where(kind == RANK, rank, facts)).astype(F32)
    for n in range(HALF):
        facts = jnp.where((kind == WEIGHT) & ((lane >> 1) == first + n), weights[n], facts)
    out_ref[0:META, :] = facts


def blur_half(half, psf_index, table, taps, patches, offsets, image, variance):
    smem = pl.BlockSpec(memory_space=pltpu.SMEM)
    tiles = pl.BlockSpec((1, HALF, PIX, PIX), lambda i: (0, half, 0, 0))
    return pl.pallas_call(
        functools.partial(blur_kernel, half * HALF),
        grid=(1,),
        in_specs=[smem] * 5 + [tiles, tiles],
        out_specs=pl.BlockSpec((GROUP_ROWS, PIX), lambda i: (0, 0)),
        out_shape=pltpu.VMEM((GROUP_ROWS, PIX), F32),
        scratch_shapes=[pltpu.VMEM((2 * PIX, NB * PIX), BF16), pltpu.VMEM((PIX, NB * PIX), BF16),
                        pltpu.VMEM((2 * PIX, NB * PIX), BF16)],
        compiler_params=pltpu.CompilerParams(vmem_limit_bytes=BLUR_LIMIT),
        cost_estimate=pl.CostEstimate(flops=HALF * 76 * 10**6, bytes_accessed=HALF * 3 * 65536,
                                      transcendentals=0),
        name="blur_half",
    )(psf_index, table, taps, patches, offsets, image, variance)


def place_kernel(runs, last, here_ref, *refs):
    count = len(runs)
    tiles, refs = refs[:count], refs[count:]
    if last:
        old_canvas, old_notes, *outs, canvas, notes = refs[:-5]
    else:
        canvas, notes = refs[:-5]
    buf, whole_facts, whole_ref, weight_ref, sems = refs[-5:]
    copies, starts, at = [], [], STRIP
    for n, source in enumerate(tiles):
        copies.append(pltpu.make_async_copy(source, buf.at[pl.ds(at, GROUP_ROWS)], sems.at[n]))
        copies[n].start()
        buf[at - STRIP:at] = jnp.zeros((STRIP, PIX), F32)
        starts.append(at + META)
        at += GROUP_ROWS + STRIP
    buf[at - STRIP:at] = jnp.zeros((STRIP, PIX), F32)
    if last:
        canvas[...] = old_canvas[...]
        notes[...] = old_notes[...]
    else:
        canvas[...] = jnp.zeros(canvas.shape, F32)
        notes[...] = jnp.zeros(notes.shape, F32)
    my_x, core, my_y = here_ref[0], here_ref[1], here_ref[2]
    to_scalars = []
    for n, copy in enumerate(copies):
        copy.wait()
        rows = pl.ds(n * META, META)
        head = pl.ds(starts[n] - META, META)
        whole_facts[n * META:(n + 1) * META] = buf[starts[n] - META:starts[n]].astype(jnp.int32)
        to_scalars.append(pltpu.make_async_copy(whole_facts.at[rows], whole_ref.at[rows], sems.at[count + n]))
        to_scalars.append(pltpu.make_async_copy(buf.at[head], weight_ref.at[rows], sems.at[2 * count + n]))
        for scalars in to_scalars[-2:]:
            scalars.start()
    for scalars in to_scalars:
        scalars.wait()
    row_of = lax.broadcasted_iota(jnp.int32, (8, PIX), 0)
    lane = lax.broadcasted_iota(jnp.int32, (8, PIX), 1)
    lane_one = lax.broadcasted_iota(jnp.int32, (1, PIX), 1)

    def add(items):
        moved = [pltpu.roll(buf[pl.ds(tile_row + skip, STRIP), :], (col + PIX) & (PIX - 1), 1)
                 for _, tile_row, skip, col in items]
        for (at, _, skip, col), strip in zip(items, moved):
            sides = [(lane >= col - n * PIX) & (lane < col - n * PIX + PIX) for n in range(2)]
            for g in range(0, STRIP, 8):
                line = row_of + (skip + g)
                inside = (line >= 0) & (line < PIX)
                for n in range(2):
                    canvas[at, n, g:g + 8] += jnp.where(inside & sides[n], strip[g:g + 8], 0.0)

    def bounded(skip):
        return jnp.clip(skip, -STRIP, PIX)

    def pair_of(index, pair, reduce_at, source_at):
        patch, row, col, rank = (whole_ref[index * META + kind, pair] for kind in (PATCH, ROW, COL, RANK))
        weight = weight_ref[index * META + WEIGHT, pair]
        slot = reduce_at * (2 * RING) + source_at * 2 + rank
        note = jnp.where(lane_one == slot, weight, 0.0)
        note = jnp.where(lane_one == slot + SLOTS, row, note.astype(jnp.int32) * 0).astype(F32) + note
        note = jnp.where(lane_one == slot + 2 * SLOTS, col, 0).astype(F32) + note
        return patch, row, col, note

    def along_y(t, carry, index, pair, base, steps):
        items = []
        for n in range(UNROLL):
            for k in range(2):
                patch, row, col, note = pair_of(index, pair + 2 * (UNROLL * t + n) + k, my_x,
                                                (my_y + steps) & (RING - 1))
                at = (((patch >> 4) - my_x) & (RING - 1)) * ENTRIES + (patch & (ENTRIES - 1))
                notes[pl.ds(at, 1), :] += note
                items.append((at, base + (UNROLL * t + n) * PIX, bounded(my_y * STRIP - row), col))
        add(items)
        return carry

    def along_x(t, carry, index, pair, base, steps):
        for k in range(2):
            @pl.when((whole_ref[index * META + PATCH, pair + 2 * t + k] >> 4) == my_x)
            def _():
                patch, row, col, note = pair_of(index, pair + 2 * t + k, my_y, (my_x + steps) & (RING - 1))
                for n in range(NY):
                    notes[pl.ds(n * ENTRIES + (patch & (ENTRIES - 1)), 1), :] += note
                items = []
                for n in range(3):
                    strip = (jnp.maximum(row, 0) >> 6) + n
                    skip = jnp.where(strip < NY, bounded(strip * STRIP - row), PIX)
                    at = ((strip - my_y) & (RING - 1)) * ENTRIES + (patch & (ENTRIES - 1))
                    items.append((at, base + t * PIX, skip, col))
                add(items)
        return carry

    def each_run(step, number):
        for index, (half, steps) in enumerate(runs):
            given = dict(index=index, pair=2 * HALF * half, base=starts[index], steps=steps)
            lax.fori_loop(0, number, functools.partial(step, **given), 0)

    @pl.when(core == 0)
    def _():
        each_run(along_y, HALF // UNROLL)

    @pl.when(core == 1)
    def _():
        each_run(along_x, HALF)

    if last:
        for n, out in enumerate(outs):
            size = ENTRIES // 2
            out[:size * ENTRY_ROWS] = canvas[n * size:(n + 1) * size].reshape(size * ENTRY_ROWS, PIX)
            out[size * ENTRY_ROWS:] = notes[n * size:(n + 1) * size]


def place(here, arrays, runs, old=(), cost=6):
    smem = pl.BlockSpec(memory_space=pltpu.SMEM)
    hbm = pl.BlockSpec(memory_space=pl.ANY)
    vmem = pl.BlockSpec(memory_space=pltpu.VMEM)
    canvas, notes = (RING * ENTRIES, 2, STRIP, PIX), (RING * ENTRIES, PIX)
    part = (ENTRIES // 2 * ENTRY_ROWS + ENTRIES // 2, PIX)
    count = len(arrays)
    outs = [part] * (2 * RING) if old else [canvas, notes]
    return pl.pallas_call(
        functools.partial(place_kernel, tuple(runs), bool(old)),
        in_specs=[smem] + [hbm] * count + [vmem] * len(old),
        out_specs=[vmem] * len(outs),
        out_shape=[pltpu.VMEM(shape, F32) for shape in outs],
        scratch_shapes=([pltpu.VMEM(canvas, F32), pltpu.VMEM(notes, F32)] if old else [])
        + [pltpu.VMEM((count * (GROUP_ROWS + STRIP) + STRIP, PIX), F32),
           pltpu.VMEM((count * META, PIX), jnp.int32),
           pltpu.SMEM((count * META, PIX), jnp.int32),
           pltpu.SMEM((count * META, PIX), F32),
           pltpu.SemaphoreType.DMA((3 * count,))],
        compiler_params=pltpu.CompilerParams(vmem_limit_bytes=PLACE_LIMIT),
        cost_estimate=pl.CostEstimate(flops=10**6, bytes_accessed=cost * 3690000, transcendentals=0),
        name="place",
    )(here, *arrays, *old)


def add_kernel(a, b, c, d, first, second):
    first[...] = a[...] + b[...]
    second[...] = c[...] + d[...]


def add_received(*arrays):
    vmem = pl.BlockSpec(memory_space=pltpu.VMEM)
    return pl.pallas_call(
        add_kernel,
        in_specs=[vmem] * 4,
        out_specs=[vmem] * 2,
        out_shape=[pltpu.VMEM(arrays[0].shape, F32)] * 2,
        compiler_params=pltpu.CompilerParams(vmem_limit_bytes=ADD_LIMIT),
        name="add_received",
    )(*arrays)


def join_kernel(here_ref, low_a, low_b, low_c, high_a, high_b, high_c, mine, theirs, total):
    core = here_ref[1]
    size = ENTRIES // 2
    for n, (a, b, c) in enumerate(((low_a, low_b, low_c), (high_a, high_b, high_c))):
        start = n * size * (ENTRY_ROWS + 1)
        total[start:start + size * (ENTRY_ROWS + 1)] = a[...] + b[...] + c[...]
    kind = lax.broadcasted_iota(jnp.int32, (8, PIX), 0)
    for out, parity in ((mine, core), (theirs, 1 - core)):
        for column in range(NZ):
            half, entry = column // (NZ // 2), NC * (column % (NZ // 2)) + parity
            start = half * size * (ENTRY_ROWS + 1)
            out[column, :ENTRY_ROWS] = total[pl.ds(pl.multiple_of(start + entry * ENTRY_ROWS, 8), ENTRY_ROWS), :]
            note = total[pl.ds(start + size * ENTRY_ROWS + entry, 1), :]
            out[column, ENTRY_ROWS:] = jnp.where(kind == core, note, 0.0)


def join(here, *arrays):
    vmem = pl.BlockSpec(memory_space=pltpu.VMEM)
    return pl.pallas_call(
        join_kernel,
        in_specs=[pl.BlockSpec(memory_space=pltpu.SMEM)] + [vmem] * 6,
        out_specs=[vmem] * 2,
        out_shape=[pltpu.VMEM((NZ, ENTRY_ROWS + 8, PIX), F32)] * 2,
        scratch_shapes=[pltpu.VMEM((ENTRIES * (ENTRY_ROWS + 1), PIX), F32)],
        compiler_params=pltpu.CompilerParams(vmem_limit_bytes=ADD_LIMIT),
        name="join",
    )(here, *arrays)


def finish_kernel(here_ref, got, out):
    my_y = here_ref[2]
    lane = lax.broadcasted_iota(jnp.int32, (1, PIX), 1)
    row_of = lax.broadcasted_iota(jnp.int32, (STRIP, PIX), 0)
    col_of = lax.broadcasted_iota(jnp.int32, (PATCH_PIX, PIX), 0)
    highs, mids, lows, hits = [], [], [], []
    for column in range(NZ):
        for core in range(NC):
            note = got[column, ENTRY_ROWS + core:ENTRY_ROWS + core + 1, :]
            weight = jnp.where(lane < SLOTS, note, 0.0)
            row = pltpu.roll(note, PIX - SLOTS, 1).astype(jnp.int32) - my_y * STRIP
            col = pltpu.roll(note, PIX - 2 * SLOTS, 1).astype(jnp.int32)
            line, pixel = row_of - row, col_of - col
            hit = (line >= 0) & (line < PIX)
            high, rest = split(weight)
            mid, low = split(weight - high.astype(F32))
            for many, piece in ((highs, high), (mids, mid), (lows, low)):
                many.append(jnp.where(hit, jnp.broadcast_to(piece.astype(F32), hit.shape), 0.0).astype(BF16))
            hits.append(jnp.where((pixel >= 0) & (pixel < PIX), 1.0, 0.0).astype(BF16))
    left = jnp.concatenate([jnp.concatenate(many, axis=1) for many in (highs, mids, lows)], axis=0)
    sums = lax.dot_general(left, jnp.concatenate(hits, axis=1), (((1,), (1,)), ((), ())),
                           preferred_element_type=F32)
    denominator = sums[:STRIP] + (sums[STRIP:2 * STRIP] + sums[2 * STRIP:]) + 1.0
    for side in range(2):
        rows = slice(side * STRIP, (side + 1) * STRIP)
        total = got[0, rows]
        for column in range(1, NZ):
            total = total + got[column, rows]
        lanes = slice(side * PIX, (side + 1) * PIX)
        out[:, lanes] = total / denominator[:, lanes]


def finish(here, got):
    vmem = pl.BlockSpec(memory_space=pltpu.VMEM)
    return pl.pallas_call(
        finish_kernel,
        in_specs=[pl.BlockSpec(memory_space=pltpu.SMEM), vmem],
        out_specs=vmem,
        out_shape=jax.ShapeDtypeStruct((STRIP, PATCH_PIX), F32),
        compiler_params=pltpu.CompilerParams(vmem_limit_bytes=ADD_LIMIT),
        name="finish",
    )(here, got)


def shift(value, along, by):
    pairs = []
    for x in range(NX):
        for core in range(NC):
            for y in range(NY):
                to = dict(x=x, y=y)
                to[along[core]] = (to[along[core]] + by) % RING
                pairs.append(((x * NC + core) * NY + y, (to["x"] * NC + core) * NY + to["y"]))
    return lax.ppermute(value, ("x", "core", "y"), pairs)


def body(image, variance, patches, offsets, psf_index, coeff_table, basis_taps):
    here = jnp.stack([lax.axis_index(axis) for axis in ("x", "core", "y")]).astype(jnp.int32)
    given = (psf_index, coeff_table.T, basis_taps, patches.transpose(0, 2, 1), offsets.transpose(0, 2, 3, 1),
             image, variance)

    own = [blur_half(half, *given) for half in range(2)]
    left = [shift(a, "yx", 1) for a in own]
    right = [shift(a, "yx", -1) for a in own]
    far = [shift(left[0], "yx", 1), shift(right[1], "yx", -1)]
    held = place(here, (*own, *left, *right), [(half, steps) for steps in (0, -1, 1) for half in range(2)], cost=9)
    far, held = lax.optimization_barrier((far, held))
    parts = place(here, far, [(0, 2), (1, 2)], held)

    stay_low, stay_high, right_low, right_high, far_low, far_high, left_low, left_high = parts
    from_left, from_right = shift(far_low, "xy", 1), shift(far_high, "xy", -1)
    high, low = shift(right_high, "xy", 1), shift(left_low, "xy", -1)
    right_low, left_high = add_received(right_low, from_left, left_high, from_right)
    mine, theirs = join(here, stay_low, low, shift(right_low, "xy", 1), stay_high, high, shift(left_high, "xy", -1))
    mine = mine + lax.ppermute(theirs, "core", [(0, 1), (1, 0)])
    got = lax.all_to_all(mine, "z", 0, 0, tiled=True)
    return finish(here, got)[None]


def solution(mesh):
    fine = Mesh(mesh.devices.reshape(NX, NZ, NC, NY), ("x", "z", "core", "y"))
    own = ("x", "z", "core")
    return jax.shard_map(
        body,
        mesh=fine,
        in_specs=(
            P("y", own, None, None),
            P("y", own, None, None),
            P("y", own, None),
            P("y", own, None, None),
            P("y", own),
            P(),
            P(),
        ),
        out_specs=P(own, "y", None),
        check_vma=False,
    )
```

time: 170 us -> 96.2 us (0.57)
  the two profiles are of different devices: /device:TPU:9 before, /device:TPU:62 now
where the time goes in v3:
time: 96.2 us; the launch traced here: 94.5 us
  waiting for transfers between devices  33.4 us (35%)
  blocking collectives  25.4 us (26%)
  Pallas kernels  20.3 us (21%)
  starting transfers between devices  15.1 us (16%)
    ppermute x12, waiting for transfers between devices, shift(): return lax.ppermute(value, ('x', 'core', 'y'), pairs)  31.4 us
    all_to_all x1, blocking collectives, body(): got = lax.all_to_all(mine, 'z', 0, 0, tiled=True)  25.4 us
    ppermute x12, starting transfers between devices, shift(): return lax.ppermute(value, ('x', 'core', 'y'), pairs)  15.1 us
    pallas_call x2, Pallas kernels, place(): pl.pallas_call(functools.partial(place_kernel, tuple(runs), bool(old)), i...  10.5 us
    pallas_call x2, Pallas kernels, blur_half(): pl.pallas_call(functools.partial(blur_kernel, half * HALF), grid=(1,), in...  6.92 us
    ppermute x1, waiting for transfers between devices, body(): mine = mine + lax.ppermute(theirs, 'core', [(0, 1), (1, 0)])  1.94 us
  transfers between devices with their start and end apart: 13, of which 10 were waited for; matrix products, arithmetic and copies ran while one was open for 0% of the time, Pallas kernels for 11%

profile of v3, /device:TPU:62, one launch (start us, length us, event | category | flops | bytes accessed | tf_op | source)
XLA Modules:
  0.0 94.5 jit_solution(12087914938285262831)
XLA Ops:
  0.0 3.5 %blur_half.2.refs_0_ = f32[1544,128]{1,0:T(8,128)S(1)} custom-call(s32[1,24]{1,0:T(1,128)} %psf_ref.3, f32[3,16]{1,0:T(4,128)} %bitcast.7, f32[3,2,21]{2,1,0:T(2,128)} %taps_ref.3, s32[1,2,24]{2,1,0:T(2,128)} %bitcast.11, s32[1,2,2,24]{3,2,1,0:T(2,128)} %bitcast.9, f32[1,24,128,128]{3,2,1,0:T(8,128)} %img_ref.3, f32[1,24,128,128]{3,2,1,0:T(8,128)} %var_ref.3), custom_call_target="tpu_custom_call" | custom-call | flops 912000000 | bytes 2359296 | tf_op jit(solution)/shard_map/blur_half/pallas_call | solution.py:102
  3.5 0.3 collective-permute-start
  3.8 3.5 %blur_half.3.refs_1_ = f32[1544,128]{1,0:T(8,128)S(1)} custom-call(s32[1,24]{1,0:T(1,128)} %psf_ref.3, f32[3,16]{1,0:T(4,128)} %bitcast.8, f32[3,2,21]{2,1,0:T(2,128)} %taps_ref.3, s32[1,2,24]{2,1,0:T(2,128)} %bitcast.12, s32[1,2,2,24]{3,2,1,0:T(2,128)} %bitcast.10, f32[1,24,128,128]{3,2,1,0:T(8,128)} %img_ref.3, f32[1,24,128,128]{3,2,1,0:T(8,128)} %var_ref.3), custom_call_target="tpu_custom_call" | custom-call | flops 912000000 | bytes 2359296 | tf_op jit(solution)/shard_map/blur_half/pallas_call | solution.py:102
  7.2 1.9 %collective-permute-start.2 = (f32[1544,128]{1,0:T(8,128)S(1)}, f32[1544,128]{1,0:T(8,128)S(1)}, u32[]{:S(2)}, u32[]{:S(2)}) collective-permute-start(f32[1544,128]{1,0:T(8,128)S(1)} %blur_half.3.refs_1_), channel_id=1, source_target_pairs={{0,3},{1,0},{2,1},{3,2},{4,196},{5,197},{6,198},{7,199},{64,67},{6... | collective-permute-start | bytes 2371592 | tf_op jit(solution)/shard_map/ppermute | solution.py:350
  9.1 0.7 collective-permute-start.5
  9.9 2.5 %collective-permute-start.4 = (f32[1544,128]{1,0:T(8,128)S(1)}, f32[1544,128]{1,0:T(8,128)}, u32[]{:S(2)}, u32[]{:S(2)}) collective-permute-start(f32[1544,128]{1,0:T(8,128)S(1)} %blur_half.3.refs_1_), channel_id=1, source_target_pairs={{0,1},{1,2},{2,3},{3,0},{4,68},{5,69},{6,70},{7,71},{64,65},{65,66... | collective-permute-start | bytes 2371592 | tf_op jit(solution)/shard_map/ppermute | solution.py:350
  12.3 3.2 %collective-permute-done.refs_2_ = f32[1544,128]{1,0:T(8,128)S(1)} collective-permute-done((f32[1544,128]{1,0:T(8,128)S(1)}, f32[1544,128]{1,0:T(8,128)S(1)}, u32[]{:S(2)}, u32[]{:S(2)}) %collective-permute-start) | collective-permute-done | bytes 790560 | tf_op jit(solution)/shard_map/ppermute | solution.py:350
  15.6 1.4 %collective-permute-start.1 = (f32[1544,128]{1,0:T(8,128)S(1)}, f32[1544,128]{1,0:T(8,128)}, u32[]{:S(2)}, u32[]{:S(2)}) collective-permute-start(f32[1544,128]{1,0:T(8,128)S(1)} %collective-permute-done.refs_2_), channel_id=1, source_target_pairs={{0,1},{1,2},{2,3},{3,0},{4,68},{5,69},{6,70},{7,71},{64,65},{65,66... | collective-permute-start | bytes 2371592 | tf_op jit(solution)/shard_map/ppermute | solution.py:350
  17.0 3.5 %collective-permute-done.2.refs_5_ = f32[1544,128]{1,0:T(8,128)S(1)} collective-permute-done((f32[1544,128]{1,0:T(8,128)S(1)}, f32[1544,128]{1,0:T(8,128)S(1)}, u32[]{:S(2)}, u32[]{:S(2)}) %collective-permute-start.2) | collective-permute-done | bytes 790560 | tf_op jit(solution)/shard_map/ppermute | solution.py:350
  20.6 0.6 collective-permute-start.3
  21.1 0.1 pad_add_fusion.here_ref
  21.2 7.9 %collective-permute-done.5.refs_4_ = f32[1544,128]{1,0:T(8,128)} collective-permute-done((f32[1544,128]{1,0:T(8,128)S(1)}, f32[1544,128]{1,0:T(8,128)}, u32[]{:S(2)}, u32[]{:S(2)}) %collective-permute-start.5) | collective-permute-done | bytes 790560 | tf_op jit(solution)/shard_map/ppermute | solution.py:350
  29.1 0.0 collective-permute-done.4.refs_3_
  29.1 6.5 %place.2 = (f32[64,2,64,128]{3,2,1,0:T(8,128)S(1)}, f32[64,128]{1,0:T(8,128)S(1)}) custom-call(s32[3]{0:T(128)S(1)} %pad_add_fusion.here_ref, f32[1544,128]{1,0:T(8,128)S(1)} %blur_half.2.refs_0_, f32[1544,128]{1,0:T(8,128)S(1)} %blur_half.3.refs_1_, f32[1544,128]{1,0:T(8,128)S(1)} %collective-permute-done.refs_2_, ...), custom_call_target="tpu_custom_call" | custom-call | flops 1000000 | bytes 33210000 | tf_op jit(solution)/shard_map/place/pallas_call | solution.py:235
  35.6 0.0 collective-permute-done.1.refs_0_
  35.6 2.0 %collective-permute-done.3.refs_1_ = f32[1544,128]{1,0:T(8,128)} collective-permute-done((f32[1544,128]{1,0:T(8,128)S(1)}, f32[1544,128]{1,0:T(8,128)}, u32[]{:S(2)}, u32[]{:S(2)}) %collective-permute-start.3) | collective-permute-done | bytes 790560 | tf_op jit(solution)/shard_map/ppermute | solution.py:350
  37.6 4.1 %place.3 = (f32[1032,128]{1,0:T(8,128)S(1)}, f32[1032,128]{1,0:T(8,128)S(1)}, f32[1032,128]{1,0:T(8,128)S(1)}, f32[1032,128]{1,0:T(8,128)S(1)}, f32[1032,128]{1,...) custom-call(s32[3]{0:T(128)S(1)} %pad_add_fusion.here_ref, ...), custom_call_target="tpu_custom_call" | custom-call | flops 1000000 | bytes 22140000 | tf_op jit(solution)/shard_map/place/pallas_call | solution.py:235
  41.7 0.7 collective-permute-start.7
  42.4 1.5 %collective-permute-start.8 = (f32[1032,128]{1,0:T(8,128)S(1)}, f32[1032,128]{1,0:T(8,128)S(1)}, u32[]{:S(2)}, u32[]{:S(2)}) collective-permute-start(f32[1032,128]{1,0:T(8,128)S(1)} %get-tuple-element.34), channel_id=1, source_target_pairs={{0,192},{1,193},{2,194},{3,195},{4,7},{5,4},{6,5},{7,6},{64,0},{65... | collective-permute-start | bytes 1585160 | tf_op jit(solution)/shard_map/ppermute | solution.py:350
  43.9 0.8 collective-permute-start.6
  44.8 2.4 %collective-permute-start.10 = (f32[1032,128]{1,0:T(8,128)S(1)}, f32[1032,128]{1,0:T(8,128)S(1)}, u32[]{:S(2)}, u32[]{:S(2)}) collective-permute-start(f32[1032,128]{1,0:T(8,128)S(1)} %get-tuple-element.37), channel_id=1, source_target_pairs={{0,64},{1,65},{2,66},{3,67},{4,5},{5,6},{6,7},{7,4},{64,128},{65,1... | collective-permute-start | bytes 1585160 | tf_op jit(solution)/shard_map/ppermute | solution.py:350
  47.2 4.0 %collective-permute-done.7.b = f32[1032,128]{1,0:T(8,128)S(1)} collective-permute-done((f32[1032,128]{1,0:T(8,128)S(1)}, f32[1032,128]{1,0:T(8,128)S(1)}, u32[]{:S(2)}, u32[]{:S(2)}) %collective-permute-start.7) | collective-permute-done | bytes 528416 | tf_op jit(solution)/shard_map/ppermute | solution.py:350
  51.1 1.7 %collective-permute-done.8.d = f32[1032,128]{1,0:T(8,128)S(1)} collective-permute-done((f32[1032,128]{1,0:T(8,128)S(1)}, f32[1032,128]{1,0:T(8,128)S(1)}, u32[]{:S(2)}, u32[]{:S(2)}) %collective-permute-start.8) | collective-permute-done | bytes 528416 | tf_op jit(solution)/shard_map/ppermute | solution.py:350
  52.8 0.1 add_received.1
  52.9 0.4 collective-permute-start.9
  53.3 1.7 %collective-permute-start.11 = (f32[1032,128]{1,0:T(8,128)S(1)}, f32[1032,128]{1,0:T(8,128)S(1)}, u32[]{:S(2)}, u32[]{:S(2)}) collective-permute-start(f32[1032,128]{1,0:T(8,128)S(1)} %get-tuple-element.38), channel_id=1, source_target_pairs={{0,192},{1,193},{2,194},{3,195},{4,7},{5,4},{6,5},{7,6},{64,0},{65... | collective-permute-start | bytes 1585160 | tf_op jit(solution)/shard_map/ppermute | solution.py:350
  55.0 3.4 %collective-permute-done.6.low_b = f32[1032,128]{1,0:T(8,128)S(1)} collective-permute-done((f32[1032,128]{1,0:T(8,128)S(1)}, f32[1032,128]{1,0:T(8,128)S(1)}, u32[]{:S(2)}, u32[]{:S(2)}) %collective-permute-start.6) | collective-permute-done | bytes 528416 | tf_op jit(solution)/shard_map/ppermute | solution.py:350
  58.5 0.0 collective-permute-done.10.high_b
  58.5 4.0 %collective-permute-done.9.low_c = f32[1032,128]{1,0:T(8,128)S(1)} collective-permute-done((f32[1032,128]{1,0:T(8,128)S(1)}, f32[1032,128]{1,0:T(8,128)S(1)}, u32[]{:S(2)}, u32[]{:S(2)}) %collective-permute-start.9) | collective-permute-done | bytes 528416 | tf_op jit(solution)/shard_map/ppermute | solution.py:350
  62.5 1.7 %collective-permute-done.11.high_c = f32[1032,128]{1,0:T(8,128)S(1)} collective-permute-done((f32[1032,128]{1,0:T(8,128)S(1)}, f32[1032,128]{1,0:T(8,128)S(1)}, u32[]{:S(2)}, u32[]{:S(2)}) %collective-permute-start.11) | collective-permute-done | bytes 528416 | tf_op jit(solution)/shard_map/ppermute | solution.py:350
  64.2 0.8 join.1
  65.0 0.1 collective-permute-start.12
  65.1 1.9 %collective-permute-done.12 = f32[8,136,128]{2,1,0:T(8,128)S(1)} collective-permute-done((f32[8,136,128]{2,1,0:T(8,128)S(1)}, f32[8,136,128]{2,1,0:T(8,128)S(1)}, u32[]{:S(2)}, u32[]{:S(2)}) %collective-permute-start.12) | collective-permute-done | bytes 557088 | tf_op jit(solution)/shard_map/ppermute | solution.py:371
  67.1 0.1 add.3
  67.1 25.4 %all_to_all.5.got = f32[8,136,128]{2,1,0:T(8,128)S(1)} all-to-all(f32[8,136,128]{2,1,0:T(8,128)S(1)} %add.3), channel_id=1, replica_groups=mesh['x'=4,'z'=8,'core'=2,'y'=4] {'z'}, dimensions={0} | all-to-all | bytes 1114112 | tf_op jit(solution)/shard_map/all_to_all | solution.py:372
  92.5 1.9 %finish.1 = f32[64,256]{1,0:T(8,128)} custom-call(s32[3]{0:T(128)S(1)} %pad_add_fusion.here_ref, f32[8,136,128]{2,1,0:T(8,128)S(1)} %all_to_all.5.got), custom_call_target="tpu_custom_call" | custom-call | tf_op jit(solution)/shard_map/finish/pallas_call | solution.py:332
Async XLA Ops:
  3.5 12.1 %collective-permute-start = (f32[1544,128]{1,0:T(8,128)S(1)}, f32[1544,128]{1,0:T(8,128)S(1)}, u32[]{:S(2)}, u32[]{:S(2)}) collective-permute-start(f32[1544,128]{1,0:T(8,128)S(1)} %blur_half.2.refs_0_), channel_id=1, source_target_pairs={{0,1},{1,2},{2,3},{3,0},{4,68},{5,69},{6,70},{7,71},{64,65},{65,66... | collective-permute-start | bytes 2371592 | tf_op jit(solution)/shard_map/ppermute | solution.py:350
  7.2 13.3 %collective-permute-start.2 = (f32[1544,128]{1,0:T(8,128)S(1)}, f32[1544,128]{1,0:T(8,128)S(1)}, u32[]{:S(2)}, u32[]{:S(2)}) collective-permute-start(f32[1544,128]{1,0:T(8,128)S(1)} %blur_half.3.refs_1_), channel_id=1, source_target_pairs={{0,3},{1,0},{2,1},{3,2},{4,196},{5,197},{6,198},{7,199},{64,67},{6... | collective-permute-start | bytes 2371592 | tf_op jit(solution)/shard_map/ppermute | solution.py:350
  9.1 20.0 %collective-permute-start.5 = (f32[1544,128]{1,0:T(8,128)S(1)}, f32[1544,128]{1,0:T(8,128)}, u32[]{:S(2)}, u32[]{:S(2)}) collective-permute-start(f32[1544,128]{1,0:T(8,128)S(1)} %blur_half.2.refs_0_), channel_id=1, source_target_pairs={{0,3},{1,0},{2,1},{3,2},{4,196},{5,197},{6,198},{7,199},{64,67},{6... | collective-permute-start | bytes 2371592 | tf_op jit(solution)/shard_map/ppermute | solution.py:350
  9.9 19.3 %collective-permute-start.4 = (f32[1544,128]{1,0:T(8,128)S(1)}, f32[1544,128]{1,0:T(8,128)}, u32[]{:S(2)}, u32[]{:S(2)}) collective-permute-start(f32[1544,128]{1,0:T(8,128)S(1)} %blur_half.3.refs_1_), channel_id=1, source_target_pairs={{0,1},{1,2},{2,3},{3,0},{4,68},{5,69},{6,70},{7,71},{64,65},{65,66... | collective-permute-start | bytes 2371592 | tf_op jit(solution)/shard_map/ppermute | solution.py:350
  15.6 20.0 %collective-permute-start.1 = (f32[1544,128]{1,0:T(8,128)S(1)}, f32[1544,128]{1,0:T(8,128)}, u32[]{:S(2)}, u32[]{:S(2)}) collective-permute-start(f32[1544,128]{1,0:T(8,128)S(1)} %collective-permute-done.refs_2_), channel_id=1, source_target_pairs={{0,1},{1,2},{2,3},{3,0},{4,68},{5,69},{6,70},{7,71},{64,65},{65,66... | collective-permute-start | bytes 2371592 | tf_op jit(solution)/shard_map/ppermute | solution.py:350
  20.6 17.0 %collective-permute-start.3 = (f32[1544,128]{1,0:T(8,128)S(1)}, f32[1544,128]{1,0:T(8,128)}, u32[]{:S(2)}, u32[]{:S(2)}) collective-permute-start(f32[1544,128]{1,0:T(8,128)S(1)} %collective-permute-done.2.refs_5_), channel_id=1, source_target_pairs={{0,3},{1,0},{2,1},{3,2},{4,196},{5,197},{6,198},{7,199},{64,67},{6... | collective-permute-start | bytes 2371592 | tf_op jit(solution)/shard_map/ppermute | solution.py:350
  41.7 9.5 %collective-permute-start.7 = (f32[1032,128]{1,0:T(8,128)S(1)}, f32[1032,128]{1,0:T(8,128)S(1)}, u32[]{:S(2)}, u32[]{:S(2)}) collective-permute-start(f32[1032,128]{1,0:T(8,128)S(1)} %get-tuple-element.32), channel_id=1, source_target_pairs={{0,64},{1,65},{2,66},{3,67},{4,5},{5,6},{6,7},{7,4},{64,128},{65,1... | collective-permute-start | bytes 1585160 | tf_op jit(solution)/shard_map/ppermute | solution.py:350
  42.4 10.4 %collective-permute-start.8 = (f32[1032,128]{1,0:T(8,128)S(1)}, f32[1032,128]{1,0:T(8,128)S(1)}, u32[]{:S(2)}, u32[]{:S(2)}) collective-permute-start(f32[1032,128]{1,0:T(8,128)S(1)} %get-tuple-element.34), channel_id=1, source_target_pairs={{0,192},{1,193},{2,194},{3,195},{4,7},{5,4},{6,5},{7,6},{64,0},{65... | collective-permute-start | bytes 1585160 | tf_op jit(solution)/shard_map/ppermute | solution.py:350
  43.9 14.5 %collective-permute-start.6 = (f32[1032,128]{1,0:T(8,128)S(1)}, f32[1032,128]{1,0:T(8,128)S(1)}, u32[]{:S(2)}, u32[]{:S(2)}) collective-permute-start(f32[1032,128]{1,0:T(8,128)S(1)} %get-tuple-element.30), channel_id=1, source_target_pairs={{0,192},{1,193},{2,194},{3,195},{4,7},{5,4},{6,5},{7,6},{64,0},{65... | collective-permute-start | bytes 1585160 | tf_op jit(solution)/shard_map/ppermute | solution.py:350
  44.8 13.7 %collective-permute-start.10 = (f32[1032,128]{1,0:T(8,128)S(1)}, f32[1032,128]{1,0:T(8,128)S(1)}, u32[]{:S(2)}, u32[]{:S(2)}) collective-permute-start(f32[1032,128]{1,0:T(8,128)S(1)} %get-tuple-element.37), channel_id=1, source_target_pairs={{0,64},{1,65},{2,66},{3,67},{4,5},{5,6},{6,7},{7,4},{64,128},{65,1... | collective-permute-start | bytes 1585160 | tf_op jit(solution)/shard_map/ppermute | solution.py:350
  52.9 9.5 %collective-permute-start.9 = (f32[1032,128]{1,0:T(8,128)S(1)}, f32[1032,128]{1,0:T(8,128)S(1)}, u32[]{:S(2)}, u32[]{:S(2)}) collective-permute-start(f32[1032,128]{1,0:T(8,128)S(1)} %get-tuple-element.35), channel_id=1, source_target_pairs={{0,64},{1,65},{2,66},{3,67},{4,5},{5,6},{6,7},{7,4},{64,128},{65,1... | collective-permute-start | bytes 1585160 | tf_op jit(solution)/shard_map/ppermute | solution.py:350
  53.3 10.9 %collective-permute-start.11 = (f32[1032,128]{1,0:T(8,128)S(1)}, f32[1032,128]{1,0:T(8,128)S(1)}, u32[]{:S(2)}, u32[]{:S(2)}) collective-permute-start(f32[1032,128]{1,0:T(8,128)S(1)} %get-tuple-element.38), channel_id=1, source_target_pairs={{0,192},{1,193},{2,194},{3,195},{4,7},{5,4},{6,5},{7,6},{64,0},{65... | collective-permute-start | bytes 1585160 | tf_op jit(solution)/shard_map/ppermute | solution.py:350
  65.0 2.0 %collective-permute-start.12 = (f32[8,136,128]{2,1,0:T(8,128)S(1)}, f32[8,136,128]{2,1,0:T(8,128)S(1)}, u32[]{:S(2)}, u32[]{:S(2)}) collective-permute-start(f32[8,136,128]{2,1,0:T(8,128)S(1)} %get-tuple-element.40), channel_id=1, source_target_pairs={{0,4},{4,0},{1,5},{5,1},{2,6},{6,2},{3,7},{7,3},{8,12},{12,8},{9,1... | collective-permute-start | bytes 1671176 | tf_op jit(solution)/shard_map/ppermute | solution.py:371

commit v4 on v3

v4 whole, which is shorter than its diff:
```python
import functools

import jax
import jax.numpy as jnp
from jax import lax
from jax.experimental import pallas as pl
from jax.experimental.pallas import tpu as pltpu
from jax.sharding import Mesh
from jax.sharding import PartitionSpec as P

PIX = 128
PATCH_PIX = 256
TAPS = 21
MARGIN = TAPS // 2
NB = 3
NX, NZ, NC, NY = 4, 8, 2, 4
RING = 4
STRIP = PATCH_PIX // NY
TILES = 24
PARTS = ((0, 12), (12, 12))
UNROLL = 3
META = 8
PATCH, ROW, COL, RANK, WEIGHT = range(5)
ENTRIES = NZ * NC
ENTRY_ROWS = 2 * STRIP
SLOTS = 32
STEPS = (1, 2, 3, -1, -2, -3)
LAST = ((0, 8), (4, 12), (32, 36), (40, 44), (24,), (28,), (48,), (52,), (16, 20), (56, 60))
F32 = jnp.float32
BF16 = jnp.bfloat16
BLUR_LIMIT = 56 * 1024 * 1024
PLACE_LIMIT = 24 * 1024 * 1024
ADD_LIMIT = 12 * 1024 * 1024


def split(value):
    high = value.astype(BF16)
    return high, (value - high.astype(F32)).astype(BF16)


def dot(a, b):
    return jnp.dot(a, b, preferred_element_type=F32)


def blur_kernel(first, tiles, psf_ref, table_ref, taps_ref, patch_ref, offset_ref, img_ref, var_ref, out_ref,
                col_hi, col_lo, rows):
    major = lax.broadcasted_iota(jnp.int32, (PIX, PIX), 0)
    minor = lax.broadcasted_iota(jnp.int32, (PIX, PIX), 1)
    for b in range(NB):
        lanes = slice(b * PIX, (b + 1) * PIX)
        for axis, diff in ((0, minor - major), (1, major - minor)):
            band = jnp.zeros((PIX, PIX), F32)
            for t in range(TAPS):
                band = jnp.where(diff == t - MARGIN, taps_ref[b, axis, t], band)
            hi, lo = split(band)
            if axis:
                col_hi[:PIX, lanes], col_hi[PIX:, lanes], col_lo[:, lanes] = hi, hi, lo
            else:
                rows[:PIX, lanes], rows[PIX:, lanes] = hi, lo

    x_hi, x_lo = split(img_ref[0].reshape(tiles * PIX, PIX))
    smooth = dot(jnp.concatenate([x_hi, x_lo], axis=1), col_hi[...]) + dot(x_hi, col_lo[...])
    weights = []
    for n in range(tiles):
        total = jnp.sum(jnp.sum(var_ref[0, n], axis=0, keepdims=True), axis=1, keepdims=True)
        weights.append(1.0 / (total * (1.0 / (PIX * PIX))))
    for pair in range(tiles // 2):
        sides = []
        for n in (2 * pair, 2 * pair + 1):
            row = psf_ref[0, first + n]
            sides.append(jnp.concatenate(
                [smooth[n * PIX:(n + 1) * PIX, b * PIX:(b + 1) * PIX] * (table_ref[b, row] * weights[n])
                 for b in range(NB)], axis=0))
        q_hi, q_lo = split(jnp.concatenate(sides, axis=1))
        both = dot(rows[...], q_hi)
        done = both[:PIX] + (both[PIX:] + dot(rows[:PIX], q_lo))
        for n in range(2):
            at = META + (2 * pair + n) * PIX
            out_ref[at:at + PIX, :] = done[:, n * PIX:(n + 1) * PIX]

    lane = lax.broadcasted_iota(jnp.int32, (META, PIX), 1)
    kind = lax.broadcasted_iota(jnp.int32, (META, PIX), 0)
    patch, facts = jnp.zeros((META, PIX), jnp.int32), jnp.zeros((META, PIX), jnp.int32)
    for t in range(TILES):
        for k in range(2):
            here = lane == 2 * t + k
            patch = jnp.where(here, patch_ref[0, k, t], patch)
            place = jnp.where(kind == ROW, offset_ref[0, k, 0, t], offset_ref[0, k, 1, t])
            facts = jnp.where(here, place, facts)
    rank = jnp.zeros((META, PIX), jnp.int32)
    for t in range(TILES):
        for k in range(2):
            rank += jnp.where((patch == patch_ref[0, k, t]) & (lane > 2 * t + k), 1, 0)
    facts = jnp.where(kind == PATCH, patch, jnp.where(kind == RANK, rank, facts)).astype(F32)
    for n in range(tiles):
        facts = jnp.where((kind == WEIGHT) & ((lane >> 1) == first + n), weights[n], facts)
    out_ref[0:META, :] = facts


def blur_part(part, psf_index, table, taps, patches, offsets, image, variance):
    first, tiles = PARTS[part]
    smem = pl.BlockSpec(memory_space=pltpu.SMEM)
    block = pl.BlockSpec((1, tiles, PIX, PIX), lambda i: (0, first // tiles, 0, 0))
    rows = META + tiles * PIX
    return pl.pallas_call(
        functools.partial(blur_kernel, first, tiles),
        grid=(1,),
        in_specs=[smem] * 5 + [block, block],
        out_specs=pl.BlockSpec((rows, PIX), lambda i: (0, 0)),
        out_shape=pltpu.VMEM((rows, PIX), F32),
        scratch_shapes=[pltpu.VMEM((2 * PIX, NB * PIX), BF16), pltpu.VMEM((PIX, NB * PIX), BF16),
                        pltpu.VMEM((2 * PIX, NB * PIX), BF16)],
        compiler_params=pltpu.CompilerParams(vmem_limit_bytes=BLUR_LIMIT),
        cost_estimate=pl.CostEstimate(flops=tiles * 76 * 10**6, bytes_accessed=tiles * 3 * 65536,
                                      transcendentals=0),
        name="blur_part",
    )(psf_index, table, taps, patches, offsets, image, variance)


def place_kernel(runs, held, last, here_ref, *refs):
    count = len(runs)
    tiles, refs = refs[:count], refs[count:]
    if held:
        old_canvas, old_notes, *refs = refs
    *outs, canvas, notes = refs[:-6]
    buf, whole_facts, whole_ref, weight_ref, list_ref, sems = refs[-6:]
    copies, starts, at = [], [], STRIP
    for n, source in enumerate(tiles):
        copies.append(pltpu.make_async_copy(source, buf.at[pl.ds(at, source.shape[0])], sems.at[n]))
        copies[n].start()
        buf[at - STRIP:at] = jnp.zeros((STRIP, PIX), F32)
        starts.append(at + META)
        at += source.shape[0] + STRIP
    buf[at - STRIP:at] = jnp.zeros((STRIP, PIX), F32)
    if held:
        canvas[...] = old_canvas[...]
        notes[...] = old_notes[...]
    else:
        canvas[...] = jnp.zeros(canvas.shape, F32)
        notes[...] = jnp.zeros(notes.shape, F32)
    my_x, core, my_y = here_ref[0], here_ref[1], here_ref[2]
    to_scalars = []
    for n, copy in enumerate(copies):
        copy.wait()
        rows = pl.ds(n * META, META)
        head = pl.ds(starts[n] - META, META)
        whole_facts[n * META:(n + 1) * META] = buf[starts[n] - META:starts[n]].astype(jnp.int32)
        to_scalars.append(pltpu.make_async_copy(whole_facts.at[rows], whole_ref.at[rows], sems.at[count + n]))
        to_scalars.append(pltpu.make_async_copy(buf.at[head], weight_ref.at[rows], sems.at[2 * count + n]))
        for scalars in to_scalars[-2:]:
            scalars.start()
    for scalars in to_scalars:
        scalars.wait()
    row_of = lax.broadcasted_iota(jnp.int32, (8, PIX), 0)
    lane = lax.broadcasted_iota(jnp.int32, (8, PIX), 1)
    lane_one = lax.broadcasted_iota(jnp.int32, (1, PIX), 1)

    def add(items):
        moved = [pltpu.roll(buf[pl.ds(tile_row + skip, STRIP), :], (col + PIX) & (PIX - 1), 1)
                 for _, tile_row, skip, col in items]
        for (at, _, skip, col), strip in zip(items, moved):
            sides = [(lane >= col - n * PIX) & (lane < col - n * PIX + PIX) for n in range(2)]
            for g in range(0, STRIP, 8):
                line = row_of + (skip + g)
                inside = (line >= 0) & (line < PIX)
                for n in range(2):
                    canvas[at, n, g:g + 8] += jnp.where(inside & sides[n], strip[g:g + 8], 0.0)

    def bounded(skip):
        return jnp.clip(skip, -STRIP, PIX)

    def pair_of(index, pair, slot):
        patch, row, col, rank = (whole_ref[index * META + kind, pair] for kind in (PATCH, ROW, COL, RANK))
        weight = weight_ref[index * META + WEIGHT, pair]
        slot = slot + rank
        place = jnp.where(lane_one == slot + SLOTS, row, jnp.where(lane_one == slot + 2 * SLOTS, col, 0))
        return patch, row, col, jnp.where(lane_one == slot, weight, place.astype(F32))

    def entry_of(patch):
        z = (patch >> 1) & (NZ - 1)
        return (z >> 2) * NZ + ((patch & 1) ^ core) * (NZ // 2) + (z & (NZ // 2 - 1))

    def slot_of(reduce_at, source_at):
        return reduce_at * (2 * RING) + (source_at & (RING - 1)) * 2

    def along_y(t, carry, index, pair, base, steps):
        items = []
        for n in range(UNROLL):
            for k in range(2):
                patch, row, col, note = pair_of(index, pair + 2 * (UNROLL * t + n) + k, slot_of(my_x, my_y + steps))
                at = (((patch >> 4) - my_x) & (RING - 1)) * ENTRIES + entry_of(patch)
                notes[pl.ds(at, 1), :] += note
                items.append((at, base + (UNROLL * t + n) * PIX, bounded(my_y * STRIP - row), col))
        add(items)
        return carry

    def list_x(t, number, index, pair, base, steps):
        for n in range(UNROLL):
            for k in range(2):
                lane_of = pair + 2 * (UNROLL * t + n) + k
                list_ref[0, number] = index * PIX + lane_of
                list_ref[1, number] = base + (UNROLL * t + n) * PIX
                list_ref[2, number] = slot_of(my_y, my_x + steps)
                number += jnp.where((whole_ref[index * META + PATCH, lane_of] >> 4) == my_x, 1, 0)
        return number

    def along_x(t, number):
        items = []
        for k in range(2):
            valid = 2 * t + k < number
            at = jnp.minimum(2 * t + k, number - 1)
            code, tile_row, slot = list_ref[0, at], list_ref[1, at], list_ref[2, at]
            patch, row, col, note = pair_of(code >> 7, code & (PIX - 1), jnp.where(valid, slot, PIX))
            for n in range(NY):
                notes[pl.ds(n * ENTRIES + entry_of(patch), 1), :] += note
            for n in range(3):
                strip = (jnp.maximum(row, 0) >> 6) + n
                skip = jnp.where(valid & (strip < NY), bounded(strip * STRIP - row), PIX)
                at = ((strip - my_y) & (RING - 1)) * ENTRIES + entry_of(patch)
                items.append((at, tile_row, skip, col))
        add(items)
        return number

    given = [(PARTS[part][1] // UNROLL, dict(index=n, pair=2 * PARTS[part][0], base=starts[n], steps=steps))
             for n, (part, steps) in enumerate(runs)]

    @pl.when(core == 0)
    def _():
        for groups, run in given:
            lax.fori_loop(0, groups, functools.partial(along_y, **run), 0)

    @pl.when(core == 1)
    def _():
        number = 0
        for groups, run in given:
            number = lax.fori_loop(0, groups, functools.partial(list_x, **run), number)
        lax.fori_loop(0, (number + 1) >> 1, along_x, number)

    if last:
        for out, first in zip(outs, LAST):
            at = 0
            for start in first:
                out[at * ENTRY_ROWS:(at + 4) * ENTRY_ROWS] = canvas[start:start + 4].reshape(4 * ENTRY_ROWS, PIX)
                out[len(first) * 4 * ENTRY_ROWS + at:len(first) * 4 * ENTRY_ROWS + at + 4] = notes[start:start + 4]
                at += 4


def place(here, arrays, runs, old=(), last=False, cost=6):
    smem = pl.BlockSpec(memory_space=pltpu.SMEM)
    hbm = pl.BlockSpec(memory_space=pl.ANY)
    vmem = pl.BlockSpec(memory_space=pltpu.VMEM)
    canvas, notes = (RING * ENTRIES, 2, STRIP, PIX), (RING * ENTRIES, PIX)
    count, rows = len(arrays), sum(a.shape[0] + STRIP for a in arrays) + STRIP
    outs = [canvas, notes]
    if last:
        outs = [(len(first) * 4 * ENTRY_ROWS + 8, PIX) for first in LAST]
    return pl.pallas_call(
        functools.partial(place_kernel, tuple(runs), bool(old), last),
        in_specs=[smem] + [hbm] * count + [vmem] * len(old),
        out_specs=[vmem] * len(outs),
        out_shape=[pltpu.VMEM(shape, F32) for shape in outs],
        scratch_shapes=([pltpu.VMEM(canvas, F32), pltpu.VMEM(notes, F32)] if last else [])
        + [pltpu.VMEM((rows, PIX), F32),
           pltpu.VMEM((count * META, PIX), jnp.int32),
           pltpu.SMEM((count * META, PIX), jnp.int32),
           pltpu.SMEM((count * META, PIX), F32),
           pltpu.SMEM((3, count * 2 * TILES), jnp.int32),
           pltpu.SemaphoreType.DMA((3 * count,))],
        compiler_params=pltpu.CompilerParams(vmem_limit_bytes=PLACE_LIMIT),
        cost_estimate=pl.CostEstimate(flops=10**6, bytes_accessed=cost * 3690000, transcendentals=0),
        name="place",
    )(here, *arrays, *old)


def add_kernel(a, b, c, d, *outs):
    size = 4 * ENTRY_ROWS
    for n, (one, other) in enumerate(((a, b), (c, d))):
        for k in range(2):
            out = outs[2 * n + k]
            out[:size] = one[k * size:(k + 1) * size] + other[k * size:(k + 1) * size]
            rows = slice(2 * size + 4 * k, 2 * size + 4 * k + 4)
            out[size:size + 4] = one[rows] + other[rows]


def add_received(*arrays):
    vmem = pl.BlockSpec(memory_space=pltpu.VMEM)
    return pl.pallas_call(
        add_kernel,
        in_specs=[vmem] * 4,
        out_specs=[vmem] * 4,
        out_shape=[pltpu.VMEM((4 * ENTRY_ROWS + 8, PIX), F32)] * 4,
        compiler_params=pltpu.CompilerParams(vmem_limit_bytes=ADD_LIMIT),
        name="add_received",
    )(*arrays)


def join_kernel(here_ref, stay, stay_cross, *refs):
    arrays, outs, total, note_sums = refs[:8], refs[8:17], refs[17], refs[18]
    core, my_z = here_ref[1], here_ref[3]
    size = 4 * ENTRY_ROWS
    for half in range(2):
        rows = slice(half * size, (half + 1) * size)
        same, cross = arrays[2 * half:2 * half + 2], arrays[4 + 2 * half:6 + 2 * half]
        total[rows] = ((stay[rows] + stay_cross[rows]) + (same[0][:size] + same[1][:size])
                       + (cross[0][:size] + cross[1][:size]))
        head = slice(2 * size + 4 * half, 2 * size + 4 * half + 4)
        for n, (first, rest) in enumerate(((stay, same), (stay_cross, cross))):
            note_sums[8 * n + 4 * half:8 * n + 4 * half + 4] = (
                first[head] + (rest[0][size:size + 4] + rest[1][size:size + 4]))
    kind = lax.broadcasted_iota(jnp.int32, (8, PIX), 0)

    def rows_of(steps, start, count):
        owner = (my_z + steps) & (NZ - 1)
        return total[pl.ds(pl.multiple_of(owner * ENTRY_ROWS + start, 8), count), :]

    def notes_of(steps, row):
        owner = (my_z + steps) & (NZ - 1)
        same, cross = (note_sums[pl.ds(8 * n + owner, 1), :] for n in range(2))
        return jnp.where(kind == row + core, same, jnp.where(kind == row + 1 - core, cross, 0.0))

    for out, steps in zip(outs, (0, *STEPS)):
        out[:ENTRY_ROWS] = rows_of(steps, 0, ENTRY_ROWS)
        out[ENTRY_ROWS:] = notes_of(steps, 0)
    outs[7][...] = rows_of(4, 0, STRIP)
    outs[8][:STRIP] = rows_of(4, STRIP, STRIP)
    outs[8][STRIP:] = notes_of(4, NC)


def join(here, *arrays):
    vmem = pl.BlockSpec(memory_space=pltpu.VMEM)
    rows = [ENTRY_ROWS + 8] * 7 + [STRIP, STRIP + 8]
    return pl.pallas_call(
        join_kernel,
        in_specs=[pl.BlockSpec(memory_space=pltpu.SMEM)] + [vmem] * 10,
        out_specs=[vmem] * 9,
        out_shape=[pltpu.VMEM((n, PIX), F32) for n in rows],
        scratch_shapes=[pltpu.VMEM((NZ * ENTRY_ROWS, PIX), F32), pltpu.VMEM((2 * NZ, PIX), F32)],
        compiler_params=pltpu.CompilerParams(vmem_limit_bytes=ADD_LIMIT),
        name="join",
    )(here, *arrays)


def relay_kernel(ahead, behind, from_left, from_right, ahead_out, behind_out):
    ahead_out[:STRIP] = ahead[:STRIP] + from_left[...]
    ahead_out[STRIP:] = ahead[STRIP:]
    behind_out[:STRIP] = behind[:STRIP]
    behind_out[STRIP:] = behind[STRIP:] + from_right[...]


def relay(*arrays):
    vmem = pl.BlockSpec(memory_space=pltpu.VMEM)
    return pl.pallas_call(
        relay_kernel,
        in_specs=[vmem] * 4,
        out_specs=[vmem] * 2,
        out_shape=[pltpu.VMEM(arrays[0].shape, F32)] * 2,
        compiler_params=pltpu.CompilerParams(vmem_limit_bytes=ADD_LIMIT),
        name="relay",
    )(*arrays)


def finish_kernel(here_ref, *refs):
    *got, out = refs
    my_y = here_ref[2]
    lane = lax.broadcasted_iota(jnp.int32, (1, PIX), 1)
    row_of = lax.broadcasted_iota(jnp.int32, (STRIP, PIX), 0)
    col_of = lax.broadcasted_iota(jnp.int32, (PATCH_PIX, PIX), 0)
    highs, mids, lows, hits = [], [], [], []
    for source in (*got, got[-1]):
        for core in range(NC):
            at = ENTRY_ROWS + core + (NC if len(hits) >= len(got) * NC else 0)
            note = source[at:at + 1, :]
            weight = jnp.where(lane < SLOTS, note, 0.0)
            row = pltpu.roll(note, PIX - SLOTS, 1).astype(jnp.int32) - my_y * STRIP
            col = pltpu.roll(note, PIX - 2 * SLOTS, 1).astype(jnp.int32)
            line, pixel = row_of - row, col_of - col
            hit = (line >= 0) & (line < PIX)
            high, rest = split(weight)
            mid, low = split(weight - high.astype(F32))
            for many, piece in ((highs, high), (mids, mid), (lows, low)):
                many.append(jnp.where(hit, jnp.broadcast_to(piece.astype(F32), hit.shape), 0.0).astype(BF16))
            hits.append(jnp.where((pixel >= 0) & (pixel < PIX), 1.0, 0.0).astype(BF16))
    left = jnp.concatenate([jnp.concatenate(many, axis=1) for many in (highs, mids, lows)], axis=0)
    sums = lax.dot_general(left, jnp.concatenate(hits, axis=1), (((1,), (1,)), ((), ())),
                           preferred_element_type=F32)
    denominator = sums[:STRIP] + (sums[STRIP:2 * STRIP] + sums[2 * STRIP:]) + 1.0
    for side in range(2):
        rows = slice(side * STRIP, (side + 1) * STRIP)
        total = got[0][rows]
        for source in got[1:]:
            total = total + source[rows]
        lanes = slice(side * PIX, (side + 1) * PIX)
        out[:, lanes] = total / denominator[:, lanes]


def finish(here, got):
    vmem = pl.BlockSpec(memory_space=pltpu.VMEM)
    return pl.pallas_call(
        finish_kernel,
        in_specs=[pl.BlockSpec(memory_space=pltpu.SMEM)] + [vmem] * len(got),
        out_specs=vmem,
        out_shape=jax.ShapeDtypeStruct((STRIP, PATCH_PIX), F32),
        compiler_params=pltpu.CompilerParams(vmem_limit_bytes=ADD_LIMIT),
        name="finish",
    )(here, *got)


def shift_z(value, by):
    return lax.ppermute(value, "z", [(z, (z + by) % NZ) for z in range(NZ)])


def shift(value, along, by, cross=False):
    pairs = []
    for x in range(NX):
        for core in range(NC):
            for y in range(NY):
                to = dict(x=x, y=y)
                to[along[core]] = (to[along[core]] + by) % RING
                to_core = 1 - core if cross else core
                pairs.append(((x * NC + core) * NY + y, (to["x"] * NC + to_core) * NY + to["y"]))
    return lax.ppermute(value, ("x", "core", "y"), pairs)


def body(image, variance, patches, offsets, psf_index, coeff_table, basis_taps):
    here = jnp.stack([lax.axis_index(axis) for axis in ("x", "core", "y", "z")]).astype(jnp.int32)
    given = (psf_index, coeff_table.T, basis_taps, patches.transpose(0, 2, 1), offsets.transpose(0, 2, 3, 1),
             image, variance)

    own = [blur_part(part, *given) for part in range(2)]
    left = [shift(a, "yx", 1) for a in own]
    right = [shift(a, "yx", -1) for a in own]
    far = [shift(left[0], "yx", 1), shift(right[1], "yx", -1)]
    held = place(here, own, [(0, 0), (1, 0)])
    held = place(here, (right[0], left[1]), [(0, 1), (1, -1)], held)
    held = place(here, (left[0], right[1]), [(0, -1), (1, 1)], held)
    far, held = lax.optimization_barrier((far, held))
    parts = place(here, far, [(0, 2), (1, 2)], held, last=True)

    stay, stay_cross, far_low, far_high, high, high_cross, low, low_cross, right_low, left_high = parts
    from_left, from_right = shift(far_low, "xy", 1), shift(far_high, "xy", -1)
    high, high_cross = shift(high, "xy", 1), shift(high_cross, "xy", 1, True)
    low, low_cross = shift(low, "xy", -1), shift(low_cross, "xy", -1, True)
    stay_cross = lax.ppermute(stay_cross, "core", [(0, 1), (1, 0)])
    last = add_received(right_low, from_left, left_high, from_right)
    same_low, cross_low = shift(last[0], "xy", 1), shift(last[1], "xy", 1, True)
    same_high, cross_high = shift(last[2], "xy", -1), shift(last[3], "xy", -1, True)
    stay, *sent, four_low, four_high = join(here, stay, stay_cross, low, same_low, high, same_high,
                                            low_cross, cross_low, high_cross, cross_high)

    low, high = shift_z(four_low, 1), shift_z(four_high, -1)
    sent[2], sent[5] = relay(sent[2], sent[5], low, high)
    return finish(here, (stay, *(shift_z(part, steps) for part, steps in zip(sent, STEPS))))[None]


def solution(mesh):
    fine = Mesh(mesh.devices.reshape(NX, NZ, NC, NY), ("x", "z", "core", "y"))
    own = ("x", "z", "core")
    return jax.shard_map(
        body,
        mesh=fine,
        in_specs=(
            P("y", own, None, None),
            P("y", own, None, None),
            P("y", own, None),
            P("y", own, None, None),
            P("y", own),
            P(),
            P(),
        ),
        out_specs=P(own, "y", None),
        check_vma=False,
    )
```

time: 96.2 us -> 93.4 us (0.971); the launches traced: 94.5 us -> 93.1 us
  blocking collectives: 25.4 us -> 0 us
  starting transfers between devices: 15.1 us -> 33.4 us
  Pallas kernels: 20.3 us -> 24.3 us
  waiting for transfers between devices: 33.4 us -> 35.2 us
    all_to_all x1 -> x0, blocking collectives: 25.4 us -> none  [body(): got = lax.all_to_all(mine, 'z', 0, 0, tiled=True)]
    ppermute x1 -> x9, starting transfers between devices: 0.09 us -> 16.8 us  [the longest x8 16.8 us: shift_z(): return lax.ppermute(value, 'z', [(z, (z + by) % NZ) for z in range(NZ)])]
    ppermute x1 -> x9, waiting for transfers between devices: 1.94 us -> 7.9 us  [the longest x8 7.9 us: shift_z(): return lax.ppermute(value, 'z', [(z, (z + by) % NZ) for z in range(NZ)])]
    ppermute x12 -> x16, waiting for transfers between devices: 31.4 us -> 27.3 us  [shift(): return lax.ppermute(value, ('x', 'core', 'y'), pairs)]
    pallas_call x5 -> x8, Pallas kernels: 17.6 us -> 21.6 us  [the longest x4 14.6 us: place(): pl.pallas_call(functools.partial(place_kernel, tuple(runs), bool(old), la...]
    ppermute x12 -> x16, starting transfers between devices: 15.1 us -> 16.6 us  [shift(): return lax.ppermute(value, ('x', 'core', 'y'), pairs)]
  transfers between devices with their start and end apart: 13 -> 25, of which waited for: 10 -> 13; matrix products, arithmetic and copies ran while one was open for 0% -> 0% of each run, Pallas kernels for 11% -> 15%
where the time goes in v4:
time: 93.4 us; the launch traced here: 93.1 us
  waiting for transfers between devices  35.2 us (38%)
  starting transfers between devices  33.4 us (36%)
  Pallas kernels  24.3 us (26%)
    ppermute x16, waiting for transfers between devices, shift(): return lax.ppermute(value, ('x', 'core', 'y'), pairs)  27.3 us
    ppermute x8, starting transfers between devices, shift_z(): return lax.ppermute(value, 'z', [(z, (z + by) % NZ) for z in range(NZ)])  16.8 us
    ppermute x16, starting transfers between devices, shift(): return lax.ppermute(value, ('x', 'core', 'y'), pairs)  16.6 us
    pallas_call x4, Pallas kernels, place(): pl.pallas_call(functools.partial(place_kernel, tuple(runs), bool(old), la...  14.6 us
    ppermute x8, waiting for transfers between devices, shift_z(): return lax.ppermute(value, 'z', [(z, (z + by) % NZ) for z in range(NZ)])  7.9 us
    pallas_call x2, Pallas kernels, blur_part(): pl.pallas_call(functools.partial(blur_kernel, first, tiles), grid=(1,), i...  6.92 us
    pallas_call x1, Pallas kernels, finish(): pl.pallas_call(finish_kernel, in_specs=[pl.BlockSpec(memory_space=pltpu.S...  1.91 us
  transfers between devices with their start and end apart: 25, of which 13 were waited for; matrix products, arithmetic and copies ran while one was open for 0% of the time, Pallas kernels for 15%

profile of v4, /device:TPU:62, one launch (start us, length us, event | category | flops | bytes accessed | tf_op | source)
XLA Modules:
  0.0 93.1 jit_solution(5078230309585006820)
XLA Ops:
  0.0 3.5 %blur_part.2.refs_0_ = f32[1544,128]{1,0:T(8,128)S(1)} custom-call(s32[1,24]{1,0:T(1,128)} %psf_ref.3, f32[3,16]{1,0:T(4,128)} %bitcast.8, f32[3,2,21]{2,1,0:T(2,128)} %taps_ref.3, s32[1,2,24]{2,1,0:T(2,128)} %bitcast.12, s32[1,2,2,24]{3,2,1,0:T(2,128)} %bitcast.10, f32[1,24,128,128]{3,2,1,0:T(8,128)} %img_ref.3, f32[1,24,128,128]{3,2,1,0:T(8,128)} %var_ref.3), custom_call_target="tpu_custom_call" | custom-call | flops 912000000 | bytes 2359296 | tf_op jit(solution)/shard_map/blur_part/pallas_call | solution.py:105
  3.5 0.3 collective-permute-start
  3.8 3.5 %blur_part.3.refs_1_ = f32[1544,128]{1,0:T(8,128)S(1)} custom-call(s32[1,24]{1,0:T(1,128)} %psf_ref.3, f32[3,16]{1,0:T(4,128)} %bitcast.9, f32[3,2,21]{2,1,0:T(2,128)} %taps_ref.3, s32[1,2,24]{2,1,0:T(2,128)} %bitcast.13, s32[1,2,2,24]{3,2,1,0:T(2,128)} %bitcast.11, f32[1,24,128,128]{3,2,1,0:T(8,128)} %img_ref.3, f32[1,24,128,128]{3,2,1,0:T(8,128)} %var_ref.3), custom_call_target="tpu_custom_call" | custom-call | flops 912000000 | bytes 2359296 | tf_op jit(solution)/shard_map/blur_part/pallas_call | solution.py:105
  7.2 1.9 %collective-permute-start.2 = (f32[1544,128]{1,0:T(8,128)S(1)}, f32[1544,128]{1,0:T(8,128)}, u32[]{:S(2)}, u32[]{:S(2)}) collective-permute-start(f32[1544,128]{1,0:T(8,128)S(1)} %blur_part.3.refs_1_), channel_id=1, source_target_pairs={{0,3},{1,0},{2,1},{3,2},{4,196},{5,197},{6,198},{7,199},{64,67},{6... | collective-permute-start | bytes 2371592 | tf_op jit(solution)/shard_map/ppermute | solution.py:421
  9.1 0.7 collective-permute-start.4
  9.9 2.5 %collective-permute-start.5 = (f32[1544,128]{1,0:T(8,128)S(1)}, f32[1544,128]{1,0:T(8,128)}, u32[]{:S(2)}, u32[]{:S(2)}) collective-permute-start(f32[1544,128]{1,0:T(8,128)S(1)} %blur_part.3.refs_1_), channel_id=1, source_target_pairs={{0,1},{1,2},{2,3},{3,0},{4,68},{5,69},{6,70},{7,71},{64,65},{65,66... | collective-permute-start | bytes 2371592 | tf_op jit(solution)/shard_map/ppermute | solution.py:421
  12.3 3.2 %collective-permute-done.refs_0_ = f32[1544,128]{1,0:T(8,128)S(1)} collective-permute-done((f32[1544,128]{1,0:T(8,128)S(1)}, f32[1544,128]{1,0:T(8,128)S(1)}, u32[]{:S(2)}, u32[]{:S(2)}) %collective-permute-start) | collective-permute-done | bytes 790560 | tf_op jit(solution)/shard_map/ppermute | solution.py:421
  15.6 1.4 %collective-permute-start.1 = (f32[1544,128]{1,0:T(8,128)S(1)}, f32[1544,128]{1,0:T(8,128)S(1)}, u32[]{:S(2)}, u32[]{:S(2)}) collective-permute-start(f32[1544,128]{1,0:T(8,128)S(1)} %collective-permute-done.refs_0_), channel_id=1, source_target_pairs={{0,1},{1,2},{2,3},{3,0},{4,68},{5,69},{6,70},{7,71},{64,65},{65,66... | collective-permute-start | bytes 2371592 | tf_op jit(solution)/shard_map/ppermute | solution.py:421
  17.0 3.6 %collective-permute-done.2.refs_1_ = f32[1544,128]{1,0:T(8,128)} collective-permute-done((f32[1544,128]{1,0:T(8,128)S(1)}, f32[1544,128]{1,0:T(8,128)}, u32[]{:S(2)}, u32[]{:S(2)}) %collective-permute-start.2) | collective-permute-done | bytes 790560 | tf_op jit(solution)/shard_map/ppermute | solution.py:421
  20.7 0.6 collective-permute-start.3
  21.3 0.1 pad_add_fusion.here_ref
  21.3 3.0 %place.4 = (f32[64,2,64,128]{3,2,1,0:T(8,128)S(1)}, f32[64,128]{1,0:T(8,128)S(1)}) custom-call(s32[4]{0:T(128)S(1)} %pad_add_fusion.here_ref, f32[1544,128]{1,0:T(8,128)S(1)} %blur_part.2.refs_0_, f32[1544,128]{1,0:T(8,128)S(1)} %blur_part.3.refs_1_), custom_call_target="tpu_custom_call" | custom-call | flops 1000000 | bytes 22140000 | tf_op jit(solution)/shard_map/place/pallas_call | solution.py:257
  24.3 4.8 %collective-permute-done.4.refs_0_ = f32[1544,128]{1,0:T(8,128)} collective-permute-done((f32[1544,128]{1,0:T(8,128)S(1)}, f32[1544,128]{1,0:T(8,128)}, u32[]{:S(2)}, u32[]{:S(2)}) %collective-permute-start.4) | collective-permute-done | bytes 790560 | tf_op jit(solution)/shard_map/ppermute | solution.py:421
  29.1 0.0 collective-permute-done.5.refs_1_
  29.1 3.8 %place.5 = (f32[64,2,64,128]{3,2,1,0:T(8,128)S(1)}, f32[64,128]{1,0:T(8,128)S(1)}) custom-call(s32[4]{0:T(128)S(1)} %pad_add_fusion.here_ref, f32[1544,128]{1,0:T(8,128)} %collective-permute-done.4.refs_0_, f32[1544,128]{1,0:T(8,128)} %collective-permute-done.5.refs_1_, f32[64,2,64,128]{3,2,1,0:T(8,128)S(1)} %get-tuple-element.40.refs_2_, ...), custom_call_target="tpu_custom_call" | custom-call | flops 1000000 | bytes 22140000 | tf_op jit(solution)/shard_map/place/pallas_call | solution.py:257
  33.0 3.7 %place.6 = (f32[64,2,64,128]{3,2,1,0:T(8,128)S(1)}, f32[64,128]{1,0:T(8,128)S(1)}) custom-call(s32[4]{0:T(128)S(1)} %pad_add_fusion.here_ref, f32[1544,128]{1,0:T(8,128)S(1)} %collective-permute-done.refs_0_, f32[1544,128]{1,0:T(8,128)} %collective-permute-done.2.refs_1_, f32[64,2,64,128]{3,2,1,0:T(8,128)S(1)} %get-tuple-element.42.refs_2_, ...), custom_call_target="tpu_custom_call" | custom-call | flops 1000000 | bytes 22140000 | tf_op jit(solution)/shard_map/place/pallas_call | solution.py:257
  36.7 0.9 %collective-permute-done.3.refs_1_ = f32[1544,128]{1,0:T(8,128)} collective-permute-done((f32[1544,128]{1,0:T(8,128)}, f32[1544,128]{1,0:T(8,128)}, u32[]{:S(2)}, u32[]{:S(2)}) %collective-permute-start.3) | collective-permute-done | bytes 790560 | tf_op jit(solution)/shard_map/ppermute | solution.py:421
  37.6 4.1 %place.7 = (f32[1032,128]{1,0:T(8,128)S(1)}, f32[1032,128]{1,0:T(8,128)S(1)}, f32[1032,128]{1,0:T(8,128)S(1)}, f32[1032,128]{1,0:T(8,128)S(1)}, f32[520,128]{1,0...) custom-call(s32[4]{0:T(128)S(1)} %pad_add_fusion.here_ref, ...), custom_call_target="tpu_custom_call" | custom-call | flops 1000000 | bytes 22140000 | tf_op jit(solution)/shard_map/place/pallas_call | solution.py:257
  41.7 0.6 collective-permute-start.8
  42.3 1.5 %collective-permute-start.9 = (f32[1032,128]{1,0:T(8,128)S(1)}, f32[1032,128]{1,0:T(8,128)S(1)}, u32[]{:S(2)}, u32[]{:S(2)}) collective-permute-start(f32[1032,128]{1,0:T(8,128)S(1)} %get-tuple-element.56), channel_id=1, source_target_pairs={{0,192},{1,193},{2,194},{3,195},{4,7},{5,4},{6,5},{7,6},{64,0},{65... | collective-permute-start | bytes 1585160 | tf_op jit(solution)/shard_map/ppermute | solution.py:421
  43.8 1.7 %collective-permute-start.11 = (f32[520,128]{1,0:T(8,128)S(1)}, f32[520,128]{1,0:T(8,128)S(1)}, u32[]{:S(2)}, u32[]{:S(2)}) collective-permute-start(f32[520,128]{1,0:T(8,128)S(1)} %get-tuple-element.58), channel_id=1, source_target_pairs={{0,64},{1,65},{2,66},{3,67},{4,5},{5,6},{6,7},{7,4},{64,128},{65,1... | collective-permute-start | bytes 798728 | tf_op jit(solution)/shard_map/ppermute | solution.py:421
  45.5 0.0 collective-permute-start.13
  45.5 0.6 collective-permute-start.15
  46.1 4.9 %collective-permute-done.8.b = f32[1032,128]{1,0:T(8,128)S(1)} collective-permute-done((f32[1032,128]{1,0:T(8,128)S(1)}, f32[1032,128]{1,0:T(8,128)S(1)}, u32[]{:S(2)}, u32[]{:S(2)}) %collective-permute-start.8) | collective-permute-done | bytes 528416 | tf_op jit(solution)/shard_map/ppermute | solution.py:421
  51.0 0.8 collective-permute-start.7
  51.8 0.9 collective-permute-done.9.d
  52.7 0.1 add_received.1
  52.8 1.0 %collective-permute-done.11.refs_2_ = f32[520,128]{1,0:T(8,128)S(1)} collective-permute-done((f32[520,128]{1,0:T(8,128)S(1)}, f32[520,128]{1,0:T(8,128)S(1)}, u32[]{:S(2)}, u32[]{:S(2)}) %collective-permute-start.11) | collective-permute-done | bytes 266272 | tf_op jit(solution)/shard_map/ppermute | solution.py:421
  53.9 1.7 %collective-permute-start.10 = (f32[520,128]{1,0:T(8,128)S(1)}, f32[520,128]{1,0:T(8,128)S(1)}, u32[]{:S(2)}, u32[]{:S(2)}) collective-permute-start(f32[520,128]{1,0:T(8,128)S(1)} %get-tuple-element.57), channel_id=1, source_target_pairs={{0,64},{1,65},{2,66},{3,67},{4,5},{5,6},{6,7},{7,4},{64,128},{65,1... | collective-permute-start | bytes 798728 | tf_op jit(solution)/shard_map/ppermute | solution.py:421
  55.5 0.0 collective-permute-done.13.refs_4_
  55.5 0.3 collective-permute-start.12
  55.9 1.9 %collective-permute-start.14 = (f32[520,128]{1,0:T(8,128)S(1)}, f32[520,128]{1,0:T(8,128)S(1)}, u32[]{:S(2)}, u32[]{:S(2)}) collective-permute-start(f32[520,128]{1,0:T(8,128)S(1)} %get-tuple-element.61), channel_id=1, source_target_pairs={{0,68},{1,69},{2,70},{3,71},{4,1},{5,2},{6,3},{7,0},{64,132},{65,1... | collective-permute-start | bytes 798728 | tf_op jit(solution)/shard_map/ppermute | solution.py:421
  57.8 0.8 collective-permute-done.7.refs_0_
  58.6 1.6 %collective-permute-done.10.refs_1_ = f32[520,128]{1,0:T(8,128)S(1)} collective-permute-done((f32[520,128]{1,0:T(8,128)S(1)}, f32[520,128]{1,0:T(8,128)S(1)}, u32[]{:S(2)}, u32[]{:S(2)}) %collective-permute-start.10) | collective-permute-done | bytes 266272 | tf_op jit(solution)/shard_map/ppermute | solution.py:421
  60.3 2.9 %collective-permute-done.12.refs_3_ = f32[520,128]{1,0:T(8,128)S(1)} collective-permute-done((f32[520,128]{1,0:T(8,128)S(1)}, f32[520,128]{1,0:T(8,128)S(1)}, u32[]{:S(2)}, u32[]{:S(2)}) %collective-permute-start.12) | collective-permute-done | bytes 266272 | tf_op jit(solution)/shard_map/ppermute | solution.py:421
  63.2 2.5 %collective-permute-done.16.refs_7_ = f32[520,128]{1,0:T(8,128)S(1)} collective-permute-done((f32[520,128]{1,0:T(8,128)S(1)}, f32[520,128]{1,0:T(8,128)S(1)}, u32[]{:S(2)}, u32[]{:S(2)}) %collective-permute-start.16) | collective-permute-done | bytes 266272 | tf_op jit(solution)/shard_map/ppermute | solution.py:421
  65.7 0.8 join.1
  66.5 2.0 %collective-permute-start.17 = (f32[136,128]{1,0:T(8,128)S(1)}, f32[136,128]{1,0:T(8,128)S(1)}, u32[]{:S(2)}, u32[]{:S(2)}) collective-permute-start(f32[136,128]{1,0:T(8,128)S(1)} %get-tuple-element.65), channel_id=1, source_target_pairs={{0,8},{8,16},{16,24},{24,32},{32,40},{40,48},{48,56},{56,0},{1,9},... | collective-permute-start | bytes 208904 | tf_op jit(solution)/shard_map/ppermute | solution.py:409
  68.5 0.1 collective-permute-start.20
  68.6 1.9 %collective-permute-start.19 = (f32[64,128]{1,0:T(8,128)S(1)}, f32[64,128]{1,0:T(8,128)S(1)}, u32[]{:S(2)}, u32[]{:S(2)}) collective-permute-start(f32[64,128]{1,0:T(8,128)S(1)} %get-tuple-element.69), channel_id=1, source_target_pairs={{0,8},{8,16},{16,24},{24,32},{32,40},{40,48},{48,56},{56,0},{1,9},... | collective-permute-start | bytes 98312 | tf_op jit(solution)/shard_map/ppermute | solution.py:409
  70.5 5.7 %collective-permute-start.18 = (f32[136,128]{1,0:T(8,128)S(1)}, f32[136,128]{1,0:T(8,128)S(1)}, u32[]{:S(2)}, u32[]{:S(2)}) collective-permute-start(f32[136,128]{1,0:T(8,128)S(1)} %get-tuple-element.66), channel_id=1, source_target_pairs={{0,16},{8,24},{16,32},{24,40},{32,48},{40,56},{48,0},{56,8},{1,17}... | collective-permute-start | bytes 208904 | tf_op jit(solution)/shard_map/ppermute | solution.py:409
  76.2 0.0 collective-permute-start.22
  76.2 2.0 %collective-permute-start.23 = (f32[136,128]{1,0:T(8,128)S(1)}, f32[136,128]{1,0:T(8,128)S(1)}, u32[]{:S(2)}, u32[]{:S(2)}) collective-permute-start(f32[136,128]{1,0:T(8,128)S(1)} %get-tuple-element.73), channel_id=1, source_target_pairs={{0,48},{8,56},{16,0},{24,8},{32,16},{40,24},{48,32},{56,40},{1,49}... | collective-permute-start | bytes 208904 | tf_op jit(solution)/shard_map/ppermute | solution.py:409
  78.2 3.7 %collective-permute-start.21 = (f32[136,128]{1,0:T(8,128)S(1)}, f32[136,128]{1,0:T(8,128)S(1)}, u32[]{:S(2)}, u32[]{:S(2)}) collective-permute-start(f32[136,128]{1,0:T(8,128)S(1)} %get-tuple-element.71), channel_id=1, source_target_pairs={{0,24},{8,32},{16,40},{24,48},{32,56},{40,0},{48,8},{56,16},{1,25}... | collective-permute-start | bytes 208904 | tf_op jit(solution)/shard_map/ppermute | solution.py:409
  81.9 1.4 %collective-permute-start.24 = (f32[136,128]{1,0:T(8,128)S(1)}, f32[136,128]{1,0:T(8,128)S(1)}, u32[]{:S(2)}, u32[]{:S(2)}) collective-permute-start(f32[136,128]{1,0:T(8,128)S(1)} %get-tuple-element.74), channel_id=1, source_target_pairs={{0,40},{8,48},{16,56},{24,0},{32,8},{40,16},{48,24},{56,32},{1,41}... | collective-permute-start | bytes 208904 | tf_op jit(solution)/shard_map/ppermute | solution.py:409
  83.3 3.6 %collective-permute-done.21.refs_3_ = f32[136,128]{1,0:T(8,128)S(1)} collective-permute-done((f32[136,128]{1,0:T(8,128)S(1)}, f32[136,128]{1,0:T(8,128)S(1)}, u32[]{:S(2)}, u32[]{:S(2)}) %collective-permute-start.21) | collective-permute-done | bytes 69664 | tf_op jit(solution)/shard_map/ppermute | solution.py:409
  87.0 4.3 %collective-permute-done.24.refs_6_ = f32[136,128]{1,0:T(8,128)S(1)} collective-permute-done((f32[136,128]{1,0:T(8,128)S(1)}, f32[136,128]{1,0:T(8,128)S(1)}, u32[]{:S(2)}, u32[]{:S(2)}) %collective-permute-start.24) | collective-permute-done | bytes 69664 | tf_op jit(solution)/shard_map/ppermute | solution.py:409
  91.2 1.9 %finish.1 = f32[64,256]{1,0:T(8,128)} custom-call(s32[4]{0:T(128)S(1)} %pad_add_fusion.here_ref, f32[136,128]{1,0:T(8,128)S(1)} %get-tuple-element.64.refs_0_, f32[136,128]{1,0:T(8,128)S(1)} %collective-permute-done.17.refs_1_, f32[136,128]{1,0:T(8,128)S(1)} %collective-permute-done.18.refs_2_, f32[136,128]{1,0:T(8,128)S(1)} %collective-permute-done.21.refs_3_, ...), custom_call_target="tpu_custom_call" | custom-call | tf_op jit(solution)/shard_map/finish/pallas_call | solution.py:398
  (13 shorter events, 0.0 us)
Async XLA Ops:
  3.5 12.1 %collective-permute-start = (f32[1544,128]{1,0:T(8,128)S(1)}, f32[1544,128]{1,0:T(8,128)S(1)}, u32[]{:S(2)}, u32[]{:S(2)}) collective-permute-start(f32[1544,128]{1,0:T(8,128)S(1)} %blur_part.2.refs_0_), channel_id=1, source_target_pairs={{0,1},{1,2},{2,3},{3,0},{4,68},{5,69},{6,70},{7,71},{64,65},{65,66... | collective-permute-start | bytes 2371592 | tf_op jit(solution)/shard_map/ppermute | solution.py:421
  7.2 13.4 %collective-permute-start.2 = (f32[1544,128]{1,0:T(8,128)S(1)}, f32[1544,128]{1,0:T(8,128)}, u32[]{:S(2)}, u32[]{:S(2)}) collective-permute-start(f32[1544,128]{1,0:T(8,128)S(1)} %blur_part.3.refs_1_), channel_id=1, source_target_pairs={{0,3},{1,0},{2,1},{3,2},{4,196},{5,197},{6,198},{7,199},{64,67},{6... | collective-permute-start | bytes 2371592 | tf_op jit(solution)/shard_map/ppermute | solution.py:421
  9.1 20.0 %collective-permute-start.4 = (f32[1544,128]{1,0:T(8,128)S(1)}, f32[1544,128]{1,0:T(8,128)}, u32[]{:S(2)}, u32[]{:S(2)}) collective-permute-start(f32[1544,128]{1,0:T(8,128)S(1)} %blur_part.2.refs_0_), channel_id=1, source_target_pairs={{0,3},{1,0},{2,1},{3,2},{4,196},{5,197},{6,198},{7,199},{64,67},{6... | collective-permute-start | bytes 2371592 | tf_op jit(solution)/shard_map/ppermute | solution.py:421
  9.9 19.3 %collective-permute-start.5 = (f32[1544,128]{1,0:T(8,128)S(1)}, f32[1544,128]{1,0:T(8,128)}, u32[]{:S(2)}, u32[]{:S(2)}) collective-permute-start(f32[1544,128]{1,0:T(8,128)S(1)} %blur_part.3.refs_1_), channel_id=1, source_target_pairs={{0,1},{1,2},{2,3},{3,0},{4,68},{5,69},{6,70},{7,71},{64,65},{65,66... | collective-permute-start | bytes 2371592 | tf_op jit(solution)/shard_map/ppermute | solution.py:421
  15.6 21.1 %collective-permute-start.1 = (f32[1544,128]{1,0:T(8,128)S(1)}, f32[1544,128]{1,0:T(8,128)S(1)}, u32[]{:S(2)}, u32[]{:S(2)}) collective-permute-start(f32[1544,128]{1,0:T(8,128)S(1)} %collective-permute-done.refs_0_), channel_id=1, source_target_pairs={{0,1},{1,2},{2,3},{3,0},{4,68},{5,69},{6,70},{7,71},{64,65},{65,66... | collective-permute-start | bytes 2371592 | tf_op jit(solution)/shard_map/ppermute | solution.py:421
  20.7 16.9 %collective-permute-start.3 = (f32[1544,128]{1,0:T(8,128)}, f32[1544,128]{1,0:T(8,128)}, u32[]{:S(2)}, u32[]{:S(2)}) collective-permute-start(f32[1544,128]{1,0:T(8,128)} %collective-permute-done.2.refs_1_), channel_id=1, source_target_pairs={{0,3},{1,0},{2,1},{3,2},{4,196},{5,197},{6,198},{7,199},{64,67},{6... | collective-permute-start | bytes 2371592 | tf_op jit(solution)/shard_map/ppermute | solution.py:421
  41.7 9.3 %collective-permute-start.8 = (f32[1032,128]{1,0:T(8,128)S(1)}, f32[1032,128]{1,0:T(8,128)S(1)}, u32[]{:S(2)}, u32[]{:S(2)}) collective-permute-start(f32[1032,128]{1,0:T(8,128)S(1)} %get-tuple-element.54), channel_id=1, source_target_pairs={{0,64},{1,65},{2,66},{3,67},{4,5},{5,6},{6,7},{7,4},{64,128},{65,1... | collective-permute-start | bytes 1585160 | tf_op jit(solution)/shard_map/ppermute | solution.py:421
  42.3 10.4 %collective-permute-start.9 = (f32[1032,128]{1,0:T(8,128)S(1)}, f32[1032,128]{1,0:T(8,128)S(1)}, u32[]{:S(2)}, u32[]{:S(2)}) collective-permute-start(f32[1032,128]{1,0:T(8,128)S(1)} %get-tuple-element.56), channel_id=1, source_target_pairs={{0,192},{1,193},{2,194},{3,195},{4,7},{5,4},{6,5},{7,6},{64,0},{65... | collective-permute-start | bytes 1585160 | tf_op jit(solution)/shard_map/ppermute | solution.py:421
  43.8 10.1 %collective-permute-start.11 = (f32[520,128]{1,0:T(8,128)S(1)}, f32[520,128]{1,0:T(8,128)S(1)}, u32[]{:S(2)}, u32[]{:S(2)}) collective-permute-start(f32[520,128]{1,0:T(8,128)S(1)} %get-tuple-element.58), channel_id=1, source_target_pairs={{0,64},{1,65},{2,66},{3,67},{4,5},{5,6},{6,7},{7,4},{64,128},{65,1... | collective-permute-start | bytes 798728 | tf_op jit(solution)/shard_map/ppermute | solution.py:421
  45.5 10.1 %collective-permute-start.13 = (f32[520,128]{1,0:T(8,128)S(1)}, f32[520,128]{1,0:T(8,128)S(1)}, u32[]{:S(2)}, u32[]{:S(2)}) collective-permute-start(f32[520,128]{1,0:T(8,128)S(1)} %get-tuple-element.60), channel_id=1, source_target_pairs={{0,196},{1,197},{2,198},{3,199},{4,3},{5,0},{6,1},{7,2},{64,4},{65... | collective-permute-start | bytes 798728 | tf_op jit(solution)/shard_map/ppermute | solution.py:421
  45.5 10.4 %collective-permute-start.15 = (f32[520,128]{1,0:T(8,128)S(1)}, f32[520,128]{1,0:T(8,128)S(1)}, u32[]{:S(2)}, u32[]{:S(2)}) collective-permute-start(f32[520,128]{1,0:T(8,128)S(1)} %get-tuple-element.62), channel_id=1, source_target_pairs={{0,68},{1,69},{2,70},{3,71},{4,1},{5,2},{6,3},{7,0},{64,132},{65,1... | collective-permute-start | bytes 798728 | tf_op jit(solution)/shard_map/ppermute | solution.py:421
  51.0 7.6 %collective-permute-start.7 = (f32[520,128]{1,0:T(8,128)S(1)}, f32[520,128]{1,0:T(8,128)S(1)}, u32[]{:S(2)}, u32[]{:S(2)}) collective-permute-start(f32[520,128]{1,0:T(8,128)S(1)} %get-tuple-element.52), channel_id=1, source_target_pairs={{0,192},{1,193},{2,194},{3,195},{4,7},{5,4},{6,5},{7,6},{64,0},{65... | collective-permute-start | bytes 798728 | tf_op jit(solution)/shard_map/ppermute | solution.py:421
  52.7 5.9 %collective-permute-start.6 = (f32[1032,128]{1,0:T(8,128)S(1)}, f32[1032,128]{1,0:T(8,128)S(1)}, u32[]{:S(2)}, u32[]{:S(2)}) collective-permute-start(f32[1032,128]{1,0:T(8,128)S(1)} %get-tuple-element.51), channel_id=1, source_target_pairs={{0,4},{4,0},{1,5},{5,1},{2,6},{6,2},{3,7},{7,3},{8,12},{12,8},{9,1... | collective-permute-start | bytes 1585160 | tf_op jit(solution)/shard_map/ppermute | solution.py:443
  53.9 6.4 %collective-permute-start.10 = (f32[520,128]{1,0:T(8,128)S(1)}, f32[520,128]{1,0:T(8,128)S(1)}, u32[]{:S(2)}, u32[]{:S(2)}) collective-permute-start(f32[520,128]{1,0:T(8,128)S(1)} %get-tuple-element.57), channel_id=1, source_target_pairs={{0,64},{1,65},{2,66},{3,67},{4,5},{5,6},{6,7},{7,4},{64,128},{65,1... | collective-permute-start | bytes 798728 | tf_op jit(solution)/shard_map/ppermute | solution.py:421
  55.5 7.6 %collective-permute-start.12 = (f32[520,128]{1,0:T(8,128)S(1)}, f32[520,128]{1,0:T(8,128)S(1)}, u32[]{:S(2)}, u32[]{:S(2)}) collective-permute-start(f32[520,128]{1,0:T(8,128)S(1)} %get-tuple-element.59), channel_id=1, source_target_pairs={{0,192},{1,193},{2,194},{3,195},{4,7},{5,4},{6,5},{7,6},{64,0},{65... | collective-permute-start | bytes 798728 | tf_op jit(solution)/shard_map/ppermute | solution.py:421
  55.9 7.3 %collective-permute-start.14 = (f32[520,128]{1,0:T(8,128)S(1)}, f32[520,128]{1,0:T(8,128)S(1)}, u32[]{:S(2)}, u32[]{:S(2)}) collective-permute-start(f32[520,128]{1,0:T(8,128)S(1)} %get-tuple-element.61), channel_id=1, source_target_pairs={{0,68},{1,69},{2,70},{3,71},{4,1},{5,2},{6,3},{7,0},{64,132},{65,1... | collective-permute-start | bytes 798728 | tf_op jit(solution)/shard_map/ppermute | solution.py:421
  58.6 7.1 %collective-permute-start.16 = (f32[520,128]{1,0:T(8,128)S(1)}, f32[520,128]{1,0:T(8,128)S(1)}, u32[]{:S(2)}, u32[]{:S(2)}) collective-permute-start(f32[520,128]{1,0:T(8,128)S(1)} %get-tuple-element.63), channel_id=1, source_target_pairs={{0,196},{1,197},{2,198},{3,199},{4,3},{5,0},{6,1},{7,2},{64,4},{65... | collective-permute-start | bytes 798728 | tf_op jit(solution)/shard_map/ppermute | solution.py:421
  66.5 15.4 %collective-permute-start.17 = (f32[136,128]{1,0:T(8,128)S(1)}, f32[136,128]{1,0:T(8,128)S(1)}, u32[]{:S(2)}, u32[]{:S(2)}) collective-permute-start(f32[136,128]{1,0:T(8,128)S(1)} %get-tuple-element.65), channel_id=1, source_target_pairs={{0,8},{8,16},{16,24},{24,32},{32,40},{40,48},{48,56},{56,0},{1,9},... | collective-permute-start | bytes 208904 | tf_op jit(solution)/shard_map/ppermute | solution.py:409
  68.5 9.7 %collective-permute-start.20 = (f32[72,128]{1,0:T(8,128)S(1)}, f32[72,128]{1,0:T(8,128)S(1)}, u32[]{:S(2)}, u32[]{:S(2)}) collective-permute-start(f32[72,128]{1,0:T(8,128)S(1)} %get-tuple-element.70), channel_id=1, source_target_pairs={{0,56},{8,0},{16,8},{24,16},{32,24},{40,32},{48,40},{56,48},{1,57}... | collective-permute-start | bytes 110600 | tf_op jit(solution)/shard_map/ppermute | solution.py:409
  68.6 7.6 %collective-permute-start.19 = (f32[64,128]{1,0:T(8,128)S(1)}, f32[64,128]{1,0:T(8,128)S(1)}, u32[]{:S(2)}, u32[]{:S(2)}) collective-permute-start(f32[64,128]{1,0:T(8,128)S(1)} %get-tuple-element.69), channel_id=1, source_target_pairs={{0,8},{8,16},{16,24},{24,32},{32,40},{40,48},{48,56},{56,0},{1,9},... | collective-permute-start | bytes 98312 | tf_op jit(solution)/shard_map/ppermute | solution.py:409
  70.5 12.8 %collective-permute-start.18 = (f32[136,128]{1,0:T(8,128)S(1)}, f32[136,128]{1,0:T(8,128)S(1)}, u32[]{:S(2)}, u32[]{:S(2)}) collective-permute-start(f32[136,128]{1,0:T(8,128)S(1)} %get-tuple-element.66), channel_id=1, source_target_pairs={{0,16},{8,24},{16,32},{24,40},{32,48},{40,56},{48,0},{56,8},{1,17}... | collective-permute-start | bytes 208904 | tf_op jit(solution)/shard_map/ppermute | solution.py:409
  76.2 7.1 %collective-permute-start.22 = (f32[136,128]{1,0:T(8,128)S(1)}, f32[136,128]{1,0:T(8,128)S(1)}, u32[]{:S(2)}, u32[]{:S(2)}) collective-permute-start(f32[136,128]{1,0:T(8,128)S(1)} %get-tuple-element.72), channel_id=1, source_target_pairs={{0,56},{8,0},{16,8},{24,16},{32,24},{40,32},{48,40},{56,48},{1,57}... | collective-permute-start | bytes 208904 | tf_op jit(solution)/shard_map/ppermute | solution.py:409
  76.2 7.1 %collective-permute-start.23 = (f32[136,128]{1,0:T(8,128)S(1)}, f32[136,128]{1,0:T(8,128)S(1)}, u32[]{:S(2)}, u32[]{:S(2)}) collective-permute-start(f32[136,128]{1,0:T(8,128)S(1)} %get-tuple-element.73), channel_id=1, source_target_pairs={{0,48},{8,56},{16,0},{24,8},{32,16},{40,24},{48,32},{56,40},{1,49}... | collective-permute-start | bytes 208904 | tf_op jit(solution)/shard_map/ppermute | solution.py:409
  78.2 8.8 %collective-permute-start.21 = (f32[136,128]{1,0:T(8,128)S(1)}, f32[136,128]{1,0:T(8,128)S(1)}, u32[]{:S(2)}, u32[]{:S(2)}) collective-permute-start(f32[136,128]{1,0:T(8,128)S(1)} %get-tuple-element.71), channel_id=1, source_target_pairs={{0,24},{8,32},{16,40},{24,48},{32,56},{40,0},{48,8},{56,16},{1,25}... | collective-permute-start | bytes 208904 | tf_op jit(solution)/shard_map/ppermute | solution.py:409
  81.9 9.3 %collective-permute-start.24 = (f32[136,128]{1,0:T(8,128)S(1)}, f32[136,128]{1,0:T(8,128)S(1)}, u32[]{:S(2)}, u32[]{:S(2)}) collective-permute-start(f32[136,128]{1,0:T(8,128)S(1)} %get-tuple-element.74), channel_id=1, source_target_pairs={{0,40},{8,48},{16,56},{24,0},{32,8},{40,16},{48,24},{56,32},{1,41}... | collective-permute-start | bytes 208904 | tf_op jit(solution)/shard_map/ppermute | solution.py:409

commit v5 on v4

--- a/solution.py
+++ b/solution.py
@@ -17,7 +17,7 @@
 RING = 4
 STRIP = PATCH_PIX // NY
 TILES = 24
-PARTS = ((0, 12), (12, 12))
+HALF = 12
 UNROLL = 3
 META = 8
 PATCH, ROW, COL, RANK, WEIGHT = range(5)
@@ -42,78 +42,84 @@
     return jnp.dot(a, b, preferred_element_type=F32)
 
 
-def blur_kernel(first, tiles, psf_ref, table_ref, taps_ref, patch_ref, offset_ref, img_ref, var_ref, out_ref,
-                col_hi, col_lo, rows):
-    major = lax.broadcasted_iota(jnp.int32, (PIX, PIX), 0)
-    minor = lax.broadcasted_iota(jnp.int32, (PIX, PIX), 1)
-    for b in range(NB):
-        lanes = slice(b * PIX, (b + 1) * PIX)
-        for axis, diff in ((0, minor - major), (1, major - minor)):
-            band = jnp.zeros((PIX, PIX), F32)
-            for t in range(TAPS):
-                band = jnp.where(diff == t - MARGIN, taps_ref[b, axis, t], band)
-            hi, lo = split(band)
-            if axis:
-                col_hi[:PIX, lanes], col_hi[PIX:, lanes], col_lo[:, lanes] = hi, hi, lo
-            else:
-                rows[:PIX, lanes], rows[PIX:, lanes] = hi, lo
-
-    x_hi, x_lo = split(img_ref[0].reshape(tiles * PIX, PIX))
-    smooth = dot(jnp.concatenate([x_hi, x_lo], axis=1), col_hi[...]) + dot(x_hi, col_lo[...])
-    weights = []
-    for n in range(tiles):
-        total = jnp.sum(jnp.sum(var_ref[0, n], axis=0, keepdims=True), axis=1, keepdims=True)
-        weights.append(1.0 / (total * (1.0 / (PIX * PIX))))
-    for pair in range(tiles // 2):
-        sides = []
-        for n in (2 * pair, 2 * pair + 1):
-            row = psf_ref[0, first + n]
-            sides.append(jnp.concatenate(
-                [smooth[n * PIX:(n + 1) * PIX, b * PIX:(b + 1) * PIX] * (table_ref[b, row] * weights[n])
-                 for b in range(NB)], axis=0))
-        q_hi, q_lo = split(jnp.concatenate(sides, axis=1))
-        both = dot(rows[...], q_hi)
-        done = both[:PIX] + (both[PIX:] + dot(rows[:PIX], q_lo))
-        for n in range(2):
-            at = META + (2 * pair + n) * PIX
-            out_ref[at:at + PIX, :] = done[:, n * PIX:(n + 1) * PIX]
-
-    lane = lax.broadcasted_iota(jnp.int32, (META, PIX), 1)
-    kind = lax.broadcasted_iota(jnp.int32, (META, PIX), 0)
-    patch, facts = jnp.zeros((META, PIX), jnp.int32), jnp.zeros((META, PIX), jnp.int32)
-    for t in range(TILES):
-        for k in range(2):
-            here = lane == 2 * t + k
-            patch = jnp.where(here, patch_ref[0, k, t], patch)
-            place = jnp.where(kind == ROW, offset_ref[0, k, 0, t], offset_ref[0, k, 1, t])
-            facts = jnp.where(here, place, facts)
-    rank = jnp.zeros((META, PIX), jnp.int32)
-    for t in range(TILES):
-        for k in range(2):
-            rank += jnp.where((patch == patch_ref[0, k, t]) & (lane > 2 * t + k), 1, 0)
-    facts = jnp.where(kind == PATCH, patch, jnp.where(kind == RANK, rank, facts)).astype(F32)
-    for n in range(tiles):
-        facts = jnp.where((kind == WEIGHT) & ((lane >> 1) == first + n), weights[n], facts)
-    out_ref[0:META, :] = facts
-
-
-def blur_part(part, psf_index, table, taps, patches, offsets, image, variance):
-    first, tiles = PARTS[part]
+def blur_kernel(psf_ref, table_ref, taps_ref, patch_ref, offset_ref, img_ref, var_ref, *refs):
+    *outs, col_hi, col_lo, rows = refs
+
+    @pl.when(pl.program_id(0) == 0)
+    def _():
+        major = lax.broadcasted_iota(jnp.int32, (PIX, PIX), 0)
+        minor = lax.broadcasted_iota(jnp.int32, (PIX, PIX), 1)
+        for b in range(NB):
+            lanes = slice(b * PIX, (b + 1) * PIX)
+            for axis, diff in ((0, minor - major), (1, major - minor)):
+                band = jnp.zeros((PIX, PIX), F32)
+                for t in range(TAPS):
+                    band = jnp.where(diff == t - MARGIN, taps_ref[b, axis, t], band)
+                hi, lo = split(band)
+                if axis:
+                    col_hi[:PIX, lanes], col_hi[PIX:, lanes], col_lo[:, lanes] = hi, hi, lo
+                else:
+                    rows[:PIX, lanes], rows[PIX:, lanes] = hi, lo
+
+    def blur(first, out_ref):
+        x_hi, x_lo = split(img_ref[0].reshape(HALF * PIX, PIX))
+        smooth = dot(jnp.concatenate([x_hi, x_lo], axis=1), col_hi[...]) + dot(x_hi, col_lo[...])
+        weights = []
+        for n in range(HALF):
+            total = jnp.sum(jnp.sum(var_ref[0, n], axis=0, keepdims=True), axis=1, keepdims=True)
+            weights.append(1.0 / (total * (1.0 / (PIX * PIX))))
+        for pair in range(HALF // 2):
+            sides = []
+            for n in (2 * pair, 2 * pair + 1):
+                row = psf_ref[0, first + n]
+                sides.append(jnp.concatenate(
+                    [smooth[n * PIX:(n + 1) * PIX, b * PIX:(b + 1) * PIX] * (table_ref[b, row] * weights[n])
+                     for b in range(NB)], axis=0))
+            q_hi, q_lo = split(jnp.concatenate(sides, axis=1))
+            both = dot(rows[...], q_hi)
+            done = both[:PIX] + (both[PIX:] + dot(rows[:PIX], q_lo))
+            for n in range(2):
+                at = META + (2 * pair + n) * PIX
+                out_ref[at:at + PIX, :] = done[:, n * PIX:(n + 1) * PIX]
+
+        lane = lax.broadcasted_iota(jnp.int32, (META, PIX), 1)
+        kind = lax.broadcasted_iota(jnp.int32, (META, PIX), 0)
+        patch, facts = jnp.zeros((META, PIX), jnp.int32), jnp.zeros((META, PIX), jnp.int32)
+        for t in range(TILES):
+            for k in range(2):
+                here = lane == 2 * t + k
+                patch = jnp.where(here, patch_ref[0, k, t], patch)
+                place = jnp.where(kind == ROW, offset_ref[0, k, 0, t], offset_ref[0, k, 1, t])
+                facts = jnp.where(here, place, facts)
+        rank = jnp.zeros((META, PIX), jnp.int32)
+        for t in range(TILES):
+            for k in range(2):
+                rank += jnp.where((patch == patch_ref[0, k, t]) & (lane > 2 * t + k), 1, 0)
+        facts = jnp.where(kind == PATCH, patch, jnp.where(kind == RANK, rank, facts)).astype(F32)
+        for n in range(HALF):
+            facts = jnp.where((kind == WEIGHT) & ((lane >> 1) == first + n), weights[n], facts)
+        out_ref[0:META, :] = facts
+
+    for part, out in enumerate(outs):
+        pl.when(pl.program_id(0) == part)(functools.partial(blur, part * HALF, out))
+
+
+def blur_tiles(psf_index, table, taps, patches, offsets, image, variance):
     smem = pl.BlockSpec(memory_space=pltpu.SMEM)
-    block = pl.BlockSpec((1, tiles, PIX, PIX), lambda i: (0, first // tiles, 0, 0))
-    rows = META + tiles * PIX
-    return pl.pallas_call(
-        functools.partial(blur_kernel, first, tiles),
-        grid=(1,),
+    block = pl.BlockSpec((1, HALF, PIX, PIX), lambda i: (0, i, 0, 0))
+    rows = META + HALF * PIX
+    return pl.pallas_call(
+        blur_kernel,
+        grid=(TILES // HALF,),
         in_specs=[smem] * 5 + [block, block],
-        out_specs=pl.BlockSpec((rows, PIX), lambda i: (0, 0)),
-        out_shape=pltpu.VMEM((rows, PIX), F32),
+        out_specs=[pl.BlockSpec((rows, PIX), lambda i: (0, 0))] * 2,
+        out_shape=[pltpu.VMEM((rows, PIX), F32)] * 2,
         scratch_shapes=[pltpu.VMEM((2 * PIX, NB * PIX), BF16), pltpu.VMEM((PIX, NB * PIX), BF16),
                         pltpu.VMEM((2 * PIX, NB * PIX), BF16)],
         compiler_params=pltpu.CompilerParams(vmem_limit_bytes=BLUR_LIMIT),
-        cost_estimate=pl.CostEstimate(flops=tiles * 76 * 10**6, bytes_accessed=tiles * 3 * 65536,
+        cost_estimate=pl.CostEstimate(flops=TILES * 76 * 10**6, bytes_accessed=TILES * 3 * 65536,
                                       transcendentals=0),
-        name="blur_part",
+        name="blur_tiles",
     )(psf_index, table, taps, patches, offsets, image, variance)
 
 
@@ -221,7 +227,7 @@
         add(items)
         return number
 
-    given = [(PARTS[part][1] // UNROLL, dict(index=n, pair=2 * PARTS[part][0], base=starts[n], steps=steps))
+    given = [(HALF // UNROLL, dict(index=n, pair=2 * HALF * part, base=starts[n], steps=steps))
              for n, (part, steps) in enumerate(runs)]
 
     @pl.when(core == 0)
@@ -426,7 +432,7 @@
     given = (psf_index, coeff_table.T, basis_taps, patches.transpose(0, 2, 1), offsets.transpose(0, 2, 3, 1),
              image, variance)
 
-    own = [blur_part(part, *given) for part in range(2)]
+    own = blur_tiles(*given)
     left = [shift(a, "yx", 1) for a in own]
     right = [shift(a, "yx", -1) for a in own]
     far = [shift(left[0], "yx", 1), shift(right[1], "yx", -1)]

time: 93.4 us -> 91.9 us (0.984)
  Pallas kernels: 24.3 us -> 23.1 us
    pallas_call x2 -> x1, Pallas kernels: 6.92 us -> 6.28 us  [blur_tiles(): pl.pallas_call(blur_kernel, grid=(TILES // HALF,), in_specs=[smem] * 5 +...]
  transfers between devices with their start and end apart: 25 -> 25, of which waited for: 13 -> 13; matrix products, arithmetic and copies ran while one was open for 0% -> 0% of each run, Pallas kernels for 15% -> 12%
where the time goes in v5:
time: 91.9 us; the launch traced here: 91.8 us
  waiting for transfers between devices  35 us (38%)
  starting transfers between devices  33.4 us (36%)
  Pallas kernels  23.1 us (25%)
    ppermute x16, waiting for transfers between devices, shift(): return lax.ppermute(value, ('x', 'core', 'y'), pairs)  27.1 us
    ppermute x8, starting transfers between devices, shift_z(): return lax.ppermute(value, 'z', [(z, (z + by) % NZ) for z in range(NZ)])  16.8 us
    ppermute x16, starting transfers between devices, shift(): return lax.ppermute(value, ('x', 'core', 'y'), pairs)  16.6 us
    pallas_call x4, Pallas kernels, place(): pl.pallas_call(functools.partial(place_kernel, tuple(runs), bool(old), la...  14 us
    ppermute x8, waiting for transfers between devices, shift_z(): return lax.ppermute(value, 'z', [(z, (z + by) % NZ) for z in range(NZ)])  7.89 us
    pallas_call x1, Pallas kernels, blur_tiles(): pl.pallas_call(blur_kernel, grid=(TILES // HALF,), in_specs=[smem] * 5 +...  6.28 us
    pallas_call x1, Pallas kernels, finish(): pl.pallas_call(finish_kernel, in_specs=[pl.BlockSpec(memory_space=pltpu.S...  1.91 us
  transfers between devices with their start and end apart: 25, of which 13 were waited for; matrix products, arithmetic and copies ran while one was open for 0% of the time, Pallas kernels for 12%

profile of v5, /device:TPU:62, one launch (start us, length us, event | category | flops | bytes accessed | tf_op | source)
XLA Modules:
  0.0 91.8 jit_solution(3168074070199854097)
XLA Ops:
  0.0 6.3 %blur_tiles.1 = (f32[1544,128]{1,0:T(8,128)}, f32[1544,128]{1,0:T(8,128)}) custom-call(s32[1,24]{1,0:T(1,128)} %psf_ref.1, f32[3,16]{1,0:T(4,128)} %bitcast.8, f32[3,2,21]{2,1,0:T(2,128)} %taps_ref.1, s32[1,2,24]{2,1,0:T(2,128)} %bitcast.10, s32[1,2,2,24]{3,2,1,0:T(2,128)} %bitcast.9, f32[1,24,128,128]{3,2,1,0:T(8,128)} %img_ref.1, f32[1,24,128,128]{3,2,1,0:T(8,128)} %var_ref.1), custom_call_target="tpu_custom_call" | custom-call | flops 1824000000 | bytes 4718592 | tf_op jit(solution)/shard_map/blur_tiles/pallas_call | solution.py:111
  6.3 0.2 collective-permute-start
  6.5 1.8 %collective-permute-start.2 = (f32[1544,128]{1,0:T(8,128)}, f32[1544,128]{1,0:T(8,128)S(1)}, u32[]{:S(2)}, u32[]{:S(2)}) collective-permute-start(f32[1544,128]{1,0:T(8,128)} %get-tuple-element.43.refs_1_), channel_id=1, source_target_pairs={{0,3},{1,0},{2,1},{3,2},{4,196},{5,197},{6,198},{7,199},{64,67},{6... | collective-permute-start | bytes 2371592 | tf_op jit(solution)/shard_map/ppermute | solution.py:427
  8.3 0.7 collective-permute-start.4
  9.1 2.5 %collective-permute-start.5 = (f32[1544,128]{1,0:T(8,128)}, f32[1544,128]{1,0:T(8,128)}, u32[]{:S(2)}, u32[]{:S(2)}) collective-permute-start(f32[1544,128]{1,0:T(8,128)} %get-tuple-element.43.refs_1_), channel_id=1, source_target_pairs={{0,1},{1,2},{2,3},{3,0},{4,68},{5,69},{6,70},{7,71},{64,65},{65,66... | collective-permute-start | bytes 2371592 | tf_op jit(solution)/shard_map/ppermute | solution.py:427
  11.5 7.0 %collective-permute-done.refs_0_ = f32[1544,128]{1,0:T(8,128)S(1)} collective-permute-done((f32[1544,128]{1,0:T(8,128)}, f32[1544,128]{1,0:T(8,128)S(1)}, u32[]{:S(2)}, u32[]{:S(2)}) %collective-permute-start) | collective-permute-done | bytes 790560 | tf_op jit(solution)/shard_map/ppermute | solution.py:427
  18.5 1.4 %collective-permute-start.1 = (f32[1544,128]{1,0:T(8,128)S(1)}, f32[1544,128]{1,0:T(8,128)S(1)}, u32[]{:S(2)}, u32[]{:S(2)}) collective-permute-start(f32[1544,128]{1,0:T(8,128)S(1)} %collective-permute-done.refs_0_), channel_id=1, source_target_pairs={{0,1},{1,2},{2,3},{3,0},{4,68},{5,69},{6,70},{7,71},{64,65},{65,66... | collective-permute-start | bytes 2371592 | tf_op jit(solution)/shard_map/ppermute | solution.py:427
  20.0 0.0 collective-permute-done.2.refs_1_
  20.0 0.6 collective-permute-start.3
  20.6 0.1 pad_add_fusion.here_ref
  20.6 3.9 %place.4 = (f32[64,2,64,128]{3,2,1,0:T(8,128)S(1)}, f32[64,128]{1,0:T(8,128)S(1)}) custom-call(s32[4]{0:T(128)S(1)} %pad_add_fusion.here_ref, f32[1544,128]{1,0:T(8,128)} %get-tuple-element.42.refs_0_, f32[1544,128]{1,0:T(8,128)} %get-tuple-element.43.refs_1_), custom_call_target="tpu_custom_call" | custom-call | flops 1000000 | bytes 22140000 | tf_op jit(solution)/shard_map/place/pallas_call | solution.py:263
  24.5 4.0 %collective-permute-done.4.refs_0_ = f32[1544,128]{1,0:T(8,128)} collective-permute-done((f32[1544,128]{1,0:T(8,128)}, f32[1544,128]{1,0:T(8,128)}, u32[]{:S(2)}, u32[]{:S(2)}) %collective-permute-start.4) | collective-permute-done | bytes 790560 | tf_op jit(solution)/shard_map/ppermute | solution.py:427
  28.5 3.8 %place.5 = (f32[64,2,64,128]{3,2,1,0:T(8,128)S(1)}, f32[64,128]{1,0:T(8,128)S(1)}) custom-call(s32[4]{0:T(128)S(1)} %pad_add_fusion.here_ref, f32[1544,128]{1,0:T(8,128)} %collective-permute-done.4.refs_0_, f32[1544,128]{1,0:T(8,128)} %collective-permute-done.5.refs_1_, f32[64,2,64,128]{3,2,1,0:T(8,128)S(1)} %get-tuple-element.44.refs_2_, ...), custom_call_target="tpu_custom_call" | custom-call | flops 1000000 | bytes 22140000 | tf_op jit(solution)/shard_map/place/pallas_call | solution.py:263
  32.4 3.0 %place.6 = (f32[64,2,64,128]{3,2,1,0:T(8,128)S(1)}, f32[64,128]{1,0:T(8,128)S(1)}) custom-call(s32[4]{0:T(128)S(1)} %pad_add_fusion.here_ref, f32[1544,128]{1,0:T(8,128)S(1)} %collective-permute-done.refs_0_, f32[1544,128]{1,0:T(8,128)S(1)} %collective-permute-done.2.refs_1_, f32[64,2,64,128]{3,2,1,0:T(8,128)S(1)} %get-tuple-element.46.refs_2_, ...), custom_call_target="tpu_custom_call" | custom-call | flops 1000000 | bytes 22140000 | tf_op jit(solution)/shard_map/place/pallas_call | solution.py:263
  35.4 0.1 collective-permute-done.1.refs_0_
  35.5 1.4 %collective-permute-done.3.refs_1_ = f32[1544,128]{1,0:T(8,128)S(1)} collective-permute-done((f32[1544,128]{1,0:T(8,128)S(1)}, f32[1544,128]{1,0:T(8,128)S(1)}, u32[]{:S(2)}, u32[]{:S(2)}) %collective-permute-start.3) | collective-permute-done | bytes 790560 | tf_op jit(solution)/shard_map/ppermute | solution.py:427
  36.9 3.2 %place.7 = (f32[1032,128]{1,0:T(8,128)S(1)}, f32[1032,128]{1,0:T(8,128)S(1)}, f32[1032,128]{1,0:T(8,128)S(1)}, f32[1032,128]{1,0:T(8,128)S(1)}, f32[520,128]{1,0...) custom-call(s32[4]{0:T(128)S(1)} %pad_add_fusion.here_ref, ...), custom_call_target="tpu_custom_call" | custom-call | flops 1000000 | bytes 22140000 | tf_op jit(solution)/shard_map/place/pallas_call | solution.py:263
  40.2 0.7 collective-permute-start.8
  40.9 1.5 %collective-permute-start.9 = (f32[1032,128]{1,0:T(8,128)S(1)}, f32[1032,128]{1,0:T(8,128)S(1)}, u32[]{:S(2)}, u32[]{:S(2)}) collective-permute-start(f32[1032,128]{1,0:T(8,128)S(1)} %get-tuple-element.60), channel_id=1, source_target_pairs={{0,192},{1,193},{2,194},{3,195},{4,7},{5,4},{6,5},{7,6},{64,0},{65... | collective-permute-start | bytes 1585160 | tf_op jit(solution)/shard_map/ppermute | solution.py:427
  42.4 1.7 %collective-permute-start.11 = (f32[520,128]{1,0:T(8,128)S(1)}, f32[520,128]{1,0:T(8,128)S(1)}, u32[]{:S(2)}, u32[]{:S(2)}) collective-permute-start(f32[520,128]{1,0:T(8,128)S(1)} %get-tuple-element.62), channel_id=1, source_target_pairs={{0,64},{1,65},{2,66},{3,67},{4,5},{5,6},{6,7},{7,4},{64,128},{65,1... | collective-permute-start | bytes 798728 | tf_op jit(solution)/shard_map/ppermute | solution.py:427
  44.1 0.6 collective-permute-start.15
  44.7 4.9 %collective-permute-done.8.b = f32[1032,128]{1,0:T(8,128)S(1)} collective-permute-done((f32[1032,128]{1,0:T(8,128)S(1)}, f32[1032,128]{1,0:T(8,128)S(1)}, u32[]{:S(2)}, u32[]{:S(2)}) %collective-permute-start.8) | collective-permute-done | bytes 528416 | tf_op jit(solution)/shard_map/ppermute | solution.py:427
  49.6 0.8 collective-permute-start.7
  50.5 0.9 collective-permute-done.9.d
  51.3 0.1 add_received.1
  51.5 1.0 %collective-permute-done.11.refs_2_ = f32[520,128]{1,0:T(8,128)S(1)} collective-permute-done((f32[520,128]{1,0:T(8,128)S(1)}, f32[520,128]{1,0:T(8,128)S(1)}, u32[]{:S(2)}, u32[]{:S(2)}) %collective-permute-start.11) | collective-permute-done | bytes 266272 | tf_op jit(solution)/shard_map/ppermute | solution.py:427
  52.5 1.7 %collective-permute-start.10 = (f32[520,128]{1,0:T(8,128)S(1)}, f32[520,128]{1,0:T(8,128)S(1)}, u32[]{:S(2)}, u32[]{:S(2)}) collective-permute-start(f32[520,128]{1,0:T(8,128)S(1)} %get-tuple-element.61), channel_id=1, source_target_pairs={{0,64},{1,65},{2,66},{3,67},{4,5},{5,6},{6,7},{7,4},{64,128},{65,1... | collective-permute-start | bytes 798728 | tf_op jit(solution)/shard_map/ppermute | solution.py:427
  54.2 0.0 collective-permute-done.13.refs_4_
  54.2 0.3 collective-permute-start.12
  54.5 0.0 collective-permute-done.15.refs_6_
  54.5 1.9 %collective-permute-start.14 = (f32[520,128]{1,0:T(8,128)S(1)}, f32[520,128]{1,0:T(8,128)S(1)}, u32[]{:S(2)}, u32[]{:S(2)}) collective-permute-start(f32[520,128]{1,0:T(8,128)S(1)} %get-tuple-element.65), channel_id=1, source_target_pairs={{0,68},{1,69},{2,70},{3,71},{4,1},{5,2},{6,3},{7,0},{64,132},{65,1... | collective-permute-start | bytes 798728 | tf_op jit(solution)/shard_map/ppermute | solution.py:427
  56.5 0.8 collective-permute-done.7.refs_0_
  57.3 0.0 collective-permute-done.6.stay_cross
  57.3 1.6 %collective-permute-done.10.refs_1_ = f32[520,128]{1,0:T(8,128)S(1)} collective-permute-done((f32[520,128]{1,0:T(8,128)S(1)}, f32[520,128]{1,0:T(8,128)S(1)}, u32[]{:S(2)}, u32[]{:S(2)}) %collective-permute-start.10) | collective-permute-done | bytes 266272 | tf_op jit(solution)/shard_map/ppermute | solution.py:427
  58.9 2.9 %collective-permute-done.12.refs_3_ = f32[520,128]{1,0:T(8,128)S(1)} collective-permute-done((f32[520,128]{1,0:T(8,128)S(1)}, f32[520,128]{1,0:T(8,128)S(1)}, u32[]{:S(2)}, u32[]{:S(2)}) %collective-permute-start.12) | collective-permute-done | bytes 266272 | tf_op jit(solution)/shard_map/ppermute | solution.py:427
  61.8 0.0 collective-permute-done.14.refs_5_
  61.8 2.5 %collective-permute-done.16.refs_7_ = f32[520,128]{1,0:T(8,128)S(1)} collective-permute-done((f32[520,128]{1,0:T(8,128)S(1)}, f32[520,128]{1,0:T(8,128)S(1)}, u32[]{:S(2)}, u32[]{:S(2)}) %collective-permute-start.16) | collective-permute-done | bytes 266272 | tf_op jit(solution)/shard_map/ppermute | solution.py:427
  64.3 0.8 join.1
  65.1 2.0 %collective-permute-start.17 = (f32[136,128]{1,0:T(8,128)S(1)}, f32[136,128]{1,0:T(8,128)S(1)}, u32[]{:S(2)}, u32[]{:S(2)}) collective-permute-start(f32[136,128]{1,0:T(8,128)S(1)} %get-tuple-element.69), channel_id=1, source_target_pairs={{0,8},{8,16},{16,24},{24,32},{32,40},{40,48},{48,56},{56,0},{1,9},... | collective-permute-start | bytes 208904 | tf_op jit(solution)/shard_map/ppermute | solution.py:415
  67.1 0.1 collective-permute-start.20
  67.2 1.9 %collective-permute-start.19 = (f32[64,128]{1,0:T(8,128)S(1)}, f32[64,128]{1,0:T(8,128)S(1)}, u32[]{:S(2)}, u32[]{:S(2)}) collective-permute-start(f32[64,128]{1,0:T(8,128)S(1)} %get-tuple-element.73), channel_id=1, source_target_pairs={{0,8},{8,16},{16,24},{24,32},{32,40},{40,48},{48,56},{56,0},{1,9},... | collective-permute-start | bytes 98312 | tf_op jit(solution)/shard_map/ppermute | solution.py:415
  69.2 5.7 %collective-permute-start.18 = (f32[136,128]{1,0:T(8,128)S(1)}, f32[136,128]{1,0:T(8,128)S(1)}, u32[]{:S(2)}, u32[]{:S(2)}) collective-permute-start(f32[136,128]{1,0:T(8,128)S(1)} %get-tuple-element.70), channel_id=1, source_target_pairs={{0,16},{8,24},{16,32},{24,40},{32,48},{40,56},{48,0},{56,8},{1,17}... | collective-permute-start | bytes 208904 | tf_op jit(solution)/shard_map/ppermute | solution.py:415
  74.9 2.0 %collective-permute-start.23 = (f32[136,128]{1,0:T(8,128)S(1)}, f32[136,128]{1,0:T(8,128)S(1)}, u32[]{:S(2)}, u32[]{:S(2)}) collective-permute-start(f32[136,128]{1,0:T(8,128)S(1)} %get-tuple-element.77), channel_id=1, source_target_pairs={{0,48},{8,56},{16,0},{24,8},{32,16},{40,24},{48,32},{56,40},{1,49}... | collective-permute-start | bytes 208904 | tf_op jit(solution)/shard_map/ppermute | solution.py:415
  76.8 3.7 %collective-permute-start.21 = (f32[136,128]{1,0:T(8,128)S(1)}, f32[136,128]{1,0:T(8,128)S(1)}, u32[]{:S(2)}, u32[]{:S(2)}) collective-permute-start(f32[136,128]{1,0:T(8,128)S(1)} %get-tuple-element.75), channel_id=1, source_target_pairs={{0,24},{8,32},{16,40},{24,48},{32,56},{40,0},{48,8},{56,16},{1,25}... | collective-permute-start | bytes 208904 | tf_op jit(solution)/shard_map/ppermute | solution.py:415
  80.6 1.4 %collective-permute-start.24 = (f32[136,128]{1,0:T(8,128)S(1)}, f32[136,128]{1,0:T(8,128)S(1)}, u32[]{:S(2)}, u32[]{:S(2)}) collective-permute-start(f32[136,128]{1,0:T(8,128)S(1)} %get-tuple-element.78), channel_id=1, source_target_pairs={{0,40},{8,48},{16,56},{24,0},{32,8},{40,16},{48,24},{56,32},{1,41}... | collective-permute-start | bytes 208904 | tf_op jit(solution)/shard_map/ppermute | solution.py:415
  82.0 3.6 %collective-permute-done.21.refs_3_ = f32[136,128]{1,0:T(8,128)S(1)} collective-permute-done((f32[136,128]{1,0:T(8,128)S(1)}, f32[136,128]{1,0:T(8,128)S(1)}, u32[]{:S(2)}, u32[]{:S(2)}) %collective-permute-start.21) | collective-permute-done | bytes 69664 | tf_op jit(solution)/shard_map/ppermute | solution.py:415
  85.6 4.3 %collective-permute-done.24.refs_6_ = f32[136,128]{1,0:T(8,128)S(1)} collective-permute-done((f32[136,128]{1,0:T(8,128)S(1)}, f32[136,128]{1,0:T(8,128)S(1)}, u32[]{:S(2)}, u32[]{:S(2)}) %collective-permute-start.24) | collective-permute-done | bytes 69664 | tf_op jit(solution)/shard_map/ppermute | solution.py:415
  89.9 1.9 %finish.1 = f32[64,256]{1,0:T(8,128)} custom-call(s32[4]{0:T(128)S(1)} %pad_add_fusion.here_ref, f32[136,128]{1,0:T(8,128)S(1)} %get-tuple-element.68.refs_0_, f32[136,128]{1,0:T(8,128)S(1)} %collective-permute-done.17.refs_1_, f32[136,128]{1,0:T(8,128)S(1)} %collective-permute-done.18.refs_2_, f32[136,128]{1,0:T(8,128)S(1)} %collective-permute-done.21.refs_3_, ...), custom_call_target="tpu_custom_call" | custom-call | tf_op jit(solution)/shard_map/finish/pallas_call | solution.py:404
  (12 shorter events, 0.0 us)
Async XLA Ops:
  6.3 12.2 %collective-permute-start = (f32[1544,128]{1,0:T(8,128)}, f32[1544,128]{1,0:T(8,128)S(1)}, u32[]{:S(2)}, u32[]{:S(2)}) collective-permute-start(f32[1544,128]{1,0:T(8,128)} %get-tuple-element.42.refs_0_), channel_id=1, source_target_pairs={{0,1},{1,2},{2,3},{3,0},{4,68},{5,69},{6,70},{7,71},{64,65},{65,66... | collective-permute-start | bytes 2371592 | tf_op jit(solution)/shard_map/ppermute | solution.py:427
  6.5 13.5 %collective-permute-start.2 = (f32[1544,128]{1,0:T(8,128)}, f32[1544,128]{1,0:T(8,128)S(1)}, u32[]{:S(2)}, u32[]{:S(2)}) collective-permute-start(f32[1544,128]{1,0:T(8,128)} %get-tuple-element.43.refs_1_), channel_id=1, source_target_pairs={{0,3},{1,0},{2,1},{3,2},{4,196},{5,197},{6,198},{7,199},{64,67},{6... | collective-permute-start | bytes 2371592 | tf_op jit(solution)/shard_map/ppermute | solution.py:427
  8.3 20.2 %collective-permute-start.4 = (f32[1544,128]{1,0:T(8,128)}, f32[1544,128]{1,0:T(8,128)}, u32[]{:S(2)}, u32[]{:S(2)}) collective-permute-start(f32[1544,128]{1,0:T(8,128)} %get-tuple-element.42.refs_0_), channel_id=1, source_target_pairs={{0,3},{1,0},{2,1},{3,2},{4,196},{5,197},{6,198},{7,199},{64,67},{6... | collective-permute-start | bytes 2371592 | tf_op jit(solution)/shard_map/ppermute | solution.py:427
  9.1 19.5 %collective-permute-start.5 = (f32[1544,128]{1,0:T(8,128)}, f32[1544,128]{1,0:T(8,128)}, u32[]{:S(2)}, u32[]{:S(2)}) collective-permute-start(f32[1544,128]{1,0:T(8,128)} %get-tuple-element.43.refs_1_), channel_id=1, source_target_pairs={{0,1},{1,2},{2,3},{3,0},{4,68},{5,69},{6,70},{7,71},{64,65},{65,66... | collective-permute-start | bytes 2371592 | tf_op jit(solution)/shard_map/ppermute | solution.py:427
  18.5 16.9 %collective-permute-start.1 = (f32[1544,128]{1,0:T(8,128)S(1)}, f32[1544,128]{1,0:T(8,128)S(1)}, u32[]{:S(2)}, u32[]{:S(2)}) collective-permute-start(f32[1544,128]{1,0:T(8,128)S(1)} %collective-permute-done.refs_0_), channel_id=1, source_target_pairs={{0,1},{1,2},{2,3},{3,0},{4,68},{5,69},{6,70},{7,71},{64,65},{65,66... | collective-permute-start | bytes 2371592 | tf_op jit(solution)/shard_map/ppermute | solution.py:427
  20.0 16.9 %collective-permute-start.3 = (f32[1544,128]{1,0:T(8,128)S(1)}, f32[1544,128]{1,0:T(8,128)S(1)}, u32[]{:S(2)}, u32[]{:S(2)}) collective-permute-start(f32[1544,128]{1,0:T(8,128)S(1)} %collective-permute-done.2.refs_1_), channel_id=1, source_target_pairs={{0,3},{1,0},{2,1},{3,2},{4,196},{5,197},{6,198},{7,199},{64,67},{6... | collective-permute-start | bytes 2371592 | tf_op jit(solution)/shard_map/ppermute | solution.py:427
  40.2 9.5 %collective-permute-start.8 = (f32[1032,128]{1,0:T(8,128)S(1)}, f32[1032,128]{1,0:T(8,128)S(1)}, u32[]{:S(2)}, u32[]{:S(2)}) collective-permute-start(f32[1032,128]{1,0:T(8,128)S(1)} %get-tuple-element.58), channel_id=1, source_target_pairs={{0,64},{1,65},{2,66},{3,67},{4,5},{5,6},{6,7},{7,4},{64,128},{65,1... | collective-permute-start | bytes 1585160 | tf_op jit(solution)/shard_map/ppermute | solution.py:427
  40.9 10.4 %collective-permute-start.9 = (f32[1032,128]{1,0:T(8,128)S(1)}, f32[1032,128]{1,0:T(8,128)S(1)}, u32[]{:S(2)}, u32[]{:S(2)}) collective-permute-start(f32[1032,128]{1,0:T(8,128)S(1)} %get-tuple-element.60), channel_id=1, source_target_pairs={{0,192},{1,193},{2,194},{3,195},{4,7},{5,4},{6,5},{7,6},{64,0},{65... | collective-permute-start | bytes 1585160 | tf_op jit(solution)/shard_map/ppermute | solution.py:427
  42.4 10.1 %collective-permute-start.11 = (f32[520,128]{1,0:T(8,128)S(1)}, f32[520,128]{1,0:T(8,128)S(1)}, u32[]{:S(2)}, u32[]{:S(2)}) collective-permute-start(f32[520,128]{1,0:T(8,128)S(1)} %get-tuple-element.62), channel_id=1, source_target_pairs={{0,64},{1,65},{2,66},{3,67},{4,5},{5,6},{6,7},{7,4},{64,128},{65,1... | collective-permute-start | bytes 798728 | tf_op jit(solution)/shard_map/ppermute | solution.py:427
  44.1 10.1 %collective-permute-start.13 = (f32[520,128]{1,0:T(8,128)S(1)}, f32[520,128]{1,0:T(8,128)S(1)}, u32[]{:S(2)}, u32[]{:S(2)}) collective-permute-start(f32[520,128]{1,0:T(8,128)S(1)} %get-tuple-element.64), channel_id=1, source_target_pairs={{0,196},{1,197},{2,198},{3,199},{4,3},{5,0},{6,1},{7,2},{64,4},{65... | collective-permute-start | bytes 798728 | tf_op jit(solution)/shard_map/ppermute | solution.py:427
  44.1 10.4 %collective-permute-start.15 = (f32[520,128]{1,0:T(8,128)S(1)}, f32[520,128]{1,0:T(8,128)S(1)}, u32[]{:S(2)}, u32[]{:S(2)}) collective-permute-start(f32[520,128]{1,0:T(8,128)S(1)} %get-tuple-element.66), channel_id=1, source_target_pairs={{0,68},{1,69},{2,70},{3,71},{4,1},{5,2},{6,3},{7,0},{64,132},{65,1... | collective-permute-start | bytes 798728 | tf_op jit(solution)/shard_map/ppermute | solution.py:427
  49.6 7.6 %collective-permute-start.7 = (f32[520,128]{1,0:T(8,128)S(1)}, f32[520,128]{1,0:T(8,128)S(1)}, u32[]{:S(2)}, u32[]{:S(2)}) collective-permute-start(f32[520,128]{1,0:T(8,128)S(1)} %get-tuple-element.56), channel_id=1, source_target_pairs={{0,192},{1,193},{2,194},{3,195},{4,7},{5,4},{6,5},{7,6},{64,0},{65... | collective-permute-start | bytes 798728 | tf_op jit(solution)/shard_map/ppermute | solution.py:427
  51.3 5.9 %collective-permute-start.6 = (f32[1032,128]{1,0:T(8,128)S(1)}, f32[1032,128]{1,0:T(8,128)S(1)}, u32[]{:S(2)}, u32[]{:S(2)}) collective-permute-start(f32[1032,128]{1,0:T(8,128)S(1)} %get-tuple-element.55), channel_id=1, source_target_pairs={{0,4},{4,0},{1,5},{5,1},{2,6},{6,2},{3,7},{7,3},{8,12},{12,8},{9,1... | collective-permute-start | bytes 1585160 | tf_op jit(solution)/shard_map/ppermute | solution.py:449
  52.5 6.4 %collective-permute-start.10 = (f32[520,128]{1,0:T(8,128)S(1)}, f32[520,128]{1,0:T(8,128)S(1)}, u32[]{:S(2)}, u32[]{:S(2)}) collective-permute-start(f32[520,128]{1,0:T(8,128)S(1)} %get-tuple-element.61), channel_id=1, source_target_pairs={{0,64},{1,65},{2,66},{3,67},{4,5},{5,6},{6,7},{7,4},{64,128},{65,1... | collective-permute-start | bytes 798728 | tf_op jit(solution)/shard_map/ppermute | solution.py:427
  54.2 7.6 %collective-permute-start.12 = (f32[520,128]{1,0:T(8,128)S(1)}, f32[520,128]{1,0:T(8,128)S(1)}, u32[]{:S(2)}, u32[]{:S(2)}) collective-permute-start(f32[520,128]{1,0:T(8,128)S(1)} %get-tuple-element.63), channel_id=1, source_target_pairs={{0,192},{1,193},{2,194},{3,195},{4,7},{5,4},{6,5},{7,6},{64,0},{65... | collective-permute-start | bytes 798728 | tf_op jit(solution)/shard_map/ppermute | solution.py:427
  54.5 7.3 %collective-permute-start.14 = (f32[520,128]{1,0:T(8,128)S(1)}, f32[520,128]{1,0:T(8,128)S(1)}, u32[]{:S(2)}, u32[]{:S(2)}) collective-permute-start(f32[520,128]{1,0:T(8,128)S(1)} %get-tuple-element.65), channel_id=1, source_target_pairs={{0,68},{1,69},{2,70},{3,71},{4,1},{5,2},{6,3},{7,0},{64,132},{65,1... | collective-permute-start | bytes 798728 | tf_op jit(solution)/shard_map/ppermute | solution.py:427
  57.3 7.1 %collective-permute-start.16 = (f32[520,128]{1,0:T(8,128)S(1)}, f32[520,128]{1,0:T(8,128)S(1)}, u32[]{:S(2)}, u32[]{:S(2)}) collective-permute-start(f32[520,128]{1,0:T(8,128)S(1)} %get-tuple-element.67), channel_id=1, source_target_pairs={{0,196},{1,197},{2,198},{3,199},{4,3},{5,0},{6,1},{7,2},{64,4},{65... | collective-permute-start | bytes 798728 | tf_op jit(solution)/shard_map/ppermute | solution.py:427
  65.1 15.4 %collective-permute-start.17 = (f32[136,128]{1,0:T(8,128)S(1)}, f32[136,128]{1,0:T(8,128)S(1)}, u32[]{:S(2)}, u32[]{:S(2)}) collective-permute-start(f32[136,128]{1,0:T(8,128)S(1)} %get-tuple-element.69), channel_id=1, source_target_pairs={{0,8},{8,16},{16,24},{24,32},{32,40},{40,48},{48,56},{56,0},{1,9},... | collective-permute-start | bytes 208904 | tf_op jit(solution)/shard_map/ppermute | solution.py:415
  67.1 9.7 %collective-permute-start.20 = (f32[72,128]{1,0:T(8,128)S(1)}, f32[72,128]{1,0:T(8,128)S(1)}, u32[]{:S(2)}, u32[]{:S(2)}) collective-permute-start(f32[72,128]{1,0:T(8,128)S(1)} %get-tuple-element.74), channel_id=1, source_target_pairs={{0,56},{8,0},{16,8},{24,16},{32,24},{40,32},{48,40},{56,48},{1,57}... | collective-permute-start | bytes 110600 | tf_op jit(solution)/shard_map/ppermute | solution.py:415
  67.2 7.6 %collective-permute-start.19 = (f32[64,128]{1,0:T(8,128)S(1)}, f32[64,128]{1,0:T(8,128)S(1)}, u32[]{:S(2)}, u32[]{:S(2)}) collective-permute-start(f32[64,128]{1,0:T(8,128)S(1)} %get-tuple-element.73), channel_id=1, source_target_pairs={{0,8},{8,16},{16,24},{24,32},{32,40},{40,48},{48,56},{56,0},{1,9},... | collective-permute-start | bytes 98312 | tf_op jit(solution)/shard_map/ppermute | solution.py:415
  69.2 12.8 %collective-permute-start.18 = (f32[136,128]{1,0:T(8,128)S(1)}, f32[136,128]{1,0:T(8,128)S(1)}, u32[]{:S(2)}, u32[]{:S(2)}) collective-permute-start(f32[136,128]{1,0:T(8,128)S(1)} %get-tuple-element.70), channel_id=1, source_target_pairs={{0,16},{8,24},{16,32},{24,40},{32,48},{40,56},{48,0},{56,8},{1,17}... | collective-permute-start | bytes 208904 | tf_op jit(solution)/shard_map/ppermute | solution.py:415
  74.9 7.1 %collective-permute-start.22 = (f32[136,128]{1,0:T(8,128)S(1)}, f32[136,128]{1,0:T(8,128)S(1)}, u32[]{:S(2)}, u32[]{:S(2)}) collective-permute-start(f32[136,128]{1,0:T(8,128)S(1)} %get-tuple-element.76), channel_id=1, source_target_pairs={{0,56},{8,0},{16,8},{24,16},{32,24},{40,32},{48,40},{56,48},{1,57}... | collective-permute-start | bytes 208904 | tf_op jit(solution)/shard_map/ppermute | solution.py:415
  74.9 7.1 %collective-permute-start.23 = (f32[136,128]{1,0:T(8,128)S(1)}, f32[136,128]{1,0:T(8,128)S(1)}, u32[]{:S(2)}, u32[]{:S(2)}) collective-permute-start(f32[136,128]{1,0:T(8,128)S(1)} %get-tuple-element.77), channel_id=1, source_target_pairs={{0,48},{8,56},{16,0},{24,8},{32,16},{40,24},{48,32},{56,40},{1,49}... | collective-permute-start | bytes 208904 | tf_op jit(solution)/shard_map/ppermute | solution.py:415
  76.8 8.8 %collective-permute-start.21 = (f32[136,128]{1,0:T(8,128)S(1)}, f32[136,128]{1,0:T(8,128)S(1)}, u32[]{:S(2)}, u32[]{:S(2)}) collective-permute-start(f32[136,128]{1,0:T(8,128)S(1)} %get-tuple-element.75), channel_id=1, source_target_pairs={{0,24},{8,32},{16,40},{24,48},{32,56},{40,0},{48,8},{56,16},{1,25}... | collective-permute-start | bytes 208904 | tf_op jit(solution)/shard_map/ppermute | solution.py:415
  80.6 9.3 %collective-permute-start.24 = (f32[136,128]{1,0:T(8,128)S(1)}, f32[136,128]{1,0:T(8,128)S(1)}, u32[]{:S(2)}, u32[]{:S(2)}) collective-permute-start(f32[136,128]{1,0:T(8,128)S(1)} %get-tuple-element.78), channel_id=1, source_target_pairs={{0,40},{8,48},{16,56},{24,0},{32,8},{40,16},{48,24},{56,32},{1,41}... | collective-permute-start | bytes 208904 | tf_op jit(solution)/shard_map/ppermute | solution.py:415

commit v6 on v5

--- a/solution.py
+++ b/solution.py
@@ -365,50 +365,68 @@
     )(*arrays)
 
 
-def finish_kernel(here_ref, *refs):
-    *got, out = refs
+def sums_of(here_ref, sources):
     my_y = here_ref[2]
     lane = lax.broadcasted_iota(jnp.int32, (1, PIX), 1)
     row_of = lax.broadcasted_iota(jnp.int32, (STRIP, PIX), 0)
     col_of = lax.broadcasted_iota(jnp.int32, (PATCH_PIX, PIX), 0)
-    highs, mids, lows, hits = [], [], [], []
-    for source in (*got, got[-1]):
-        for core in range(NC):
-            at = ENTRY_ROWS + core + (NC if len(hits) >= len(got) * NC else 0)
-            note = source[at:at + 1, :]
-            weight = jnp.where(lane < SLOTS, note, 0.0)
-            row = pltpu.roll(note, PIX - SLOTS, 1).astype(jnp.int32) - my_y * STRIP
-            col = pltpu.roll(note, PIX - 2 * SLOTS, 1).astype(jnp.int32)
-            line, pixel = row_of - row, col_of - col
-            hit = (line >= 0) & (line < PIX)
-            high, rest = split(weight)
-            mid, low = split(weight - high.astype(F32))
-            for many, piece in ((highs, high), (mids, mid), (lows, low)):
-                many.append(jnp.where(hit, jnp.broadcast_to(piece.astype(F32), hit.shape), 0.0).astype(BF16))
-            hits.append(jnp.where((pixel >= 0) & (pixel < PIX), 1.0, 0.0).astype(BF16))
-    left = jnp.concatenate([jnp.concatenate(many, axis=1) for many in (highs, mids, lows)], axis=0)
-    sums = lax.dot_general(left, jnp.concatenate(hits, axis=1), (((1,), (1,)), ((), ())),
-                           preferred_element_type=F32)
-    denominator = sums[:STRIP] + (sums[STRIP:2 * STRIP] + sums[2 * STRIP:]) + 1.0
+    lines = [source[n:n + 1, :] for source, start, stop in sources for n in range(start, stop)]
+    pieces, hits = [], []
+    for first in range(0, len(lines), PIX // SLOTS):
+        weight, row, col = (sum(
+            pltpu.roll(jnp.where((lane >= kind * SLOTS) & (lane < (kind + 1) * SLOTS), note, 0.0),
+                       (n - kind) * SLOTS % PIX, 1) if n != kind else
+            jnp.where((lane >= kind * SLOTS) & (lane < (kind + 1) * SLOTS), note, 0.0)
+            for n, note in enumerate(lines[first:first + PIX // SLOTS])) for kind in range(3))
+        line = row_of + my_y * STRIP - row.astype(jnp.int32)
+        pixel = col_of - col.astype(jnp.int32)
+        hit = (line >= 0) & (line < PIX)
+        high, rest = split(weight)
+        mid, low = split(weight - high.astype(F32))
+        pieces.append(jnp.concatenate(
+            [jnp.where(hit, jnp.broadcast_to(piece.astype(F32), hit.shape), 0.0).astype(BF16)
+             for piece in (high, mid, low)], axis=0))
+        hits.append(jnp.where((pixel >= 0) & (pixel < PIX), 1.0, 0.0).astype(BF16))
+    sums = lax.dot_general(jnp.concatenate(pieces, axis=1), jnp.concatenate(hits, axis=1),
+                           (((1,), (1,)), ((), ())), preferred_element_type=F32)
+    total = sources[0][0][:ENTRY_ROWS]
+    for source, _, _ in sources[1:]:
+        total = total + source[:ENTRY_ROWS]
+    return total, sums[:STRIP] + (sums[STRIP:2 * STRIP] + sums[2 * STRIP:])
+
+
+def begin_kernel(here_ref, *refs):
+    *got, numerator, denominator = refs
+    numerator[...], denominator[...] = sums_of(here_ref, [(a, ENTRY_ROWS, ENTRY_ROWS + NC) for a in got])
+
+
+def finish_kernel(here_ref, numerator, denominator, ahead, behind, out):
+    total, sums = sums_of(here_ref, ((ahead, ENTRY_ROWS, ENTRY_ROWS + NC), (behind, ENTRY_ROWS, ENTRY_ROWS + 2 * NC)))
+    total, sums = total + numerator[...], sums + denominator[...] + 1.0
     for side in range(2):
-        rows = slice(side * STRIP, (side + 1) * STRIP)
-        total = got[0][rows]
-        for source in got[1:]:
-            total = total + source[rows]
         lanes = slice(side * PIX, (side + 1) * PIX)
-        out[:, lanes] = total / denominator[:, lanes]
-
-
-def finish(here, got):
+        out[:, lanes] = total[side * STRIP:(side + 1) * STRIP] / sums[:, lanes]
+
+
+def finish(here, early, late):
+    smem = pl.BlockSpec(memory_space=pltpu.SMEM)
     vmem = pl.BlockSpec(memory_space=pltpu.VMEM)
+    held = pl.pallas_call(
+        begin_kernel,
+        in_specs=[smem] + [vmem] * len(early),
+        out_specs=[vmem] * 2,
+        out_shape=[pltpu.VMEM((ENTRY_ROWS, PIX), F32), pltpu.VMEM((STRIP, PATCH_PIX), F32)],
+        compiler_params=pltpu.CompilerParams(vmem_limit_bytes=ADD_LIMIT),
+        name="begin",
+    )(here, *early)
     return pl.pallas_call(
         finish_kernel,
-        in_specs=[pl.BlockSpec(memory_space=pltpu.SMEM)] + [vmem] * len(got),
+        in_specs=[smem] + [vmem] * 4,
         out_specs=vmem,
         out_shape=jax.ShapeDtypeStruct((STRIP, PATCH_PIX), F32),
         compiler_params=pltpu.CompilerParams(vmem_limit_bytes=ADD_LIMIT),
         name="finish",
-    )(here, *got)
+    )(here, *held, *late)
 
 
 def shift_z(value, by):
@@ -455,7 +473,8 @@
 
     low, high = shift_z(four_low, 1), shift_z(four_high, -1)
     sent[2], sent[5] = relay(sent[2], sent[5], low, high)
-    return finish(here, (stay, *(shift_z(part, steps) for part, steps in zip(sent, STEPS))))[None]
+    got = [shift_z(part, steps) for part, steps in zip(sent, STEPS)]
+    return finish(here, (stay, got[0], got[1], got[3], got[4]), (got[2], got[5]))[None]
 
 
 def solution(mesh):

time: 91.9 us -> 91.5 us (level)
    pallas_call x1 -> x2, Pallas kernels: 1.91 us -> 2.35 us  [the longest x1 1.48 us: finish(): pl.pallas_call(finish_kernel, in_specs=[smem] + [vmem] * 4, out_specs=vme...]
  transfers between devices with their start and end apart: 25 -> 25, of which waited for: 13 -> 13; matrix products, arithmetic and copies ran while one was open for 0% -> 0% of each run, Pallas kernels for 12% -> 13%
where the time goes in v6:
time: 91.5 us; the launch traced here: 91.3 us
  waiting for transfers between devices  34.2 us (37%)
  starting transfers between devices  33.4 us (37%)
  Pallas kernels  23.6 us (26%)
    ppermute x16, waiting for transfers between devices, shift(): return lax.ppermute(value, ('x', 'core', 'y'), pairs)  27.1 us
    ppermute x8, starting transfers between devices, shift_z(): return lax.ppermute(value, 'z', [(z, (z + by) % NZ) for z in range(NZ)])  16.8 us
    ppermute x16, starting transfers between devices, shift(): return lax.ppermute(value, ('x', 'core', 'y'), pairs)  16.6 us
    pallas_call x4, Pallas kernels, place(): pl.pallas_call(functools.partial(place_kernel, tuple(runs), bool(old), la...  14 us
    ppermute x8, waiting for transfers between devices, shift_z(): return lax.ppermute(value, 'z', [(z, (z + by) % NZ) for z in range(NZ)])  7.02 us
    pallas_call x1, Pallas kernels, blur_tiles(): pl.pallas_call(blur_kernel, grid=(TILES // HALF,), in_specs=[smem] * 5 +...  6.27 us
  transfers between devices with their start and end apart: 25, of which 13 were waited for; matrix products, arithmetic and copies ran while one was open for 0% of the time, Pallas kernels for 13%

profile of v6, /device:TPU:62, one launch (start us, length us, event | category | flops | bytes accessed | tf_op | source)
XLA Modules:
  0.0 91.3 jit_solution(14329134557231444040)
XLA Ops:
  0.0 6.3 %blur_tiles.1 = (f32[1544,128]{1,0:T(8,128)}, f32[1544,128]{1,0:T(8,128)}) custom-call(s32[1,24]{1,0:T(1,128)} %psf_ref.1, f32[3,16]{1,0:T(4,128)} %bitcast.8, f32[3,2,21]{2,1,0:T(2,128)} %taps_ref.1, s32[1,2,24]{2,1,0:T(2,128)} %bitcast.10, s32[1,2,2,24]{3,2,1,0:T(2,128)} %bitcast.9, f32[1,24,128,128]{3,2,1,0:T(8,128)} %img_ref.1, f32[1,24,128,128]{3,2,1,0:T(8,128)} %var_ref.1), custom_call_target="tpu_custom_call" | custom-call | flops 1824000000 | bytes 4718592 | tf_op jit(solution)/shard_map/blur_tiles/pallas_call | solution.py:111
  6.3 0.2 collective-permute-start
  6.5 1.8 %collective-permute-start.2 = (f32[1544,128]{1,0:T(8,128)}, f32[1544,128]{1,0:T(8,128)S(1)}, u32[]{:S(2)}, u32[]{:S(2)}) collective-permute-start(f32[1544,128]{1,0:T(8,128)} %get-tuple-element.45.refs_1_), channel_id=1, source_target_pairs={{0,3},{1,0},{2,1},{3,2},{4,196},{5,197},{6,198},{7,199},{64,67},{6... | collective-permute-start | bytes 2371592 | tf_op jit(solution)/shard_map/ppermute | solution.py:445
  8.3 0.7 collective-permute-start.4
  9.0 2.5 %collective-permute-start.5 = (f32[1544,128]{1,0:T(8,128)}, f32[1544,128]{1,0:T(8,128)}, u32[]{:S(2)}, u32[]{:S(2)}) collective-permute-start(f32[1544,128]{1,0:T(8,128)} %get-tuple-element.45.refs_1_), channel_id=1, source_target_pairs={{0,1},{1,2},{2,3},{3,0},{4,68},{5,69},{6,70},{7,71},{64,65},{65,66... | collective-permute-start | bytes 2371592 | tf_op jit(solution)/shard_map/ppermute | solution.py:445
  11.5 7.0 %collective-permute-done.refs_0_ = f32[1544,128]{1,0:T(8,128)S(1)} collective-permute-done((f32[1544,128]{1,0:T(8,128)}, f32[1544,128]{1,0:T(8,128)S(1)}, u32[]{:S(2)}, u32[]{:S(2)}) %collective-permute-start) | collective-permute-done | bytes 790560 | tf_op jit(solution)/shard_map/ppermute | solution.py:445
  18.5 1.4 %collective-permute-start.1 = (f32[1544,128]{1,0:T(8,128)S(1)}, f32[1544,128]{1,0:T(8,128)S(1)}, u32[]{:S(2)}, u32[]{:S(2)}) collective-permute-start(f32[1544,128]{1,0:T(8,128)S(1)} %collective-permute-done.refs_0_), channel_id=1, source_target_pairs={{0,1},{1,2},{2,3},{3,0},{4,68},{5,69},{6,70},{7,71},{64,65},{65,66... | collective-permute-start | bytes 2371592 | tf_op jit(solution)/shard_map/ppermute | solution.py:445
  19.9 0.0 collective-permute-done.2.refs_1_
  20.0 0.6 collective-permute-start.3
  20.5 0.1 pad_add_fusion.here_ref
  20.6 3.9 %place.4 = (f32[64,2,64,128]{3,2,1,0:T(8,128)S(1)}, f32[64,128]{1,0:T(8,128)S(1)}) custom-call(s32[4]{0:T(128)S(1)} %pad_add_fusion.here_ref, f32[1544,128]{1,0:T(8,128)} %get-tuple-element.44.refs_0_, f32[1544,128]{1,0:T(8,128)} %get-tuple-element.45.refs_1_), custom_call_target="tpu_custom_call" | custom-call | flops 1000000 | bytes 22140000 | tf_op jit(solution)/shard_map/place/pallas_call | solution.py:263
  24.5 4.0 %collective-permute-done.4.refs_0_ = f32[1544,128]{1,0:T(8,128)} collective-permute-done((f32[1544,128]{1,0:T(8,128)}, f32[1544,128]{1,0:T(8,128)}, u32[]{:S(2)}, u32[]{:S(2)}) %collective-permute-start.4) | collective-permute-done | bytes 790560 | tf_op jit(solution)/shard_map/ppermute | solution.py:445
  28.5 3.8 %place.5 = (f32[64,2,64,128]{3,2,1,0:T(8,128)S(1)}, f32[64,128]{1,0:T(8,128)S(1)}) custom-call(s32[4]{0:T(128)S(1)} %pad_add_fusion.here_ref, f32[1544,128]{1,0:T(8,128)} %collective-permute-done.4.refs_0_, f32[1544,128]{1,0:T(8,128)} %collective-permute-done.5.refs_1_, f32[64,2,64,128]{3,2,1,0:T(8,128)S(1)} %get-tuple-element.46.refs_2_, ...), custom_call_target="tpu_custom_call" | custom-call | flops 1000000 | bytes 22140000 | tf_op jit(solution)/shard_map/place/pallas_call | solution.py:263
  32.4 3.0 %place.6 = (f32[64,2,64,128]{3,2,1,0:T(8,128)S(1)}, f32[64,128]{1,0:T(8,128)S(1)}) custom-call(s32[4]{0:T(128)S(1)} %pad_add_fusion.here_ref, f32[1544,128]{1,0:T(8,128)S(1)} %collective-permute-done.refs_0_, f32[1544,128]{1,0:T(8,128)S(1)} %collective-permute-done.2.refs_1_, f32[64,2,64,128]{3,2,1,0:T(8,128)S(1)} %get-tuple-element.48.refs_2_, ...), custom_call_target="tpu_custom_call" | custom-call | flops 1000000 | bytes 22140000 | tf_op jit(solution)/shard_map/place/pallas_call | solution.py:263
  35.4 0.1 collective-permute-done.1.refs_0_
  35.5 1.4 %collective-permute-done.3.refs_1_ = f32[1544,128]{1,0:T(8,128)S(1)} collective-permute-done((f32[1544,128]{1,0:T(8,128)S(1)}, f32[1544,128]{1,0:T(8,128)S(1)}, u32[]{:S(2)}, u32[]{:S(2)}) %collective-permute-start.3) | collective-permute-done | bytes 790560 | tf_op jit(solution)/shard_map/ppermute | solution.py:445
  36.9 3.2 %place.7 = (f32[1032,128]{1,0:T(8,128)S(1)}, f32[1032,128]{1,0:T(8,128)S(1)}, f32[1032,128]{1,0:T(8,128)S(1)}, f32[1032,128]{1,0:T(8,128)S(1)}, f32[520,128]{1,0...) custom-call(s32[4]{0:T(128)S(1)} %pad_add_fusion.here_ref, ...), custom_call_target="tpu_custom_call" | custom-call | flops 1000000 | bytes 22140000 | tf_op jit(solution)/shard_map/place/pallas_call | solution.py:263
  40.1 0.7 collective-permute-start.8
  40.9 1.5 %collective-permute-start.9 = (f32[1032,128]{1,0:T(8,128)S(1)}, f32[1032,128]{1,0:T(8,128)S(1)}, u32[]{:S(2)}, u32[]{:S(2)}) collective-permute-start(f32[1032,128]{1,0:T(8,128)S(1)} %get-tuple-element.62), channel_id=1, source_target_pairs={{0,192},{1,193},{2,194},{3,195},{4,7},{5,4},{6,5},{7,6},{64,0},{65... | collective-permute-start | bytes 1585160 | tf_op jit(solution)/shard_map/ppermute | solution.py:445
  42.4 1.7 %collective-permute-start.11 = (f32[520,128]{1,0:T(8,128)S(1)}, f32[520,128]{1,0:T(8,128)S(1)}, u32[]{:S(2)}, u32[]{:S(2)}) collective-permute-start(f32[520,128]{1,0:T(8,128)S(1)} %get-tuple-element.64), channel_id=1, source_target_pairs={{0,64},{1,65},{2,66},{3,67},{4,5},{5,6},{6,7},{7,4},{64,128},{65,1... | collective-permute-start | bytes 798728 | tf_op jit(solution)/shard_map/ppermute | solution.py:445
  44.1 0.0 collective-permute-start.13
  44.1 0.6 collective-permute-start.15
  44.7 4.9 %collective-permute-done.8.b = f32[1032,128]{1,0:T(8,128)S(1)} collective-permute-done((f32[1032,128]{1,0:T(8,128)S(1)}, f32[1032,128]{1,0:T(8,128)S(1)}, u32[]{:S(2)}, u32[]{:S(2)}) %collective-permute-start.8) | collective-permute-done | bytes 528416 | tf_op jit(solution)/shard_map/ppermute | solution.py:445
  49.6 0.8 collective-permute-start.7
  50.5 0.9 collective-permute-done.9.d
  51.3 0.1 add_received.1
  51.5 1.0 %collective-permute-done.11.refs_2_ = f32[520,128]{1,0:T(8,128)S(1)} collective-permute-done((f32[520,128]{1,0:T(8,128)S(1)}, f32[520,128]{1,0:T(8,128)S(1)}, u32[]{:S(2)}, u32[]{:S(2)}) %collective-permute-start.11) | collective-permute-done | bytes 266272 | tf_op jit(solution)/shard_map/ppermute | solution.py:445
  52.5 1.7 %collective-permute-start.10 = (f32[520,128]{1,0:T(8,128)S(1)}, f32[520,128]{1,0:T(8,128)S(1)}, u32[]{:S(2)}, u32[]{:S(2)}) collective-permute-start(f32[520,128]{1,0:T(8,128)S(1)} %get-tuple-element.63), channel_id=1, source_target_pairs={{0,64},{1,65},{2,66},{3,67},{4,5},{5,6},{6,7},{7,4},{64,128},{65,1... | collective-permute-start | bytes 798728 | tf_op jit(solution)/shard_map/ppermute | solution.py:445
  54.2 0.0 collective-permute-done.13.refs_4_
  54.2 0.3 collective-permute-start.12
  54.5 1.9 %collective-permute-start.14 = (f32[520,128]{1,0:T(8,128)S(1)}, f32[520,128]{1,0:T(8,128)S(1)}, u32[]{:S(2)}, u32[]{:S(2)}) collective-permute-start(f32[520,128]{1,0:T(8,128)S(1)} %get-tuple-element.67), channel_id=1, source_target_pairs={{0,68},{1,69},{2,70},{3,71},{4,1},{5,2},{6,3},{7,0},{64,132},{65,1... | collective-permute-start | bytes 798728 | tf_op jit(solution)/shard_map/ppermute | solution.py:445
  56.4 0.8 collective-permute-done.7.refs_0_
  57.3 0.0 collective-permute-start.16
  57.3 1.6 %collective-permute-done.10.refs_1_ = f32[520,128]{1,0:T(8,128)S(1)} collective-permute-done((f32[520,128]{1,0:T(8,128)S(1)}, f32[520,128]{1,0:T(8,128)S(1)}, u32[]{:S(2)}, u32[]{:S(2)}) %collective-permute-start.10) | collective-permute-done | bytes 266272 | tf_op jit(solution)/shard_map/ppermute | solution.py:445
  58.9 2.9 %collective-permute-done.12.refs_3_ = f32[520,128]{1,0:T(8,128)S(1)} collective-permute-done((f32[520,128]{1,0:T(8,128)S(1)}, f32[520,128]{1,0:T(8,128)S(1)}, u32[]{:S(2)}, u32[]{:S(2)}) %collective-permute-start.12) | collective-permute-done | bytes 266272 | tf_op jit(solution)/shard_map/ppermute | solution.py:445
  61.8 2.5 %collective-permute-done.16.refs_7_ = f32[520,128]{1,0:T(8,128)S(1)} collective-permute-done((f32[520,128]{1,0:T(8,128)S(1)}, f32[520,128]{1,0:T(8,128)S(1)}, u32[]{:S(2)}, u32[]{:S(2)}) %collective-permute-start.16) | collective-permute-done | bytes 266272 | tf_op jit(solution)/shard_map/ppermute | solution.py:445
  64.3 0.8 join.1
  65.1 2.0 %collective-permute-start.17 = (f32[136,128]{1,0:T(8,128)S(1)}, f32[136,128]{1,0:T(8,128)S(1)}, u32[]{:S(2)}, u32[]{:S(2)}) collective-permute-start(f32[136,128]{1,0:T(8,128)S(1)} %get-tuple-element.71), channel_id=1, source_target_pairs={{0,8},{8,16},{16,24},{24,32},{32,40},{40,48},{48,56},{56,0},{1,9},... | collective-permute-start | bytes 208904 | tf_op jit(solution)/shard_map/ppermute | solution.py:433
  67.1 0.1 collective-permute-start.22
  67.2 1.9 %collective-permute-start.21 = (f32[64,128]{1,0:T(8,128)S(1)}, f32[64,128]{1,0:T(8,128)S(1)}, u32[]{:S(2)}, u32[]{:S(2)}) collective-permute-start(f32[64,128]{1,0:T(8,128)S(1)} %get-tuple-element.79), channel_id=1, source_target_pairs={{0,8},{8,16},{16,24},{24,32},{32,40},{40,48},{48,56},{56,0},{1,9},... | collective-permute-start | bytes 98312 | tf_op jit(solution)/shard_map/ppermute | solution.py:433
  69.2 5.7 %collective-permute-start.18 = (f32[136,128]{1,0:T(8,128)S(1)}, f32[136,128]{1,0:T(8,128)S(1)}, u32[]{:S(2)}, u32[]{:S(2)}) collective-permute-start(f32[136,128]{1,0:T(8,128)S(1)} %get-tuple-element.72), channel_id=1, source_target_pairs={{0,16},{8,24},{16,32},{24,40},{32,48},{40,56},{48,0},{56,8},{1,17}... | collective-permute-start | bytes 208904 | tf_op jit(solution)/shard_map/ppermute | solution.py:433
  74.9 2.0 %collective-permute-start.20 = (f32[136,128]{1,0:T(8,128)S(1)}, f32[136,128]{1,0:T(8,128)S(1)}, u32[]{:S(2)}, u32[]{:S(2)}) collective-permute-start(f32[136,128]{1,0:T(8,128)S(1)} %get-tuple-element.74), channel_id=1, source_target_pairs={{0,48},{8,56},{16,0},{24,8},{32,16},{40,24},{48,32},{56,40},{1,49}... | collective-permute-start | bytes 208904 | tf_op jit(solution)/shard_map/ppermute | solution.py:433
  76.8 3.7 %collective-permute-start.23 = (f32[136,128]{1,0:T(8,128)S(1)}, f32[136,128]{1,0:T(8,128)S(1)}, u32[]{:S(2)}, u32[]{:S(2)}) collective-permute-start(f32[136,128]{1,0:T(8,128)S(1)} %get-tuple-element.81), channel_id=1, source_target_pairs={{0,24},{8,32},{16,40},{24,48},{32,56},{40,0},{48,8},{56,16},{1,25}... | collective-permute-start | bytes 208904 | tf_op jit(solution)/shard_map/ppermute | solution.py:433
  80.6 1.4 %collective-permute-start.24 = (f32[136,128]{1,0:T(8,128)S(1)}, f32[136,128]{1,0:T(8,128)S(1)}, u32[]{:S(2)}, u32[]{:S(2)}) collective-permute-start(f32[136,128]{1,0:T(8,128)S(1)} %get-tuple-element.82), channel_id=1, source_target_pairs={{0,40},{8,48},{16,56},{24,0},{32,8},{40,16},{48,24},{56,32},{1,41}... | collective-permute-start | bytes 208904 | tf_op jit(solution)/shard_map/ppermute | solution.py:433
  82.0 0.9 begin.1
  82.8 2.7 %collective-permute-done.23.ahead = f32[136,128]{1,0:T(8,128)S(1)} collective-permute-done((f32[136,128]{1,0:T(8,128)S(1)}, f32[136,128]{1,0:T(8,128)S(1)}, u32[]{:S(2)}, u32[]{:S(2)}) %collective-permute-start.23) | collective-permute-done | bytes 69664 | tf_op jit(solution)/shard_map/ppermute | solution.py:433
  85.6 4.3 %collective-permute-done.24.behind = f32[136,128]{1,0:T(8,128)S(1)} collective-permute-done((f32[136,128]{1,0:T(8,128)S(1)}, f32[136,128]{1,0:T(8,128)S(1)}, u32[]{:S(2)}, u32[]{:S(2)}) %collective-permute-start.24) | collective-permute-done | bytes 69664 | tf_op jit(solution)/shard_map/ppermute | solution.py:433
  89.8 1.5 %finish.1 = f32[64,256]{1,0:T(8,128)} custom-call(s32[4]{0:T(128)S(1)} %pad_add_fusion.here_ref, f32[128,128]{1,0:T(8,128)S(1)} %get-tuple-element.75.numerator, f32[64,256]{1,0:T(8,128)S(1)} %get-tuple-element.76.denominator, f32[136,128]{1,0:T(8,128)S(1)} %collective-permute-done.23.ahead, f32[136,128]{1,0:T(8,128)S(1)} %collective-permute-done.24.behind), custom_call_target="tpu_custom_call" | custom-call | tf_op jit(solution)/shard_map/finish/pallas_call | solution.py:422
  (13 shorter events, 0.0 us)
Async XLA Ops:
  6.3 12.2 %collective-permute-start = (f32[1544,128]{1,0:T(8,128)}, f32[1544,128]{1,0:T(8,128)S(1)}, u32[]{:S(2)}, u32[]{:S(2)}) collective-permute-start(f32[1544,128]{1,0:T(8,128)} %get-tuple-element.44.refs_0_), channel_id=1, source_target_pairs={{0,1},{1,2},{2,3},{3,0},{4,68},{5,69},{6,70},{7,71},{64,65},{65,66... | collective-permute-start | bytes 2371592 | tf_op jit(solution)/shard_map/ppermute | solution.py:445
  6.5 13.5 %collective-permute-start.2 = (f32[1544,128]{1,0:T(8,128)}, f32[1544,128]{1,0:T(8,128)S(1)}, u32[]{:S(2)}, u32[]{:S(2)}) collective-permute-start(f32[1544,128]{1,0:T(8,128)} %get-tuple-element.45.refs_1_), channel_id=1, source_target_pairs={{0,3},{1,0},{2,1},{3,2},{4,196},{5,197},{6,198},{7,199},{64,67},{6... | collective-permute-start | bytes 2371592 | tf_op jit(solution)/shard_map/ppermute | solution.py:445
  8.3 20.2 %collective-permute-start.4 = (f32[1544,128]{1,0:T(8,128)}, f32[1544,128]{1,0:T(8,128)}, u32[]{:S(2)}, u32[]{:S(2)}) collective-permute-start(f32[1544,128]{1,0:T(8,128)} %get-tuple-element.44.refs_0_), channel_id=1, source_target_pairs={{0,3},{1,0},{2,1},{3,2},{4,196},{5,197},{6,198},{7,199},{64,67},{6... | collective-permute-start | bytes 2371592 | tf_op jit(solution)/shard_map/ppermute | solution.py:445
  9.0 19.5 %collective-permute-start.5 = (f32[1544,128]{1,0:T(8,128)}, f32[1544,128]{1,0:T(8,128)}, u32[]{:S(2)}, u32[]{:S(2)}) collective-permute-start(f32[1544,128]{1,0:T(8,128)} %get-tuple-element.45.refs_1_), channel_id=1, source_target_pairs={{0,1},{1,2},{2,3},{3,0},{4,68},{5,69},{6,70},{7,71},{64,65},{65,66... | collective-permute-start | bytes 2371592 | tf_op jit(solution)/shard_map/ppermute | solution.py:445
  18.5 16.9 %collective-permute-start.1 = (f32[1544,128]{1,0:T(8,128)S(1)}, f32[1544,128]{1,0:T(8,128)S(1)}, u32[]{:S(2)}, u32[]{:S(2)}) collective-permute-start(f32[1544,128]{1,0:T(8,128)S(1)} %collective-permute-done.refs_0_), channel_id=1, source_target_pairs={{0,1},{1,2},{2,3},{3,0},{4,68},{5,69},{6,70},{7,71},{64,65},{65,66... | collective-permute-start | bytes 2371592 | tf_op jit(solution)/shard_map/ppermute | solution.py:445
  20.0 16.9 %collective-permute-start.3 = (f32[1544,128]{1,0:T(8,128)S(1)}, f32[1544,128]{1,0:T(8,128)S(1)}, u32[]{:S(2)}, u32[]{:S(2)}) collective-permute-start(f32[1544,128]{1,0:T(8,128)S(1)} %collective-permute-done.2.refs_1_), channel_id=1, source_target_pairs={{0,3},{1,0},{2,1},{3,2},{4,196},{5,197},{6,198},{7,199},{64,67},{6... | collective-permute-start | bytes 2371592 | tf_op jit(solution)/shard_map/ppermute | solution.py:445
  40.1 9.5 %collective-permute-start.8 = (f32[1032,128]{1,0:T(8,128)S(1)}, f32[1032,128]{1,0:T(8,128)S(1)}, u32[]{:S(2)}, u32[]{:S(2)}) collective-permute-start(f32[1032,128]{1,0:T(8,128)S(1)} %get-tuple-element.60), channel_id=1, source_target_pairs={{0,64},{1,65},{2,66},{3,67},{4,5},{5,6},{6,7},{7,4},{64,128},{65,1... | collective-permute-start | bytes 1585160 | tf_op jit(solution)/shard_map/ppermute | solution.py:445
  40.9 10.4 %collective-permute-start.9 = (f32[1032,128]{1,0:T(8,128)S(1)}, f32[1032,128]{1,0:T(8,128)S(1)}, u32[]{:S(2)}, u32[]{:S(2)}) collective-permute-start(f32[1032,128]{1,0:T(8,128)S(1)} %get-tuple-element.62), channel_id=1, source_target_pairs={{0,192},{1,193},{2,194},{3,195},{4,7},{5,4},{6,5},{7,6},{64,0},{65... | collective-permute-start | bytes 1585160 | tf_op jit(solution)/shard_map/ppermute | solution.py:445
  42.4 10.1 %collective-permute-start.11 = (f32[520,128]{1,0:T(8,128)S(1)}, f32[520,128]{1,0:T(8,128)S(1)}, u32[]{:S(2)}, u32[]{:S(2)}) collective-permute-start(f32[520,128]{1,0:T(8,128)S(1)} %get-tuple-element.64), channel_id=1, source_target_pairs={{0,64},{1,65},{2,66},{3,67},{4,5},{5,6},{6,7},{7,4},{64,128},{65,1... | collective-permute-start | bytes 798728 | tf_op jit(solution)/shard_map/ppermute | solution.py:445
  44.1 10.1 %collective-permute-start.13 = (f32[520,128]{1,0:T(8,128)S(1)}, f32[520,128]{1,0:T(8,128)S(1)}, u32[]{:S(2)}, u32[]{:S(2)}) collective-permute-start(f32[520,128]{1,0:T(8,128)S(1)} %get-tuple-element.66), channel_id=1, source_target_pairs={{0,196},{1,197},{2,198},{3,199},{4,3},{5,0},{6,1},{7,2},{64,4},{65... | collective-permute-start | bytes 798728 | tf_op jit(solution)/shard_map/ppermute | solution.py:445
  44.1 10.4 %collective-permute-start.15 = (f32[520,128]{1,0:T(8,128)S(1)}, f32[520,128]{1,0:T(8,128)S(1)}, u32[]{:S(2)}, u32[]{:S(2)}) collective-permute-start(f32[520,128]{1,0:T(8,128)S(1)} %get-tuple-element.68), channel_id=1, source_target_pairs={{0,68},{1,69},{2,70},{3,71},{4,1},{5,2},{6,3},{7,0},{64,132},{65,1... | collective-permute-start | bytes 798728 | tf_op jit(solution)/shard_map/ppermute | solution.py:445
  49.6 7.6 %collective-permute-start.7 = (f32[520,128]{1,0:T(8,128)S(1)}, f32[520,128]{1,0:T(8,128)S(1)}, u32[]{:S(2)}, u32[]{:S(2)}) collective-permute-start(f32[520,128]{1,0:T(8,128)S(1)} %get-tuple-element.58), channel_id=1, source_target_pairs={{0,192},{1,193},{2,194},{3,195},{4,7},{5,4},{6,5},{7,6},{64,0},{65... | collective-permute-start | bytes 798728 | tf_op jit(solution)/shard_map/ppermute | solution.py:445
  51.3 5.9 %collective-permute-start.6 = (f32[1032,128]{1,0:T(8,128)S(1)}, f32[1032,128]{1,0:T(8,128)S(1)}, u32[]{:S(2)}, u32[]{:S(2)}) collective-permute-start(f32[1032,128]{1,0:T(8,128)S(1)} %get-tuple-element.57), channel_id=1, source_target_pairs={{0,4},{4,0},{1,5},{5,1},{2,6},{6,2},{3,7},{7,3},{8,12},{12,8},{9,1... | collective-permute-start | bytes 1585160 | tf_op jit(solution)/shard_map/ppermute | solution.py:467
  52.5 6.4 %collective-permute-start.10 = (f32[520,128]{1,0:T(8,128)S(1)}, f32[520,128]{1,0:T(8,128)S(1)}, u32[]{:S(2)}, u32[]{:S(2)}) collective-permute-start(f32[520,128]{1,0:T(8,128)S(1)} %get-tuple-element.63), channel_id=1, source_target_pairs={{0,64},{1,65},{2,66},{3,67},{4,5},{5,6},{6,7},{7,4},{64,128},{65,1... | collective-permute-start | bytes 798728 | tf_op jit(solution)/shard_map/ppermute | solution.py:445
  54.2 7.6 %collective-permute-start.12 = (f32[520,128]{1,0:T(8,128)S(1)}, f32[520,128]{1,0:T(8,128)S(1)}, u32[]{:S(2)}, u32[]{:S(2)}) collective-permute-start(f32[520,128]{1,0:T(8,128)S(1)} %get-tuple-element.65), channel_id=1, source_target_pairs={{0,192},{1,193},{2,194},{3,195},{4,7},{5,4},{6,5},{7,6},{64,0},{65... | collective-permute-start | bytes 798728 | tf_op jit(solution)/shard_map/ppermute | solution.py:445
  54.5 7.3 %collective-permute-start.14 = (f32[520,128]{1,0:T(8,128)S(1)}, f32[520,128]{1,0:T(8,128)S(1)}, u32[]{:S(2)}, u32[]{:S(2)}) collective-permute-start(f32[520,128]{1,0:T(8,128)S(1)} %get-tuple-element.67), channel_id=1, source_target_pairs={{0,68},{1,69},{2,70},{3,71},{4,1},{5,2},{6,3},{7,0},{64,132},{65,1... | collective-permute-start | bytes 798728 | tf_op jit(solution)/shard_map/ppermute | solution.py:445
  57.3 7.1 %collective-permute-start.16 = (f32[520,128]{1,0:T(8,128)S(1)}, f32[520,128]{1,0:T(8,128)S(1)}, u32[]{:S(2)}, u32[]{:S(2)}) collective-permute-start(f32[520,128]{1,0:T(8,128)S(1)} %get-tuple-element.69), channel_id=1, source_target_pairs={{0,196},{1,197},{2,198},{3,199},{4,3},{5,0},{6,1},{7,2},{64,4},{65... | collective-permute-start | bytes 798728 | tf_op jit(solution)/shard_map/ppermute | solution.py:445
  65.1 15.4 %collective-permute-start.17 = (f32[136,128]{1,0:T(8,128)S(1)}, f32[136,128]{1,0:T(8,128)S(1)}, u32[]{:S(2)}, u32[]{:S(2)}) collective-permute-start(f32[136,128]{1,0:T(8,128)S(1)} %get-tuple-element.71), channel_id=1, source_target_pairs={{0,8},{8,16},{16,24},{24,32},{32,40},{40,48},{48,56},{56,0},{1,9},... | collective-permute-start | bytes 208904 | tf_op jit(solution)/shard_map/ppermute | solution.py:433
  67.1 9.7 %collective-permute-start.22 = (f32[72,128]{1,0:T(8,128)S(1)}, f32[72,128]{1,0:T(8,128)S(1)}, u32[]{:S(2)}, u32[]{:S(2)}) collective-permute-start(f32[72,128]{1,0:T(8,128)S(1)} %get-tuple-element.80), channel_id=1, source_target_pairs={{0,56},{8,0},{16,8},{24,16},{32,24},{40,32},{48,40},{56,48},{1,57}... | collective-permute-start | bytes 110600 | tf_op jit(solution)/shard_map/ppermute | solution.py:433
  67.2 7.6 %collective-permute-start.21 = (f32[64,128]{1,0:T(8,128)S(1)}, f32[64,128]{1,0:T(8,128)S(1)}, u32[]{:S(2)}, u32[]{:S(2)}) collective-permute-start(f32[64,128]{1,0:T(8,128)S(1)} %get-tuple-element.79), channel_id=1, source_target_pairs={{0,8},{8,16},{16,24},{24,32},{32,40},{40,48},{48,56},{56,0},{1,9},... | collective-permute-start | bytes 98312 | tf_op jit(solution)/shard_map/ppermute | solution.py:433
  69.2 12.8 %collective-permute-start.18 = (f32[136,128]{1,0:T(8,128)S(1)}, f32[136,128]{1,0:T(8,128)S(1)}, u32[]{:S(2)}, u32[]{:S(2)}) collective-permute-start(f32[136,128]{1,0:T(8,128)S(1)} %get-tuple-element.72), channel_id=1, source_target_pairs={{0,16},{8,24},{16,32},{24,40},{32,48},{40,56},{48,0},{56,8},{1,17}... | collective-permute-start | bytes 208904 | tf_op jit(solution)/shard_map/ppermute | solution.py:433
  74.9 7.1 %collective-permute-start.19 = (f32[136,128]{1,0:T(8,128)S(1)}, f32[136,128]{1,0:T(8,128)S(1)}, u32[]{:S(2)}, u32[]{:S(2)}) collective-permute-start(f32[136,128]{1,0:T(8,128)S(1)} %get-tuple-element.73), channel_id=1, source_target_pairs={{0,56},{8,0},{16,8},{24,16},{32,24},{40,32},{48,40},{56,48},{1,57}... | collective-permute-start | bytes 208904 | tf_op jit(solution)/shard_map/ppermute | solution.py:433
  74.9 7.1 %collective-permute-start.20 = (f32[136,128]{1,0:T(8,128)S(1)}, f32[136,128]{1,0:T(8,128)S(1)}, u32[]{:S(2)}, u32[]{:S(2)}) collective-permute-start(f32[136,128]{1,0:T(8,128)S(1)} %get-tuple-element.74), channel_id=1, source_target_pairs={{0,48},{8,56},{16,0},{24,8},{32,16},{40,24},{48,32},{56,40},{1,49}... | collective-permute-start | bytes 208904 | tf_op jit(solution)/shard_map/ppermute | solution.py:433
  76.8 8.8 %collective-permute-start.23 = (f32[136,128]{1,0:T(8,128)S(1)}, f32[136,128]{1,0:T(8,128)S(1)}, u32[]{:S(2)}, u32[]{:S(2)}) collective-permute-start(f32[136,128]{1,0:T(8,128)S(1)} %get-tuple-element.81), channel_id=1, source_target_pairs={{0,24},{8,32},{16,40},{24,48},{32,56},{40,0},{48,8},{56,16},{1,25}... | collective-permute-start | bytes 208904 | tf_op jit(solution)/shard_map/ppermute | solution.py:433
  80.6 9.3 %collective-permute-start.24 = (f32[136,128]{1,0:T(8,128)S(1)}, f32[136,128]{1,0:T(8,128)S(1)}, u32[]{:S(2)}, u32[]{:S(2)}) collective-permute-start(f32[136,128]{1,0:T(8,128)S(1)} %get-tuple-element.82), channel_id=1, source_target_pairs={{0,40},{8,48},{16,56},{24,0},{32,8},{40,16},{48,24},{56,32},{1,41}... | collective-permute-start | bytes 208904 | tf_op jit(solution)/shard_map/ppermute | solution.py:433

commit v7 on v6

--- a/solution.py
+++ b/solution.py
@@ -18,7 +18,8 @@
 STRIP = PATCH_PIX // NY
 TILES = 24
 HALF = 12
-UNROLL = 3
+UNROLL = 6
+LISTED = 4
 META = 8
 PATCH, ROW, COL, RANK, WEIGHT = range(5)
 ENTRIES = NZ * NC
@@ -212,9 +213,9 @@
 
     def along_x(t, number):
         items = []
-        for k in range(2):
-            valid = 2 * t + k < number
-            at = jnp.minimum(2 * t + k, number - 1)
+        for k in range(LISTED):
+            valid = LISTED * t + k < number
+            at = jnp.minimum(LISTED * t + k, number - 1)
             code, tile_row, slot = list_ref[0, at], list_ref[1, at], list_ref[2, at]
             patch, row, col, note = pair_of(code >> 7, code & (PIX - 1), jnp.where(valid, slot, PIX))
             for n in range(NY):
@@ -240,7 +241,7 @@
         number = 0
         for groups, run in given:
             number = lax.fori_loop(0, groups, functools.partial(list_x, **run), number)
-        lax.fori_loop(0, (number + 1) >> 1, along_x, number)
+        lax.fori_loop(0, (number + LISTED - 1) // LISTED, along_x, number)
 
     if last:
         for out, first in zip(outs, LAST):

time: 91.5 us -> 91.2 us (level)
  no operation moved by 1% of the time
where the time goes in v7:
time: 91.2 us; the launch traced here: 91 us
  waiting for transfers between devices  34.4 us (38%)
  starting transfers between devices  33.3 us (37%)
  Pallas kernels  23.2 us (25%)
    ppermute x16, waiting for transfers between devices, shift(): return lax.ppermute(value, ('x', 'core', 'y'), pairs)  27.4 us
    ppermute x8, starting transfers between devices, shift_z(): return lax.ppermute(value, 'z', [(z, (z + by) % NZ) for z in range(NZ)])  16.8 us
    ppermute x16, starting transfers between devices, shift(): return lax.ppermute(value, ('x', 'core', 'y'), pairs)  16.5 us
    pallas_call x4, Pallas kernels, place(): pl.pallas_call(functools.partial(place_kernel, tuple(runs), bool(old), la...  13.6 us
    ppermute x8, waiting for transfers between devices, shift_z(): return lax.ppermute(value, 'z', [(z, (z + by) % NZ) for z in range(NZ)])  7.02 us
    pallas_call x1, Pallas kernels, blur_tiles(): pl.pallas_call(blur_kernel, grid=(TILES // HALF,), in_specs=[smem] * 5 +...  6.27 us
  transfers between devices with their start and end apart: 25, of which 13 were waited for; matrix products, arithmetic and copies ran while one was open for 0% of the time, Pallas kernels for 13%

profile of v7, /device:TPU:62, one launch (start us, length us, event | category | flops | bytes accessed | tf_op | source)
XLA Modules:
  0.0 91.0 jit_solution(12137006201030221225)
XLA Ops:
  0.0 6.3 %blur_tiles.1 = (f32[1544,128]{1,0:T(8,128)}, f32[1544,128]{1,0:T(8,128)}) custom-call(s32[1,24]{1,0:T(1,128)} %psf_ref.1, f32[3,16]{1,0:T(4,128)} %bitcast.8, f32[3,2,21]{2,1,0:T(2,128)} %taps_ref.1, s32[1,2,24]{2,1,0:T(2,128)} %bitcast.10, s32[1,2,2,24]{3,2,1,0:T(2,128)} %bitcast.9, f32[1,24,128,128]{3,2,1,0:T(8,128)} %img_ref.1, f32[1,24,128,128]{3,2,1,0:T(8,128)} %var_ref.1), custom_call_target="tpu_custom_call" | custom-call | flops 1824000000 | bytes 4718592 | tf_op jit(solution)/shard_map/blur_tiles/pallas_call | solution.py:112
  6.3 0.2 collective-permute-start
  6.5 1.8 %collective-permute-start.2 = (f32[1544,128]{1,0:T(8,128)}, f32[1544,128]{1,0:T(8,128)S(1)}, u32[]{:S(2)}, u32[]{:S(2)}) collective-permute-start(f32[1544,128]{1,0:T(8,128)} %get-tuple-element.45.refs_1_), channel_id=1, source_target_pairs={{0,3},{1,0},{2,1},{3,2},{4,196},{5,197},{6,198},{7,199},{64,67},{6... | collective-permute-start | bytes 2371592 | tf_op jit(solution)/shard_map/ppermute | solution.py:446
  8.3 0.7 collective-permute-start.4
  9.0 2.5 %collective-permute-start.5 = (f32[1544,128]{1,0:T(8,128)}, f32[1544,128]{1,0:T(8,128)}, u32[]{:S(2)}, u32[]{:S(2)}) collective-permute-start(f32[1544,128]{1,0:T(8,128)} %get-tuple-element.45.refs_1_), channel_id=1, source_target_pairs={{0,1},{1,2},{2,3},{3,0},{4,68},{5,69},{6,70},{7,71},{64,65},{65,66... | collective-permute-start | bytes 2371592 | tf_op jit(solution)/shard_map/ppermute | solution.py:446
  11.5 7.0 %collective-permute-done.refs_0_ = f32[1544,128]{1,0:T(8,128)S(1)} collective-permute-done((f32[1544,128]{1,0:T(8,128)}, f32[1544,128]{1,0:T(8,128)S(1)}, u32[]{:S(2)}, u32[]{:S(2)}) %collective-permute-start) | collective-permute-done | bytes 790560 | tf_op jit(solution)/shard_map/ppermute | solution.py:446
  18.5 1.4 %collective-permute-start.1 = (f32[1544,128]{1,0:T(8,128)S(1)}, f32[1544,128]{1,0:T(8,128)S(1)}, u32[]{:S(2)}, u32[]{:S(2)}) collective-permute-start(f32[1544,128]{1,0:T(8,128)S(1)} %collective-permute-done.refs_0_), channel_id=1, source_target_pairs={{0,1},{1,2},{2,3},{3,0},{4,68},{5,69},{6,70},{7,71},{64,65},{65,66... | collective-permute-start | bytes 2371592 | tf_op jit(solution)/shard_map/ppermute | solution.py:446
  19.9 0.0 collective-permute-done.2.refs_1_
  20.0 0.6 collective-permute-start.3
  20.5 0.1 pad_add_fusion.here_ref
  20.6 3.8 %place.4 = (f32[64,2,64,128]{3,2,1,0:T(8,128)S(1)}, f32[64,128]{1,0:T(8,128)S(1)}) custom-call(s32[4]{0:T(128)S(1)} %pad_add_fusion.here_ref, f32[1544,128]{1,0:T(8,128)} %get-tuple-element.44.refs_0_, f32[1544,128]{1,0:T(8,128)} %get-tuple-element.45.refs_1_), custom_call_target="tpu_custom_call" | custom-call | flops 1000000 | bytes 22140000 | tf_op jit(solution)/shard_map/place/pallas_call | solution.py:264
  24.4 4.1 %collective-permute-done.4.refs_0_ = f32[1544,128]{1,0:T(8,128)} collective-permute-done((f32[1544,128]{1,0:T(8,128)}, f32[1544,128]{1,0:T(8,128)}, u32[]{:S(2)}, u32[]{:S(2)}) %collective-permute-start.4) | collective-permute-done | bytes 790560 | tf_op jit(solution)/shard_map/ppermute | solution.py:446
  28.5 3.7 %place.5 = (f32[64,2,64,128]{3,2,1,0:T(8,128)S(1)}, f32[64,128]{1,0:T(8,128)S(1)}) custom-call(s32[4]{0:T(128)S(1)} %pad_add_fusion.here_ref, f32[1544,128]{1,0:T(8,128)} %collective-permute-done.4.refs_0_, f32[1544,128]{1,0:T(8,128)} %collective-permute-done.5.refs_1_, f32[64,2,64,128]{3,2,1,0:T(8,128)S(1)} %get-tuple-element.46.refs_2_, ...), custom_call_target="tpu_custom_call" | custom-call | flops 1000000 | bytes 22140000 | tf_op jit(solution)/shard_map/place/pallas_call | solution.py:264
  32.2 3.0 %place.6 = (f32[64,2,64,128]{3,2,1,0:T(8,128)S(1)}, f32[64,128]{1,0:T(8,128)S(1)}) custom-call(s32[4]{0:T(128)S(1)} %pad_add_fusion.here_ref, f32[1544,128]{1,0:T(8,128)S(1)} %collective-permute-done.refs_0_, f32[1544,128]{1,0:T(8,128)S(1)} %collective-permute-done.2.refs_1_, f32[64,2,64,128]{3,2,1,0:T(8,128)S(1)} %get-tuple-element.48.refs_2_, ...), custom_call_target="tpu_custom_call" | custom-call | flops 1000000 | bytes 22140000 | tf_op jit(solution)/shard_map/place/pallas_call | solution.py:264
  35.2 0.2 collective-permute-done.1.refs_0_
  35.5 1.4 %collective-permute-done.3.refs_1_ = f32[1544,128]{1,0:T(8,128)S(1)} collective-permute-done((f32[1544,128]{1,0:T(8,128)S(1)}, f32[1544,128]{1,0:T(8,128)S(1)}, u32[]{:S(2)}, u32[]{:S(2)}) %collective-permute-start.3) | collective-permute-done | bytes 790560 | tf_op jit(solution)/shard_map/ppermute | solution.py:446
  36.9 3.1 %place.7 = (f32[1032,128]{1,0:T(8,128)S(1)}, f32[1032,128]{1,0:T(8,128)S(1)}, f32[1032,128]{1,0:T(8,128)S(1)}, f32[1032,128]{1,0:T(8,128)S(1)}, f32[520,128]{1,0...) custom-call(s32[4]{0:T(128)S(1)} %pad_add_fusion.here_ref, ...), custom_call_target="tpu_custom_call" | custom-call | flops 1000000 | bytes 22140000 | tf_op jit(solution)/shard_map/place/pallas_call | solution.py:264
  40.0 0.6 collective-permute-start.8
  40.6 1.5 %collective-permute-start.9 = (f32[1032,128]{1,0:T(8,128)S(1)}, f32[1032,128]{1,0:T(8,128)S(1)}, u32[]{:S(2)}, u32[]{:S(2)}) collective-permute-start(f32[1032,128]{1,0:T(8,128)S(1)} %get-tuple-element.62), channel_id=1, source_target_pairs={{0,192},{1,193},{2,194},{3,195},{4,7},{5,4},{6,5},{7,6},{64,0},{65... | collective-permute-start | bytes 1585160 | tf_op jit(solution)/shard_map/ppermute | solution.py:446
  42.1 1.7 %collective-permute-start.11 = (f32[520,128]{1,0:T(8,128)S(1)}, f32[520,128]{1,0:T(8,128)S(1)}, u32[]{:S(2)}, u32[]{:S(2)}) collective-permute-start(f32[520,128]{1,0:T(8,128)S(1)} %get-tuple-element.64), channel_id=1, source_target_pairs={{0,64},{1,65},{2,66},{3,67},{4,5},{5,6},{6,7},{7,4},{64,128},{65,1... | collective-permute-start | bytes 798728 | tf_op jit(solution)/shard_map/ppermute | solution.py:446
  43.8 0.6 collective-permute-start.15
  44.4 4.9 %collective-permute-done.8.b = f32[1032,128]{1,0:T(8,128)S(1)} collective-permute-done((f32[1032,128]{1,0:T(8,128)S(1)}, f32[1032,128]{1,0:T(8,128)S(1)}, u32[]{:S(2)}, u32[]{:S(2)}) %collective-permute-start.8) | collective-permute-done | bytes 528416 | tf_op jit(solution)/shard_map/ppermute | solution.py:446
  49.3 0.8 collective-permute-start.7
  50.2 0.9 collective-permute-done.9.d
  51.0 0.0 collective-permute-start.6
  51.0 0.1 add_received.1
  51.2 1.0 %collective-permute-done.11.refs_2_ = f32[520,128]{1,0:T(8,128)S(1)} collective-permute-done((f32[520,128]{1,0:T(8,128)S(1)}, f32[520,128]{1,0:T(8,128)S(1)}, u32[]{:S(2)}, u32[]{:S(2)}) %collective-permute-start.11) | collective-permute-done | bytes 266272 | tf_op jit(solution)/shard_map/ppermute | solution.py:446
  52.2 1.7 %collective-permute-start.10 = (f32[520,128]{1,0:T(8,128)S(1)}, f32[520,128]{1,0:T(8,128)S(1)}, u32[]{:S(2)}, u32[]{:S(2)}) collective-permute-start(f32[520,128]{1,0:T(8,128)S(1)} %get-tuple-element.63), channel_id=1, source_target_pairs={{0,64},{1,65},{2,66},{3,67},{4,5},{5,6},{6,7},{7,4},{64,128},{65,1... | collective-permute-start | bytes 798728 | tf_op jit(solution)/shard_map/ppermute | solution.py:446
  53.9 0.3 collective-permute-start.12
  54.2 0.0 collective-permute-done.15.refs_6_
  54.2 1.9 %collective-permute-start.14 = (f32[520,128]{1,0:T(8,128)S(1)}, f32[520,128]{1,0:T(8,128)S(1)}, u32[]{:S(2)}, u32[]{:S(2)}) collective-permute-start(f32[520,128]{1,0:T(8,128)S(1)} %get-tuple-element.67), channel_id=1, source_target_pairs={{0,68},{1,69},{2,70},{3,71},{4,1},{5,2},{6,3},{7,0},{64,132},{65,1... | collective-permute-start | bytes 798728 | tf_op jit(solution)/shard_map/ppermute | solution.py:446
  56.2 0.8 collective-permute-done.7.refs_0_
  57.0 1.6 %collective-permute-done.10.refs_1_ = f32[520,128]{1,0:T(8,128)S(1)} collective-permute-done((f32[520,128]{1,0:T(8,128)S(1)}, f32[520,128]{1,0:T(8,128)S(1)}, u32[]{:S(2)}, u32[]{:S(2)}) %collective-permute-start.10) | collective-permute-done | bytes 266272 | tf_op jit(solution)/shard_map/ppermute | solution.py:446
  58.6 2.9 %collective-permute-done.12.refs_3_ = f32[520,128]{1,0:T(8,128)S(1)} collective-permute-done((f32[520,128]{1,0:T(8,128)S(1)}, f32[520,128]{1,0:T(8,128)S(1)}, u32[]{:S(2)}, u32[]{:S(2)}) %collective-permute-start.12) | collective-permute-done | bytes 266272 | tf_op jit(solution)/shard_map/ppermute | solution.py:446
  61.5 0.0 collective-permute-done.14.refs_5_
  61.5 2.5 %collective-permute-done.16.refs_7_ = f32[520,128]{1,0:T(8,128)S(1)} collective-permute-done((f32[520,128]{1,0:T(8,128)S(1)}, f32[520,128]{1,0:T(8,128)S(1)}, u32[]{:S(2)}, u32[]{:S(2)}) %collective-permute-start.16) | collective-permute-done | bytes 266272 | tf_op jit(solution)/shard_map/ppermute | solution.py:446
  64.0 0.8 join.1
  64.8 2.0 %collective-permute-start.17 = (f32[136,128]{1,0:T(8,128)S(1)}, f32[136,128]{1,0:T(8,128)S(1)}, u32[]{:S(2)}, u32[]{:S(2)}) collective-permute-start(f32[136,128]{1,0:T(8,128)S(1)} %get-tuple-element.71), channel_id=1, source_target_pairs={{0,8},{8,16},{16,24},{24,32},{32,40},{40,48},{48,56},{56,0},{1,9},... | collective-permute-start | bytes 208904 | tf_op jit(solution)/shard_map/ppermute | solution.py:434
  66.8 0.1 collective-permute-start.22
  66.9 1.9 %collective-permute-start.21 = (f32[64,128]{1,0:T(8,128)S(1)}, f32[64,128]{1,0:T(8,128)S(1)}, u32[]{:S(2)}, u32[]{:S(2)}) collective-permute-start(f32[64,128]{1,0:T(8,128)S(1)} %get-tuple-element.79), channel_id=1, source_target_pairs={{0,8},{8,16},{16,24},{24,32},{32,40},{40,48},{48,56},{56,0},{1,9},... | collective-permute-start | bytes 98312 | tf_op jit(solution)/shard_map/ppermute | solution.py:434
  68.9 5.7 %collective-permute-start.18 = (f32[136,128]{1,0:T(8,128)S(1)}, f32[136,128]{1,0:T(8,128)S(1)}, u32[]{:S(2)}, u32[]{:S(2)}) collective-permute-start(f32[136,128]{1,0:T(8,128)S(1)} %get-tuple-element.72), channel_id=1, source_target_pairs={{0,16},{8,24},{16,32},{24,40},{32,48},{40,56},{48,0},{56,8},{1,17}... | collective-permute-start | bytes 208904 | tf_op jit(solution)/shard_map/ppermute | solution.py:434
  74.6 2.0 %collective-permute-start.20 = (f32[136,128]{1,0:T(8,128)S(1)}, f32[136,128]{1,0:T(8,128)S(1)}, u32[]{:S(2)}, u32[]{:S(2)}) collective-permute-start(f32[136,128]{1,0:T(8,128)S(1)} %get-tuple-element.74), channel_id=1, source_target_pairs={{0,48},{8,56},{16,0},{24,8},{32,16},{40,24},{48,32},{56,40},{1,49}... | collective-permute-start | bytes 208904 | tf_op jit(solution)/shard_map/ppermute | solution.py:434
  76.5 3.7 %collective-permute-start.23 = (f32[136,128]{1,0:T(8,128)S(1)}, f32[136,128]{1,0:T(8,128)S(1)}, u32[]{:S(2)}, u32[]{:S(2)}) collective-permute-start(f32[136,128]{1,0:T(8,128)S(1)} %get-tuple-element.81), channel_id=1, source_target_pairs={{0,24},{8,32},{16,40},{24,48},{32,56},{40,0},{48,8},{56,16},{1,25}... | collective-permute-start | bytes 208904 | tf_op jit(solution)/shard_map/ppermute | solution.py:434
  80.3 1.4 %collective-permute-start.24 = (f32[136,128]{1,0:T(8,128)S(1)}, f32[136,128]{1,0:T(8,128)S(1)}, u32[]{:S(2)}, u32[]{:S(2)}) collective-permute-start(f32[136,128]{1,0:T(8,128)S(1)} %get-tuple-element.82), channel_id=1, source_target_pairs={{0,40},{8,48},{16,56},{24,0},{32,8},{40,16},{48,24},{56,32},{1,41}... | collective-permute-start | bytes 208904 | tf_op jit(solution)/shard_map/ppermute | solution.py:434
  81.7 0.9 begin.1
  82.6 2.7 %collective-permute-done.23.ahead = f32[136,128]{1,0:T(8,128)S(1)} collective-permute-done((f32[136,128]{1,0:T(8,128)S(1)}, f32[136,128]{1,0:T(8,128)S(1)}, u32[]{:S(2)}, u32[]{:S(2)}) %collective-permute-start.23) | collective-permute-done | bytes 69664 | tf_op jit(solution)/shard_map/ppermute | solution.py:434
  85.3 4.3 %collective-permute-done.24.behind = f32[136,128]{1,0:T(8,128)S(1)} collective-permute-done((f32[136,128]{1,0:T(8,128)S(1)}, f32[136,128]{1,0:T(8,128)S(1)}, u32[]{:S(2)}, u32[]{:S(2)}) %collective-permute-start.24) | collective-permute-done | bytes 69664 | tf_op jit(solution)/shard_map/ppermute | solution.py:434
  89.6 1.5 %finish.1 = f32[64,256]{1,0:T(8,128)} custom-call(s32[4]{0:T(128)S(1)} %pad_add_fusion.here_ref, f32[128,128]{1,0:T(8,128)S(1)} %get-tuple-element.75.numerator, f32[64,256]{1,0:T(8,128)S(1)} %get-tuple-element.76.denominator, f32[136,128]{1,0:T(8,128)S(1)} %collective-permute-done.23.ahead, f32[136,128]{1,0:T(8,128)S(1)} %collective-permute-done.24.behind), custom_call_target="tpu_custom_call" | custom-call | tf_op jit(solution)/shard_map/finish/pallas_call | solution.py:423
  (13 shorter events, 0.0 us)
Async XLA Ops:
  6.3 12.2 %collective-permute-start = (f32[1544,128]{1,0:T(8,128)}, f32[1544,128]{1,0:T(8,128)S(1)}, u32[]{:S(2)}, u32[]{:S(2)}) collective-permute-start(f32[1544,128]{1,0:T(8,128)} %get-tuple-element.44.refs_0_), channel_id=1, source_target_pairs={{0,1},{1,2},{2,3},{3,0},{4,68},{5,69},{6,70},{7,71},{64,65},{65,66... | collective-permute-start | bytes 2371592 | tf_op jit(solution)/shard_map/ppermute | solution.py:446
  6.5 13.5 %collective-permute-start.2 = (f32[1544,128]{1,0:T(8,128)}, f32[1544,128]{1,0:T(8,128)S(1)}, u32[]{:S(2)}, u32[]{:S(2)}) collective-permute-start(f32[1544,128]{1,0:T(8,128)} %get-tuple-element.45.refs_1_), channel_id=1, source_target_pairs={{0,3},{1,0},{2,1},{3,2},{4,196},{5,197},{6,198},{7,199},{64,67},{6... | collective-permute-start | bytes 2371592 | tf_op jit(solution)/shard_map/ppermute | solution.py:446
  8.3 20.2 %collective-permute-start.4 = (f32[1544,128]{1,0:T(8,128)}, f32[1544,128]{1,0:T(8,128)}, u32[]{:S(2)}, u32[]{:S(2)}) collective-permute-start(f32[1544,128]{1,0:T(8,128)} %get-tuple-element.44.refs_0_), channel_id=1, source_target_pairs={{0,3},{1,0},{2,1},{3,2},{4,196},{5,197},{6,198},{7,199},{64,67},{6... | collective-permute-start | bytes 2371592 | tf_op jit(solution)/shard_map/ppermute | solution.py:446
  9.0 19.5 %collective-permute-start.5 = (f32[1544,128]{1,0:T(8,128)}, f32[1544,128]{1,0:T(8,128)}, u32[]{:S(2)}, u32[]{:S(2)}) collective-permute-start(f32[1544,128]{1,0:T(8,128)} %get-tuple-element.45.refs_1_), channel_id=1, source_target_pairs={{0,1},{1,2},{2,3},{3,0},{4,68},{5,69},{6,70},{7,71},{64,65},{65,66... | collective-permute-start | bytes 2371592 | tf_op jit(solution)/shard_map/ppermute | solution.py:446
  18.5 16.9 %collective-permute-start.1 = (f32[1544,128]{1,0:T(8,128)S(1)}, f32[1544,128]{1,0:T(8,128)S(1)}, u32[]{:S(2)}, u32[]{:S(2)}) collective-permute-start(f32[1544,128]{1,0:T(8,128)S(1)} %collective-permute-done.refs_0_), channel_id=1, source_target_pairs={{0,1},{1,2},{2,3},{3,0},{4,68},{5,69},{6,70},{7,71},{64,65},{65,66... | collective-permute-start | bytes 2371592 | tf_op jit(solution)/shard_map/ppermute | solution.py:446
  20.0 16.9 %collective-permute-start.3 = (f32[1544,128]{1,0:T(8,128)S(1)}, f32[1544,128]{1,0:T(8,128)S(1)}, u32[]{:S(2)}, u32[]{:S(2)}) collective-permute-start(f32[1544,128]{1,0:T(8,128)S(1)} %collective-permute-done.2.refs_1_), channel_id=1, source_target_pairs={{0,3},{1,0},{2,1},{3,2},{4,196},{5,197},{6,198},{7,199},{64,67},{6... | collective-permute-start | bytes 2371592 | tf_op jit(solution)/shard_map/ppermute | solution.py:446
  40.0 9.3 %collective-permute-start.8 = (f32[1032,128]{1,0:T(8,128)S(1)}, f32[1032,128]{1,0:T(8,128)S(1)}, u32[]{:S(2)}, u32[]{:S(2)}) collective-permute-start(f32[1032,128]{1,0:T(8,128)S(1)} %get-tuple-element.60), channel_id=1, source_target_pairs={{0,64},{1,65},{2,66},{3,67},{4,5},{5,6},{6,7},{7,4},{64,128},{65,1... | collective-permute-start | bytes 1585160 | tf_op jit(solution)/shard_map/ppermute | solution.py:446
  40.6 10.4 %collective-permute-start.9 = (f32[1032,128]{1,0:T(8,128)S(1)}, f32[1032,128]{1,0:T(8,128)S(1)}, u32[]{:S(2)}, u32[]{:S(2)}) collective-permute-start(f32[1032,128]{1,0:T(8,128)S(1)} %get-tuple-element.62), channel_id=1, source_target_pairs={{0,192},{1,193},{2,194},{3,195},{4,7},{5,4},{6,5},{7,6},{64,0},{65... | collective-permute-start | bytes 1585160 | tf_op jit(solution)/shard_map/ppermute | solution.py:446
  42.1 10.1 %collective-permute-start.11 = (f32[520,128]{1,0:T(8,128)S(1)}, f32[520,128]{1,0:T(8,128)S(1)}, u32[]{:S(2)}, u32[]{:S(2)}) collective-permute-start(f32[520,128]{1,0:T(8,128)S(1)} %get-tuple-element.64), channel_id=1, source_target_pairs={{0,64},{1,65},{2,66},{3,67},{4,5},{5,6},{6,7},{7,4},{64,128},{65,1... | collective-permute-start | bytes 798728 | tf_op jit(solution)/shard_map/ppermute | solution.py:446
  43.8 10.1 %collective-permute-start.13 = (f32[520,128]{1,0:T(8,128)S(1)}, f32[520,128]{1,0:T(8,128)S(1)}, u32[]{:S(2)}, u32[]{:S(2)}) collective-permute-start(f32[520,128]{1,0:T(8,128)S(1)} %get-tuple-element.66), channel_id=1, source_target_pairs={{0,196},{1,197},{2,198},{3,199},{4,3},{5,0},{6,1},{7,2},{64,4},{65... | collective-permute-start | bytes 798728 | tf_op jit(solution)/shard_map/ppermute | solution.py:446
  43.8 10.4 %collective-permute-start.15 = (f32[520,128]{1,0:T(8,128)S(1)}, f32[520,128]{1,0:T(8,128)S(1)}, u32[]{:S(2)}, u32[]{:S(2)}) collective-permute-start(f32[520,128]{1,0:T(8,128)S(1)} %get-tuple-element.68), channel_id=1, source_target_pairs={{0,68},{1,69},{2,70},{3,71},{4,1},{5,2},{6,3},{7,0},{64,132},{65,1... | collective-permute-start | bytes 798728 | tf_op jit(solution)/shard_map/ppermute | solution.py:446
  49.3 7.6 %collective-permute-start.7 = (f32[520,128]{1,0:T(8,128)S(1)}, f32[520,128]{1,0:T(8,128)S(1)}, u32[]{:S(2)}, u32[]{:S(2)}) collective-permute-start(f32[520,128]{1,0:T(8,128)S(1)} %get-tuple-element.58), channel_id=1, source_target_pairs={{0,192},{1,193},{2,194},{3,195},{4,7},{5,4},{6,5},{7,6},{64,0},{65... | collective-permute-start | bytes 798728 | tf_op jit(solution)/shard_map/ppermute | solution.py:446
  51.0 5.9 %collective-permute-start.6 = (f32[1032,128]{1,0:T(8,128)S(1)}, f32[1032,128]{1,0:T(8,128)S(1)}, u32[]{:S(2)}, u32[]{:S(2)}) collective-permute-start(f32[1032,128]{1,0:T(8,128)S(1)} %get-tuple-element.57), channel_id=1, source_target_pairs={{0,4},{4,0},{1,5},{5,1},{2,6},{6,2},{3,7},{7,3},{8,12},{12,8},{9,1... | collective-permute-start | bytes 1585160 | tf_op jit(solution)/shard_map/ppermute | solution.py:468
  52.2 6.4 %collective-permute-start.10 = (f32[520,128]{1,0:T(8,128)S(1)}, f32[520,128]{1,0:T(8,128)S(1)}, u32[]{:S(2)}, u32[]{:S(2)}) collective-permute-start(f32[520,128]{1,0:T(8,128)S(1)} %get-tuple-element.63), channel_id=1, source_target_pairs={{0,64},{1,65},{2,66},{3,67},{4,5},{5,6},{6,7},{7,4},{64,128},{65,1... | collective-permute-start | bytes 798728 | tf_op jit(solution)/shard_map/ppermute | solution.py:446
  53.9 7.6 %collective-permute-start.12 = (f32[520,128]{1,0:T(8,128)S(1)}, f32[520,128]{1,0:T(8,128)S(1)}, u32[]{:S(2)}, u32[]{:S(2)}) collective-permute-start(f32[520,128]{1,0:T(8,128)S(1)} %get-tuple-element.65), channel_id=1, source_target_pairs={{0,192},{1,193},{2,194},{3,195},{4,7},{5,4},{6,5},{7,6},{64,0},{65... | collective-permute-start | bytes 798728 | tf_op jit(solution)/shard_map/ppermute | solution.py:446
  54.2 7.3 %collective-permute-start.14 = (f32[520,128]{1,0:T(8,128)S(1)}, f32[520,128]{1,0:T(8,128)S(1)}, u32[]{:S(2)}, u32[]{:S(2)}) collective-permute-start(f32[520,128]{1,0:T(8,128)S(1)} %get-tuple-element.67), channel_id=1, source_target_pairs={{0,68},{1,69},{2,70},{3,71},{4,1},{5,2},{6,3},{7,0},{64,132},{65,1... | collective-permute-start | bytes 798728 | tf_op jit(solution)/shard_map/ppermute | solution.py:446
  57.0 7.1 %collective-permute-start.16 = (f32[520,128]{1,0:T(8,128)S(1)}, f32[520,128]{1,0:T(8,128)S(1)}, u32[]{:S(2)}, u32[]{:S(2)}) collective-permute-start(f32[520,128]{1,0:T(8,128)S(1)} %get-tuple-element.69), channel_id=1, source_target_pairs={{0,196},{1,197},{2,198},{3,199},{4,3},{5,0},{6,1},{7,2},{64,4},{65... | collective-permute-start | bytes 798728 | tf_op jit(solution)/shard_map/ppermute | solution.py:446
  64.8 15.4 %collective-permute-start.17 = (f32[136,128]{1,0:T(8,128)S(1)}, f32[136,128]{1,0:T(8,128)S(1)}, u32[]{:S(2)}, u32[]{:S(2)}) collective-permute-start(f32[136,128]{1,0:T(8,128)S(1)} %get-tuple-element.71), channel_id=1, source_target_pairs={{0,8},{8,16},{16,24},{24,32},{32,40},{40,48},{48,56},{56,0},{1,9},... | collective-permute-start | bytes 208904 | tf_op jit(solution)/shard_map/ppermute | solution.py:434
  66.8 9.7 %collective-permute-start.22 = (f32[72,128]{1,0:T(8,128)S(1)}, f32[72,128]{1,0:T(8,128)S(1)}, u32[]{:S(2)}, u32[]{:S(2)}) collective-permute-start(f32[72,128]{1,0:T(8,128)S(1)} %get-tuple-element.80), channel_id=1, source_target_pairs={{0,56},{8,0},{16,8},{24,16},{32,24},{40,32},{48,40},{56,48},{1,57}... | collective-permute-start | bytes 110600 | tf_op jit(solution)/shard_map/ppermute | solution.py:434
  66.9 7.6 %collective-permute-start.21 = (f32[64,128]{1,0:T(8,128)S(1)}, f32[64,128]{1,0:T(8,128)S(1)}, u32[]{:S(2)}, u32[]{:S(2)}) collective-permute-start(f32[64,128]{1,0:T(8,128)S(1)} %get-tuple-element.79), channel_id=1, source_target_pairs={{0,8},{8,16},{16,24},{24,32},{32,40},{40,48},{48,56},{56,0},{1,9},... | collective-permute-start | bytes 98312 | tf_op jit(solution)/shard_map/ppermute | solution.py:434
  68.9 12.8 %collective-permute-start.18 = (f32[136,128]{1,0:T(8,128)S(1)}, f32[136,128]{1,0:T(8,128)S(1)}, u32[]{:S(2)}, u32[]{:S(2)}) collective-permute-start(f32[136,128]{1,0:T(8,128)S(1)} %get-tuple-element.72), channel_id=1, source_target_pairs={{0,16},{8,24},{16,32},{24,40},{32,48},{40,56},{48,0},{56,8},{1,17}... | collective-permute-start | bytes 208904 | tf_op jit(solution)/shard_map/ppermute | solution.py:434
  74.6 7.1 %collective-permute-start.19 = (f32[136,128]{1,0:T(8,128)S(1)}, f32[136,128]{1,0:T(8,128)S(1)}, u32[]{:S(2)}, u32[]{:S(2)}) collective-permute-start(f32[136,128]{1,0:T(8,128)S(1)} %get-tuple-element.73), channel_id=1, source_target_pairs={{0,56},{8,0},{16,8},{24,16},{32,24},{40,32},{48,40},{56,48},{1,57}... | collective-permute-start | bytes 208904 | tf_op jit(solution)/shard_map/ppermute | solution.py:434
  74.6 7.1 %collective-permute-start.20 = (f32[136,128]{1,0:T(8,128)S(1)}, f32[136,128]{1,0:T(8,128)S(1)}, u32[]{:S(2)}, u32[]{:S(2)}) collective-permute-start(f32[136,128]{1,0:T(8,128)S(1)} %get-tuple-element.74), channel_id=1, source_target_pairs={{0,48},{8,56},{16,0},{24,8},{32,16},{40,24},{48,32},{56,40},{1,49}... | collective-permute-start | bytes 208904 | tf_op jit(solution)/shard_map/ppermute | solution.py:434
  76.5 8.8 %collective-permute-start.23 = (f32[136,128]{1,0:T(8,128)S(1)}, f32[136,128]{1,0:T(8,128)S(1)}, u32[]{:S(2)}, u32[]{:S(2)}) collective-permute-start(f32[136,128]{1,0:T(8,128)S(1)} %get-tuple-element.81), channel_id=1, source_target_pairs={{0,24},{8,32},{16,40},{24,48},{32,56},{40,0},{48,8},{56,16},{1,25}... | collective-permute-start | bytes 208904 | tf_op jit(solution)/shard_map/ppermute | solution.py:434
  80.3 9.3 %collective-permute-start.24 = (f32[136,128]{1,0:T(8,128)S(1)}, f32[136,128]{1,0:T(8,128)S(1)}, u32[]{:S(2)}, u32[]{:S(2)}) collective-permute-start(f32[136,128]{1,0:T(8,128)S(1)} %get-tuple-element.82), channel_id=1, source_target_pairs={{0,40},{8,48},{16,56},{24,0},{32,8},{40,16},{48,24},{56,32},{1,41}... | collective-permute-start | bytes 208904 | tf_op jit(solution)/shard_map/ppermute | solution.py:434
